TPU v7x, 256 devices: a whole 4x4x8 slice. The times are simulated.
256 devices in a mesh: dp: 32 (over y_hi, z, core), proto: 8 (over y_lo, x).
Axes of the slice: x: 4, y: 4 (y_hi: 2, y_lo: 2; y = y_hi * 2 + y_lo), z: 8, core: 2. Of those that a mesh axis runs over, the one named last changes fastest.
Arguments:
- cls_features: bfloat16 [128, 384], P('dp')
- patch_features: bfloat16 [128, 256, 384], P('dp')
- mask_index: int32 [128, 64], P('dp'), may hold values from 0 to 255, as said below
- cls_protos: bfloat16 [384, 131072], P(None, ('proto', 'dp'))
- patch_protos: bfloat16 [384, 131072], P(None, ('proto', 'dp'))
Outputs:
- cls_targets: bfloat16 [128, 131072], P('dp', 'proto')
- patch_targets: bfloat16 [8192, 131072], P('dp', 'proto')
Inputs may be any that keep to these rules, and one draw needn't show every extreme that they name: `mask_index`: the 64 numbers of one crop are distinct.
All inputs are finite; a program needn't handle non-finite values.
Results may differ from a plain program's by a relative error of at most 0.0036.
Values may be sent and summed in bfloat16 or wider, within the bound.
No kernel may reach another device: no remote copies, remote signals or barrier semaphores. Data moves between devices by JAX's collectives and lax.ppermute only.
A program may use at most 128 MiB of HBM per device.

v0:
```python
import functools

import jax
import jax.numpy as jnp
import numpy as np
from jax import lax
from jax.experimental import pallas as pl
from jax.experimental.pallas import tpu as pltpu
from jax.sharding import PartitionSpec as P

PROTOS = 131072
ITERS = 3
TEMP = 0.07
SLOPE = float(1.0 / (TEMP * np.log(2.0)))
F32 = jnp.float32
BF16 = jnp.bfloat16
BOTH = ("dp", "proto")
MIB = 1 << 20

NZ, NX = 8, 4


def coords(g):
    d, p = g // 8, g % 8
    return d % 2, (d // 2) % NZ, d // (2 * NZ), p % NX, p // NX


def flat(core, z, yh, x, yl):
    return ((yh * NZ + z) * 2 + core) * 8 + yl * NX + x


def swap(dcore=0, dz=0, dyh=0, dx=0, dyl=0):
    pairs = []
    for g in range(256):
        core, z, yh, x, yl = coords(g)
        pairs.append((g, flat(core ^ dcore, z ^ dz, yh ^ dyh, x ^ dx, yl ^ dyl)))
    return pairs


def groups(key):
    found = {}
    for g in range(256):
        found.setdefault(key(*coords(g)), []).append(g)
    return [found[k] for k in sorted(found)]


CORE = swap(dcore=1)
Y_STEPS = ((1, 1), (1, 0), (0, 1))
GROUPS_Z = groups(lambda core, z, yh, x, yl: (core, yh, x, yl))
GROUPS_ZX = groups(lambda core, z, yh, x, yl: (core, yh, yl))


def exchange(value, group):
    return lax.all_to_all(value, BOTH, 0, 0, axis_index_groups=group, tiled=True)


VM = pl.BlockSpec(memory_space=pltpu.VMEM)
SM = pl.BlockSpec(memory_space=pltpu.SMEM)
HBM = pl.BlockSpec(memory_space=pltpu.HBM)


def call(body, out_shape, specs, name, scratch=(), limit=8):
    return pl.pallas_call(
        body,
        out_shape=out_shape,
        in_specs=specs,
        out_specs=jax.tree.map(lambda _: VM, out_shape),
        scratch_shapes=list(scratch),
        compiler_params=pltpu.CompilerParams(vmem_limit_bytes=limit * MIB),
        name=name,
    )


def shape(dims, dtype=F32):
    return jax.ShapeDtypeStruct(dims, dtype)


def down(row):
    return jnp.transpose(jnp.broadcast_to(row, (128, 128)))


def across(block):
    return jnp.sum(jnp.transpose(block), axis=0, keepdims=True)


def swapped(rows, step):
    return jnp.concatenate([rows[k ^ step : (k ^ step) + 1] for k in range(8)], axis=0)


def inv_norms(protos):
    wide = protos.astype(F32)
    return SLOPE * lax.rsqrt(jnp.sum(wide * wide, axis=0, keepdims=True) + 1e-06)


def unit(values):
    return (values * lax.rsqrt(jnp.sum(values * values, -1, keepdims=True) + 1e-06)).astype(BF16)


def units_body(where_ref, feat_ref, mask_ref, cls_ref, a_ref, b_ref, c_ref, unit_ref, send_ref):
    core, yh = where_ref[0], where_ref[2]
    for image in range(4):
        pick = lax.broadcasted_iota(jnp.int32, (256, 64), 0) == mask_ref[image : image + 1, :]
        chosen = lax.dot_general(
            pick.astype(BF16), feat_ref[image], (((0,), (0,)), ((), ())), preferred_element_type=F32
        )
        unit_ref[image * 64 : image * 64 + 64, :] = unit(chosen)
    half = unit_ref[pl.ds(pl.multiple_of(where_ref[4] * 128, 128), 128), :]
    cls = [unit(ref[...].astype(F32)).astype(F32) for ref in (cls_ref, a_ref, b_ref, c_ref)]
    near = [jnp.where(core == 0, cls[0], cls[1]), jnp.where(core == 0, cls[1], cls[0])]
    far = [jnp.where(core == 0, cls[2], cls[3]), jnp.where(core == 0, cls[3], cls[2])]
    first = [jnp.where(yh == 0, n, f) for n, f in zip(near, far)]
    second = [jnp.where(yh == 0, f, n) for n, f in zip(near, far)]
    tail = jnp.concatenate(first + second, axis=0).astype(BF16)
    for z in range(NZ):
        send_ref[z, :128, :] = half
        send_ref[z, 128:, :] = tail


def kernel_body(units_ref, *refs):
    pieces, (kern_ref, sums_ref) = refs[:8], refs[8:]
    for k in range(8):
        for half in range(2):
            lanes = slice(half * 256, half * 256 + 256)
            protos = pieces[k][:, lanes]
            scale = inv_norms(protos)
            total = jnp.zeros((8, 256), F32)
            for part in range(2):
                units = units_ref[part * 4 : part * 4 + 4, :128, :].reshape(512, 384)
                dots = jnp.dot(units, protos, preferred_element_type=F32)
                value = jnp.exp2(dots * scale - SLOPE)
                at = k * 512 + half * 256
                kern_ref[part * 512 : part * 512 + 512, at : at + 256] = value
                total = total + jnp.sum(value.reshape(64, 8, 256), axis=0)
            sums_ref[k : k + 1, lanes] = jnp.sum(total, axis=0, keepdims=True)


def cls_step(cls_kern, row_scale):
    wide = down(row_scale)
    cols = [
        1.0 / jnp.sum(cls_kern[:, q * 128 : q * 128 + 128] * wide, axis=0, keepdims=True)
        for q in range(4)
    ]
    total = cls_kern[:, :128] * cols[0]
    for q in range(1, 4):
        total = total + cls_kern[:, q * 128 : q * 128 + 128] * cols[q]
    return cols, across(total)


def cls_body(units_ref, protos_ref, sums_ref, kern_ref, message_ref):
    units = jnp.concatenate([units_ref[z, 128:, :] for z in range(NZ)], axis=0)
    protos = protos_ref[...]
    dots = jnp.dot(units, protos, preferred_element_type=F32)
    kern_ref[...] = jnp.exp2(dots * inv_norms(protos) - SLOPE)
    _, sums = cls_step(kern_ref[...], jnp.ones((1, 128), F32))
    message_ref[:, :512] = sums_ref[...]
    message_ref[:, 512:] = jnp.broadcast_to(sums, (8, 128))


def columns_body(last, got_ref, kern_ref, cls_kern_ref, message_ref, *more):
    total = got_ref[0]
    for k in range(1, 32):
        total = total + got_ref[k]
    row_scale = 1.0 / total[:9]
    cls_kern = cls_kern_ref[...]
    cols, sums = cls_step(cls_kern, row_scale[8:9])
    if last:
        for q in range(4):
            scaled = cls_kern[:, q * 128 : q * 128 + 128] * cols[q]
            for n in range(32):
                z, yh, core = n // 4, (n // 2) % 2, n % 2
                more[0][(yh * NZ + z) * 2 + core, :, q * 128 : q * 128 + 128] = scaled[n * 4 : n * 4 + 4]
    acc = more[-1]
    for z in range(NZ):
        wide = down(row_scale[z : z + 1]).reshape(16, 8, 128)
        for t in range(32):
            block = kern_ref[z * 128 : z * 128 + 128, t * 128 : t * 128 + 128]
            part = jnp.sum(block.reshape(16, 8, 128) * wide, axis=0)
            if z == 0:
                acc[:, t * 128 : t * 128 + 128] = part
            else:
                acc[:, t * 128 : t * 128 + 128] += part
    for k in range(8):
        message_ref[k : k + 1, :512] = jnp.sum(acc[:, k * 512 : k * 512 + 512], axis=0, keepdims=True)
    message_ref[:, 512:] = jnp.broadcast_to(sums, (8, 128))


def add_body(mine_ref, other_ref, out_ref):
    out_ref[...] = mine_ref[...] + swapped(other_ref[...], 4)


def rows_body(last, mine_ref, a_ref, b_ref, c_ref, kern_ref, send_ref, wide_ref):
    total = mine_ref[...]
    for ref, (dyh, dyl) in zip((a_ref, b_ref, c_ref), Y_STEPS):
        total = total + swapped(ref[...], dyh * 2 + dyl)
    cols = 1.0 / total[:, :512]
    cls = total[:1, 512:]
    for k in range(8):
        wide_ref[:, k * 512 : k * 512 + 512] = jnp.broadcast_to(cols[k : k + 1], (8, 512))
    sums = []
    for z in range(NZ):
        acc = jnp.zeros((16, 8, 128), F32)
        for t in range(32):
            block = kern_ref[z * 128 : z * 128 + 128, t * 128 : t * 128 + 128]
            acc = acc + block.reshape(16, 8, 128) * wide_ref[:, t * 128 : t * 128 + 128][None]
        sums.append(across(acc.reshape(128, 128)))
    if last:
        own = [cols[k : k + 1, q * 128 : q * 128 + 128] for k in (0, 2, 4, 6) for q in range(4)]
        own = jnp.concatenate(own, axis=0)
        rest = jnp.zeros((6, 128), F32)
        for z in range(NZ):
            block = jnp.concatenate([own, sums[z], cls, rest], axis=0)
            for x in range(NX):
                send_ref[z * NX + x] = block
    else:
        block = jnp.concatenate(sums + [cls, jnp.zeros((7, 128), F32)], axis=0)
        for k in range(32):
            send_ref[k] = block


def settle_body(where_ref, got_ref, cols_ref, sums_ref):
    core, yh, x = where_ref[0], where_ref[2], where_ref[3]
    total = got_ref[0, 16:24, :]
    for k in range(1, 32):
        total = total + got_ref[k, 16:24, :]
    sums_ref[...] = total
    for z in range(NZ):
        for cr in range(2):
            for yr in range(2):
                row = (jnp.bitwise_xor(yh, yr) * NZ + z) * 2 + jnp.bitwise_xor(core, cr)
                for q in range(4):
                    at = (cr * 2 + yr) * 4 + q
                    cols_ref[row, :, q * 128 : q * 128 + 128] = got_ref[z * NX + x, at : at + 1, :]


def cls_final_body(where_ref, scaled_ref, sums_ref, out_ref):
    base = ((where_ref[1] * 2 + where_ref[2]) * 2 + where_ref[0]) * 4
    scale = PROTOS / sums_ref[1:2, :]
    lane = lax.broadcasted_iota(jnp.int32, (1, 128), 1)
    rows = [jnp.sum(jnp.where(lane == base + v, scale, 0.0), axis=1, keepdims=True) for v in range(4)]
    scale = jnp.concatenate(rows, axis=0)
    for d in range(32):
        out_ref[:, d * 512 : d * 512 + 512] = (scaled_ref[d] * scale).astype(BF16)


WIDTH = 2048


def final_body(
    where_ref, protos_ref, units_ref, cols_ref, mine_ref, other_ref, out_ref, wide_ref, in_ref, stage_ref, in_sems, out_sems
):
    parts = 16384 // WIDTH
    lanes = [slice(n * WIDTH, n * WIDTH + WIDTH) for n in range(parts)]
    ins = [pltpu.make_async_copy(protos_ref.at[:, lanes[n]], in_ref.at[n], in_sems.at[n]) for n in range(parts)]
    outs = [pltpu.make_async_copy(stage_ref.at[n], out_ref.at[:, lanes[n]], out_sems.at[n]) for n in range(parts)]
    for copy in ins:
        copy.start()
    yl = where_ref[4]
    mine, other = mine_ref[:1], other_ref[:1]
    wide_ref[:128] = PROTOS / down(jnp.where(yl == 0, mine, other))
    wide_ref[128:] = PROTOS / down(jnp.where(yl == 0, other, mine))
    for n in range(parts):
        ins[n].wait()
        for at in range(0, WIDTH, 256):
            protos = in_ref[n, :, at : at + 256]
            cols = cols_ref[n * (WIDTH // 512) + at // 512][:, at % 512 : at % 512 + 256]
            dots = jnp.dot(units_ref[...], protos, preferred_element_type=F32)
            value = jnp.exp2(dots * inv_norms(protos) - SLOPE) * cols
            for q in (0, 128):
                scaled = value[:, q : q + 128] * wide_ref[...]
                stage_ref[n, :, at + q : at + q + 128] = scaled.astype(BF16)
        outs[n].start()
    for copy in outs:
        copy.wait()


def final(where, protos, units, cols, mine, other):
    parts = 16384 // WIDTH
    return pl.pallas_call(
        final_body,
        out_shape=shape((256, 16384), BF16),
        in_specs=[SM, HBM, VM, VM, VM, VM],
        out_specs=pl.BlockSpec(memory_space=pl.ANY),
        scratch_shapes=[
            pltpu.VMEM((256, 128), F32),
            pltpu.VMEM((parts, 384, WIDTH), BF16),
            pltpu.VMEM((parts, 256, WIDTH), BF16),
            pltpu.SemaphoreType.DMA((parts,)),
            pltpu.SemaphoreType.DMA((parts,)),
        ],
        compiler_params=pltpu.CompilerParams(vmem_limit_bytes=56 * MIB),
        name="final_scale",
    )(where, protos, units, cols, mine, other)


def per_device(cls_features, patch_features, mask_index, cls_protos, patch_protos):
    dp, proto = lax.axis_index("dp"), lax.axis_index("proto")
    core, z, yh = dp % 2, (dp // 2) % NZ, dp // (2 * NZ)
    x, yl = proto % NX, proto // NX
    where = jnp.stack([core, z, yh, x, yl]).astype(jnp.int32)

    gathered = lax.all_gather(patch_protos, "dp", axis=1, tiled=True)

    cls_near = [lax.ppermute(cls_features, BOTH, swap(dcore=c, dyh=h)) for c, h in ((1, 0), (0, 1), (1, 1))]

    near = {(0, 0): patch_protos}
    for dyh, dyl in Y_STEPS:
        near[dyh, dyl] = lax.ppermute(patch_protos, BOTH, swap(dyh=dyh, dyl=dyl))
    pieces = [near[k // 2, k % 2] for k in range(4)]
    pieces += [lax.ppermute(piece, BOTH, CORE) for piece in pieces]

    units, send = call(
        units_body, (shape((256, 384), BF16), shape((NZ, 144, 384), BF16)), [SM] + [VM] * 6, "units"
    )(where, patch_features, mask_index, cls_features, *cls_near)
    rows = exchange(send, GROUPS_Z)

    kern, col_sums = call(
        kernel_body, (pltpu.VMEM((1024, 4096), F32), shape((8, 512))), [VM] * 9, "patch_kernel"
    )(rows, *pieces)
    cls_kern, message = call(cls_body, (shape((128, 512)), shape((8, 640))), [VM] * 3, "cls_kernel")(
        rows, cls_protos, col_sums
    )

    for step in range(ITERS):
        last = step == ITERS - 1
        if step:
            outs = [shape((8, 640))]
            if last:
                outs.append(shape((32, 4, 512)))
            done = call(
                functools.partial(columns_body, last),
                tuple(outs),
                [VM] * 3,
                "column_sums",
                [pltpu.VMEM((8, 4096), F32)],
            )(got, kern, cls_kern)
            message = done[0]
        message = call(add_body, shape((8, 640)), [VM] * 2, "add_core")(message, lax.ppermute(message, BOTH, CORE))
        parts = [lax.ppermute(message, BOTH, swap(dyh=dyh, dyl=dyl)) for dyh, dyl in Y_STEPS]
        send = call(
            functools.partial(rows_body, last),
            shape((32, 24 if last else 16, 128)),
            [VM] * 5,
            "row_sums",
            [pltpu.VMEM((8, 4096), F32)],
        )(message, *parts, kern)
        got = exchange(send, GROUPS_ZX)

    cols, sums = call(settle_body, (shape((32, 1, 512)), shape((8, 128))), [SM, VM], "settle")(where, got)
    cls_scaled = lax.optimization_barrier((done[1], sums))[0]
    cls_scaled = lax.all_to_all(cls_scaled, "dp", 0, 0, tiled=True)
    other = lax.ppermute(sums, BOTH, swap(dyl=1))
    patch_targets = final(where, gathered, units, cols, sums, other)
    cls_scaled, patch_targets = lax.optimization_barrier((cls_scaled, patch_targets))
    cls_targets = call(cls_final_body, shape((4, 16384), BF16), [SM, VM, VM], "cls_final")(where, cls_scaled, sums)
    return (cls_targets, patch_targets)


def solution(mesh):
    return jax.shard_map(
        per_device,
        mesh=mesh,
        in_specs=(
            P("dp", None),
            P("dp", None, None),
            P("dp", None),
            P(None, ("proto", "dp")),
            P(None, ("proto", "dp")),
        ),
        out_specs=(P("dp", "proto"), P("dp", "proto")),
        check_vma=False,
    )
```

profile of v0, /device:TPU:1, one launch (start us, length us, event | category | flops | bytes accessed | tf_op | source)
XLA Modules:
  0.0 188.7 jit_solution(11934527775159736194)
XLA Ops:
  7.9 3.3 %collective-permute-start = (bf16[4,384]{1,0:T(4,128)(2,1)}, bf16[4,384]{1,0:T(4,128)(2,1)S(1)}, u32[]{:S(2)}, u32[]{:S(2)}) collective-permute-start(bf16[4,384]{1,0:T(4,128)(2,1)} %cls_ref.1), channel_id=1, source_target_pairs={{0,8},{1,9},{2,10},{3,11},{4,12},{5,13},{6,14},{7,15},{8,0},{9,1},... | collective-permute-start | bytes 9224 | tf_op jit(solution)/shard_map/ppermute | solution.py:303
  12.4 2.0 %collective-permute-start.2 = (bf16[4,384]{1,0:T(4,128)(2,1)}, bf16[4,384]{1,0:T(4,128)(2,1)S(1)}, u32[]{:S(2)}, u32[]{:S(2)}) collective-permute-start(bf16[4,384]{1,0:T(4,128)(2,1)} %cls_ref.1), channel_id=1, source_target_pairs={{0,136},{1,137},{2,138},{3,139},{4,140},{5,141},{6,142},{7,143},{8... | collective-permute-start | bytes 9224 | tf_op jit(solution)/shard_map/ppermute | solution.py:303
  15.4 1.8 collective-permute-done.2.c_ref
  19.7 1.9 %units.1 = (bf16[256,384]{1,0:T(8,128)(2,1)S(1)}, bf16[8,144,384]{2,1,0:T(8,128)(2,1)}) custom-call(s32[5]{0:T(128)S(1)} %stack.23.where_ref, bf16[4,256,384]{2,1,0:T(8,128)(2,1)S(1)} %copy-done.1, s32[4,64]{1,0:T(4,128)S(1)} %copy-done.12, bf16[4,384]{1,0:T(4,128)(2,1)S(1)} %copy-done.11, bf16[4,384]{1,0:T(4,128)(2,1)S(1)} %collective-permute-done.a_ref, ...), custom_call_target="tpu_custom_call" | custom-call | tf_op jit(solution)/shard_map/units/pallas_call | solution.py:311
  22.2 8.2 %all-to-all-start = ((bf16[8,144,384]{2,1,0:T(8,128)(2,1)}), bf16[8,144,384]{2,1,0:T(8,128)(2,1)S(1)}, u32[]{:S(2)}, u32[]{:S(2)}) async-start(bf16[8,144,384]{2,1,0:T(8,128)(2,1)} %get-tuple-element.15), calls=%async_computation | async-start | bytes 1769472 | tf_op jit(solution)/shard_map/all_to_all | solution.py:54
  30.8 1.6 collective-permute-start.4
  32.4 1.9 %collective-permute-start.5 = (bf16[384,512]{1,0:T(8,128)(2,1)}, bf16[384,512]{1,0:T(8,128)(2,1)S(1)}, u32[]{:S(2)}, u32[]{:S(2)}) collective-permute-start(bf16[384,512]{1,0:T(8,128)(2,1)} %refs_0_.1), channel_id=1, source_target_pairs={{0,132},{1,133},{2,134},{3,135},{4,128},{5,129},{6,130},{7,131},{8... | collective-permute-start | bytes 1179656 | tf_op jit(solution)/shard_map/ppermute | solution.py:307
  34.3 1.5 collective-permute-start.6
  35.8 6.5 %collective-permute-done.3.refs_1_ = bf16[384,512]{1,0:T(8,128)(2,1)S(1)} collective-permute-done((bf16[384,512]{1,0:T(8,128)(2,1)}, bf16[384,512]{1,0:T(8,128)(2,1)S(1)}, u32[]{:S(2)}, u32[]{:S(2)}) %collective-permute-start.3) | collective-permute-done | bytes 393248 | tf_op jit(solution)/shard_map/ppermute | solution.py:307
  43.3 8.8 %collective-permute-done.4.refs_2_ = bf16[384,512]{1,0:T(8,128)(2,1)S(1)} collective-permute-done((bf16[384,512]{1,0:T(8,128)(2,1)}, bf16[384,512]{1,0:T(8,128)(2,1)S(1)}, u32[]{:S(2)}, u32[]{:S(2)}) %collective-permute-start.4) | collective-permute-done | bytes 393248 | tf_op jit(solution)/shard_map/ppermute | solution.py:307
  56.2 4.2 %all-to-all-done.units_ref = bf16[8,144,384]{2,1,0:T(8,128)(2,1)S(1)} async-done(((bf16[8,144,384]{2,1,0:T(8,128)(2,1)}), bf16[8,144,384]{2,1,0:T(8,128)(2,1)S(1)}, u32[]{:S(2)}, u32[]{:S(2)}) %all-to-all-start) | async-done | bytes 884768 | tf_op jit(solution)/shard_map/all_to_all | solution.py:54
  62.4 4.7 %patch_kernel.1 = (f32[1024,4096]{1,0:T(8,128)S(1)}, f32[8,512]{1,0:T(8,128)S(1)}) custom-call(bf16[8,144,384]{2,1,0:T(8,128)(2,1)S(1)} %all-to-all-done.units_ref, bf16[384,512]{1,0:T(8,128)(2,1)S(1)} %copy-done, bf16[384,512]{1,0:T(8,128)(2,1)S(1)} %collective-permute-done.3.refs_1_, bf16[384,512]{1,0:T(8,128)(2,1)S(1)} %collective-permute-done.4.refs_2_, ...), custom_call_target="tpu_custom_call" | custom-call | tf_op jit(solution)/shard_map/patch_kernel/pallas_call | solution.py:316
  70.0 1.8 collective-permute-start.11
  74.2 1.7 collective-permute-done.12.b_ref
  75.9 1.2 row_sums.3
  77.1 15.1 %all_to_all.25.got_ref = f32[32,16,128]{2,1,0:T(8,128)S(1)} all-to-all(f32[32,16,128]{2,1,0:T(8,128)S(1)} %row_sums.3), channel_id=1, replica_groups={{0,1,2,3,16,17,18,19,32,33,34,35,48,49,50,51,64,65,66,67,80,81,82,83,96..., dimensions={0} | all-to-all | bytes 524288 | tf_op jit(solution)/shard_map/all_to_all | solution.py:54
  92.2 1.4 column_sums.2.mine_ref
  93.6 5.3 %collective-permute-start.14 = (f32[8,640]{1,0:T(8,128)S(1)}, f32[8,640]{1,0:T(8,128)S(1)}, u32[]{:S(2)}, u32[]{:S(2)}) collective-permute-start(f32[8,640]{1,0:T(8,128)S(1)} %column_sums.2.mine_ref), channel_id=1, source_target_pairs={{0,8},{1,9},{2,10},{3,11},{4,12},{5,13},{6,14},{7,15},{8,0},{9,1},... | collective-permute-start | bytes 61448 | tf_op jit(solution)/shard_map/ppermute | solution.py:337
  100.9 2.1 %collective-permute-start.17 = (f32[8,640]{1,0:T(8,128)S(1)}, f32[8,640]{1,0:T(8,128)S(1)}, u32[]{:S(2)}, u32[]{:S(2)}) collective-permute-start(f32[8,640]{1,0:T(8,128)S(1)} %add_core.4.mine_ref), channel_id=1, source_target_pairs={{0,4},{1,5},{2,6},{3,7},{4,0},{5,1},{6,2},{7,3},{8,12},{9,13},{10,... | collective-permute-start | bytes 61448 | tf_op jit(solution)/shard_map/ppermute | solution.py:338
  103.0 3.9 %collective-permute-done.15.a_ref = f32[8,640]{1,0:T(8,128)S(1)} collective-permute-done((f32[8,640]{1,0:T(8,128)S(1)}, f32[8,640]{1,0:T(8,128)S(1)}, u32[]{:S(2)}, u32[]{:S(2)}) %collective-permute-start.15) | collective-permute-done | bytes 20512 | tf_op jit(solution)/shard_map/ppermute | solution.py:338
  107.0 1.2 row_sums.4
  108.2 15.5 %all_to_all.26.got_ref = f32[32,16,128]{2,1,0:T(8,128)S(1)} all-to-all(f32[32,16,128]{2,1,0:T(8,128)S(1)} %row_sums.4), channel_id=1, replica_groups={{0,1,2,3,16,17,18,19,32,33,34,35,48,49,50,51,64,65,66,67,80,81,82,83,96..., dimensions={0} | all-to-all | bytes 524288 | tf_op jit(solution)/shard_map/all_to_all | solution.py:54
  123.7 1.4 column_sums.3
  125.2 2.4 %collective-permute-start.18 = (f32[8,640]{1,0:T(8,128)S(1)}, f32[8,640]{1,0:T(8,128)S(1)}, u32[]{:S(2)}, u32[]{:S(2)}) collective-permute-start(f32[8,640]{1,0:T(8,128)S(1)} %get-tuple-element.21.mine_ref), channel_id=1, source_target_pairs={{0,8},{1,9},{2,10},{3,11},{4,12},{5,13},{6,14},{7,15},{8,0},{9,1},... | collective-permute-start | bytes 61448 | tf_op jit(solution)/shard_map/ppermute | solution.py:337
  128.4 2.0 %collective-permute-start.19 = (f32[8,640]{1,0:T(8,128)S(1)}, f32[8,640]{1,0:T(8,128)S(1)}, u32[]{:S(2)}, u32[]{:S(2)}) collective-permute-start(f32[8,640]{1,0:T(8,128)S(1)} %add_core.5.mine_ref), channel_id=1, source_target_pairs={{0,132},{1,133},{2,134},{3,135},{4,128},{5,129},{6,130},{7,131},{8... | collective-permute-start | bytes 61448 | tf_op jit(solution)/shard_map/ppermute | solution.py:338
  132.4 2.1 %collective-permute-done.20.b_ref = f32[8,640]{1,0:T(8,128)S(1)} collective-permute-done((f32[8,640]{1,0:T(8,128)S(1)}, f32[8,640]{1,0:T(8,128)S(1)}, u32[]{:S(2)}, u32[]{:S(2)}) %collective-permute-start.20) | collective-permute-done | bytes 20512 | tf_op jit(solution)/shard_map/ppermute | solution.py:338
  134.5 1.2 row_sums.5
  135.8 21.0 %all_to_all.27.got_ref = f32[32,24,128]{2,1,0:T(8,128)S(1)} all-to-all(f32[32,24,128]{2,1,0:T(8,128)S(1)} %row_sums.5), channel_id=1, replica_groups={{0,1,2,3,16,17,18,19,32,33,34,35,48,49,50,51,64,65,66,67,80,81,82,83,96..., dimensions={0} | all-to-all | bytes 786432 | tf_op jit(solution)/shard_map/all_to_all | solution.py:54
  158.0 7.6 %all-to-all-start.4 = ((f32[32,4,512]{2,1,0:T(4,128)}), f32[32,4,512]{2,1,0:T(4,128)S(1)}, u32[]{:S(2)}, u32[]{:S(2)}) async-start(f32[32,4,512]{2,1,0:T(4,128)} %get-tuple-element.23), calls=%async_computation.4 | async-start | bytes 524288 | tf_op jit(solution)/shard_map/all_to_all | solution.py:350
  165.6 2.7 %collective-permute-done.22.other_ref = f32[8,128]{1,0:T(8,128)S(1)} collective-permute-done((f32[8,128]{1,0:T(8,128)S(1)}, f32[8,128]{1,0:T(8,128)S(1)}, u32[]{:S(2)}, u32[]{:S(2)}) %collective-permute-start.22) | collective-permute-done | bytes 4128 | tf_op jit(solution)/shard_map/ppermute | solution.py:351
  168.9 10.8 %final_scale.1 = bf16[256,16384]{1,0:T(8,128)(2,1)} custom-call(s32[5]{0:T(128)} %copy-done.9, bf16[384,16384]{1,0:T(8,128)(2,1)} %all-gather.2.cloned.1.call-done.protos_ref, bf16[256,384]{1,0:T(8,128)(2,1)} %copy-done.5, f32[32,1,512]{2,1,0:T(1,128)} %copy-done.6, f32[8,128]{1,0:T(8,128)} %copy-done.7, f32[8,128]{1,0:T(8,128)} %copy-done.13), custom_call_target="tpu_custom_call" | custom-call | tf_op jit(solution)/shard_map/final_scale/pallas_call | solution.py:278
  180.4 1.4 cls_final.1
  (67 shorter events, 26.4 us)
Async XLA Ops:
  7.2 161.2 %all-gather.2.cloned.1.call-start = ((), (), s32[]{:S(2)}) async-start(), calls=%async_computation.5 | async-start | bytes 12976128 | tf_op jit(solution)/shard_map/all_gather | solution.py:301
  7.9 6.7 %collective-permute-start = (bf16[4,384]{1,0:T(4,128)(2,1)}, bf16[4,384]{1,0:T(4,128)(2,1)S(1)}, u32[]{:S(2)}, u32[]{:S(2)}) collective-permute-start(bf16[4,384]{1,0:T(4,128)(2,1)} %cls_ref.1), channel_id=1, source_target_pairs={{0,8},{1,9},{2,10},{3,11},{4,12},{5,13},{6,14},{7,15},{8,0},{9,1},... | collective-permute-start | bytes 9224 | tf_op jit(solution)/shard_map/ppermute | solution.py:303
  11.2 4.2 %collective-permute-start.1 = (bf16[4,384]{1,0:T(4,128)(2,1)}, bf16[4,384]{1,0:T(4,128)(2,1)S(1)}, u32[]{:S(2)}, u32[]{:S(2)}) collective-permute-start(bf16[4,384]{1,0:T(4,128)(2,1)} %cls_ref.1), channel_id=1, source_target_pairs={{0,128},{1,129},{2,130},{3,131},{4,132},{5,133},{6,134},{7,135},{8... | collective-permute-start | bytes 9224 | tf_op jit(solution)/shard_map/ppermute | solution.py:303
  12.4 4.7 %collective-permute-start.2 = (bf16[4,384]{1,0:T(4,128)(2,1)}, bf16[4,384]{1,0:T(4,128)(2,1)S(1)}, u32[]{:S(2)}, u32[]{:S(2)}) collective-permute-start(bf16[4,384]{1,0:T(4,128)(2,1)} %cls_ref.1), channel_id=1, source_target_pairs={{0,136},{1,137},{2,138},{3,139},{4,140},{5,141},{6,142},{7,143},{8... | collective-permute-start | bytes 9224 | tf_op jit(solution)/shard_map/ppermute | solution.py:303
  14.5 142.2 %copy-start.9 = (s32[5]{0:T(128)}, s32[5]{0:T(128)S(1)}, u32[]{:S(2)}) copy-start(s32[5]{0:T(128)S(1)} %stack.23.where_ref) | copy-start | bytes 64
  17.2 1.1 copy-start.1
  22.2 38.2 %all-to-all-start = ((bf16[8,144,384]{2,1,0:T(8,128)(2,1)}), bf16[8,144,384]{2,1,0:T(8,128)(2,1)S(1)}, u32[]{:S(2)}, u32[]{:S(2)}) async-start(bf16[8,144,384]{2,1,0:T(8,128)(2,1)} %get-tuple-element.15), calls=%async_computation | async-start | bytes 1769472 | tf_op jit(solution)/shard_map/all_to_all | solution.py:54
  30.4 11.8 %collective-permute-start.3 = (bf16[384,512]{1,0:T(8,128)(2,1)}, bf16[384,512]{1,0:T(8,128)(2,1)S(1)}, u32[]{:S(2)}, u32[]{:S(2)}) collective-permute-start(bf16[384,512]{1,0:T(8,128)(2,1)} %refs_0_.1), channel_id=1, source_target_pairs={{0,4},{1,5},{2,6},{3,7},{4,0},{5,1},{6,2},{7,3},{8,12},{9,13},{10,... | collective-permute-start | bytes 1179656 | tf_op jit(solution)/shard_map/ppermute | solution.py:307
  30.8 21.4 %collective-permute-start.4 = (bf16[384,512]{1,0:T(8,128)(2,1)}, bf16[384,512]{1,0:T(8,128)(2,1)S(1)}, u32[]{:S(2)}, u32[]{:S(2)}) collective-permute-start(bf16[384,512]{1,0:T(8,128)(2,1)} %refs_0_.1), channel_id=1, source_target_pairs={{0,128},{1,129},{2,130},{3,131},{4,132},{5,133},{6,134},{7,135},{8... | collective-permute-start | bytes 1179656 | tf_op jit(solution)/shard_map/ppermute | solution.py:307
  32.4 20.6 %collective-permute-start.5 = (bf16[384,512]{1,0:T(8,128)(2,1)}, bf16[384,512]{1,0:T(8,128)(2,1)S(1)}, u32[]{:S(2)}, u32[]{:S(2)}) collective-permute-start(bf16[384,512]{1,0:T(8,128)(2,1)} %refs_0_.1), channel_id=1, source_target_pairs={{0,132},{1,133},{2,134},{3,135},{4,128},{5,129},{6,130},{7,131},{8... | collective-permute-start | bytes 1179656 | tf_op jit(solution)/shard_map/ppermute | solution.py:307
  34.3 19.8 %collective-permute-start.6 = (bf16[384,512]{1,0:T(8,128)(2,1)}, bf16[384,512]{1,0:T(8,128)(2,1)S(1)}, u32[]{:S(2)}, u32[]{:S(2)}) collective-permute-start(bf16[384,512]{1,0:T(8,128)(2,1)} %refs_0_.1), channel_id=1, source_target_pairs={{0,8},{1,9},{2,10},{3,11},{4,12},{5,13},{6,14},{7,15},{8,0},{9,1},... | collective-permute-start | bytes 1179656 | tf_op jit(solution)/shard_map/ppermute | solution.py:309
  42.2 11.8 %collective-permute-start.7 = (bf16[384,512]{1,0:T(8,128)(2,1)S(1)}, bf16[384,512]{1,0:T(8,128)(2,1)S(1)}, u32[]{:S(2)}, u32[]{:S(2)}) collective-permute-start(bf16[384,512]{1,0:T(8,128)(2,1)S(1)} %collective-permute-done.3.refs_1_), channel_id=1, source_target_pairs={{0,8},{1,9},{2,10},{3,11},{4,12},{5,13},{6,14},{7,15},{8,0},{9,1},... | collective-permute-start | bytes 1179656 | tf_op jit(solution)/shard_map/ppermute | solution.py:309
  52.2 2.2 %collective-permute-start.8 = (bf16[384,512]{1,0:T(8,128)(2,1)S(1)}, bf16[384,512]{1,0:T(8,128)(2,1)S(1)}, u32[]{:S(2)}, u32[]{:S(2)}) collective-permute-start(bf16[384,512]{1,0:T(8,128)(2,1)S(1)} %collective-permute-done.4.refs_2_), channel_id=1, source_target_pairs={{0,8},{1,9},{2,10},{3,11},{4,12},{5,13},{6,14},{7,15},{8,0},{9,1},... | collective-permute-start | bytes 1179656 | tf_op jit(solution)/shard_map/ppermute | solution.py:309
  53.0 2.4 %collective-permute-start.9 = (bf16[384,512]{1,0:T(8,128)(2,1)S(1)}, bf16[384,512]{1,0:T(8,128)(2,1)S(1)}, u32[]{:S(2)}, u32[]{:S(2)}) collective-permute-start(bf16[384,512]{1,0:T(8,128)(2,1)S(1)} %collective-permute-done.5.refs_3_), channel_id=1, source_target_pairs={{0,8},{1,9},{2,10},{3,11},{4,12},{5,13},{6,14},{7,15},{8,0},{9,1},... | collective-permute-start | bytes 1179656 | tf_op jit(solution)/shard_map/ppermute | solution.py:309
  60.4 1.0 copy-start
  67.0 1.0 copy-start.2
  68.4 1.5 collective-permute-start.10
  70.0 4.2 %collective-permute-start.11 = (f32[8,640]{1,0:T(8,128)S(1)}, f32[8,640]{1,0:T(8,128)S(1)}, u32[]{:S(2)}, u32[]{:S(2)}) collective-permute-start(f32[8,640]{1,0:T(8,128)S(1)} %add_core.3.mine_ref), channel_id=1, source_target_pairs={{0,132},{1,133},{2,134},{3,135},{4,128},{5,129},{6,130},{7,131},{8... | collective-permute-start | bytes 61448 | tf_op jit(solution)/shard_map/ppermute | solution.py:338
  71.7 4.1 %collective-permute-start.12 = (f32[8,640]{1,0:T(8,128)S(1)}, f32[8,640]{1,0:T(8,128)S(1)}, u32[]{:S(2)}, u32[]{:S(2)}) collective-permute-start(f32[8,640]{1,0:T(8,128)S(1)} %add_core.3.mine_ref), channel_id=1, source_target_pairs={{0,128},{1,129},{2,130},{3,131},{4,132},{5,133},{6,134},{7,135},{8... | collective-permute-start | bytes 61448 | tf_op jit(solution)/shard_map/ppermute | solution.py:338
  72.3 3.6 %collective-permute-start.13 = (f32[8,640]{1,0:T(8,128)S(1)}, f32[8,640]{1,0:T(8,128)S(1)}, u32[]{:S(2)}, u32[]{:S(2)}) collective-permute-start(f32[8,640]{1,0:T(8,128)S(1)} %add_core.3.mine_ref), channel_id=1, source_target_pairs={{0,4},{1,5},{2,6},{3,7},{4,0},{5,1},{6,2},{7,3},{8,12},{9,13},{10,... | collective-permute-start | bytes 61448 | tf_op jit(solution)/shard_map/ppermute | solution.py:338
  93.6 6.2 %collective-permute-start.14 = (f32[8,640]{1,0:T(8,128)S(1)}, f32[8,640]{1,0:T(8,128)S(1)}, u32[]{:S(2)}, u32[]{:S(2)}) collective-permute-start(f32[8,640]{1,0:T(8,128)S(1)} %column_sums.2.mine_ref), channel_id=1, source_target_pairs={{0,8},{1,9},{2,10},{3,11},{4,12},{5,13},{6,14},{7,15},{8,0},{9,1},... | collective-permute-start | bytes 61448 | tf_op jit(solution)/shard_map/ppermute | solution.py:337
  99.8 7.2 %collective-permute-start.15 = (f32[8,640]{1,0:T(8,128)S(1)}, f32[8,640]{1,0:T(8,128)S(1)}, u32[]{:S(2)}, u32[]{:S(2)}) collective-permute-start(f32[8,640]{1,0:T(8,128)S(1)} %add_core.4.mine_ref), channel_id=1, source_target_pairs={{0,132},{1,133},{2,134},{3,135},{4,128},{5,129},{6,130},{7,131},{8... | collective-permute-start | bytes 61448 | tf_op jit(solution)/shard_map/ppermute | solution.py:338
  99.8 7.2 %collective-permute-start.16 = (f32[8,640]{1,0:T(8,128)S(1)}, f32[8,640]{1,0:T(8,128)S(1)}, u32[]{:S(2)}, u32[]{:S(2)}) collective-permute-start(f32[8,640]{1,0:T(8,128)S(1)} %add_core.4.mine_ref), channel_id=1, source_target_pairs={{0,128},{1,129},{2,130},{3,131},{4,132},{5,133},{6,134},{7,135},{8... | collective-permute-start | bytes 61448 | tf_op jit(solution)/shard_map/ppermute | solution.py:338
  100.9 6.1 %collective-permute-start.17 = (f32[8,640]{1,0:T(8,128)S(1)}, f32[8,640]{1,0:T(8,128)S(1)}, u32[]{:S(2)}, u32[]{:S(2)}) collective-permute-start(f32[8,640]{1,0:T(8,128)S(1)} %add_core.4.mine_ref), channel_id=1, source_target_pairs={{0,4},{1,5},{2,6},{3,7},{4,0},{5,1},{6,2},{7,3},{8,12},{9,13},{10,... | collective-permute-start | bytes 61448 | tf_op jit(solution)/shard_map/ppermute | solution.py:338
  125.2 3.2 %collective-permute-start.18 = (f32[8,640]{1,0:T(8,128)S(1)}, f32[8,640]{1,0:T(8,128)S(1)}, u32[]{:S(2)}, u32[]{:S(2)}) collective-permute-start(f32[8,640]{1,0:T(8,128)S(1)} %get-tuple-element.21.mine_ref), channel_id=1, source_target_pairs={{0,8},{1,9},{2,10},{3,11},{4,12},{5,13},{6,14},{7,15},{8,0},{9,1},... | collective-permute-start | bytes 61448 | tf_op jit(solution)/shard_map/ppermute | solution.py:337
  128.4 4.0 %collective-permute-start.19 = (f32[8,640]{1,0:T(8,128)S(1)}, f32[8,640]{1,0:T(8,128)S(1)}, u32[]{:S(2)}, u32[]{:S(2)}) collective-permute-start(f32[8,640]{1,0:T(8,128)S(1)} %add_core.5.mine_ref), channel_id=1, source_target_pairs={{0,132},{1,133},{2,134},{3,135},{4,128},{5,129},{6,130},{7,131},{8... | collective-permute-start | bytes 61448 | tf_op jit(solution)/shard_map/ppermute | solution.py:338
  130.4 4.1 %collective-permute-start.20 = (f32[8,640]{1,0:T(8,128)S(1)}, f32[8,640]{1,0:T(8,128)S(1)}, u32[]{:S(2)}, u32[]{:S(2)}) collective-permute-start(f32[8,640]{1,0:T(8,128)S(1)} %add_core.5.mine_ref), channel_id=1, source_target_pairs={{0,128},{1,129},{2,130},{3,131},{4,132},{5,133},{6,134},{7,135},{8... | collective-permute-start | bytes 61448 | tf_op jit(solution)/shard_map/ppermute | solution.py:338
  130.5 4.0 %collective-permute-start.21 = (f32[8,640]{1,0:T(8,128)S(1)}, f32[8,640]{1,0:T(8,128)S(1)}, u32[]{:S(2)}, u32[]{:S(2)}) collective-permute-start(f32[8,640]{1,0:T(8,128)S(1)} %add_core.5.mine_ref), channel_id=1, source_target_pairs={{0,4},{1,5},{2,6},{3,7},{4,0},{5,1},{6,2},{7,3},{8,12},{9,13},{10,... | collective-permute-start | bytes 61448 | tf_op jit(solution)/shard_map/ppermute | solution.py:338
  158.0 10.4 %copy-start.7 = (f32[8,128]{1,0:T(8,128)}, f32[8,128]{1,0:T(8,128)S(1)}, u32[]{:S(2)}) copy-start(f32[8,128]{1,0:T(8,128)S(1)} %get-tuple-element.22.mine_ref.sums_ref) | copy-start | bytes 12292
  158.0 21.8 %copy-start.10 = (s32[5]{0:T(128)S(1)}, s32[5]{0:T(128)}, u32[]{:S(2)}) copy-start(s32[5]{0:T(128)} %copy-done.9) | copy-start | bytes 64
  158.0 21.8 %all-to-all-start.4 = ((f32[32,4,512]{2,1,0:T(4,128)}), f32[32,4,512]{2,1,0:T(4,128)S(1)}, u32[]{:S(2)}, u32[]{:S(2)}) async-start(f32[32,4,512]{2,1,0:T(4,128)} %get-tuple-element.23), calls=%async_computation.4 | async-start | bytes 524288 | tf_op jit(solution)/shard_map/all_to_all | solution.py:350
  165.5 2.8 %collective-permute-start.22 = (f32[8,128]{1,0:T(8,128)S(1)}, f32[8,128]{1,0:T(8,128)S(1)}, u32[]{:S(2)}, u32[]{:S(2)}) collective-permute-start(f32[8,128]{1,0:T(8,128)S(1)} %get-tuple-element.22.mine_ref.sums_ref), channel_id=1, source_target_pairs={{0,4},{1,5},{2,6},{3,7},{4,0},{5,1},{6,2},{7,3},{8,12},{9,13},{10,... | collective-permute-start | bytes 12296 | tf_op jit(solution)/shard_map/ppermute | solution.py:351
  (8 other events, 5.7 us)
Sparse Core Ops, SparseCore 0:
  10.6 156.4 all-gather.1
where the time goes:
time: 189 us
  blocking collectives  51.6 us (27%)
  starting transfers between devices  48.9 us (26%)
  waiting for transfers between devices  38.9 us (21%)
  Pallas kernels  26.2 us (14%)
  between operations  14.2 us (8%)
  local copies, waits for them, and re-layouts  8.89 us (5%)
    all_to_all x3, blocking collectives, exchange(): lax.all_to_all(value, BOTH, 0, 0, axis_index_groups=group, tiled=True)  51.6 us
    ppermute x3, waiting for transfers between devices, per_device(): near[dyh, dyl] = lax.ppermute(patch_protos, BOTH, swap(dyh=dyh, dyl=dyl))  15.3 us
    pallas_call x1, Pallas kernels, final(): pl.pallas_call(final_body, out_shape=shape((256, 16384), BF16), in_specs=...  10.8 us
    ppermute x9, starting transfers between devices, per_device(): lax.ppermute(message, BOTH, swap(dyh=dyh, dyl=dyl))  9.76 us
    ppermute x9, waiting for transfers between devices, per_device(): lax.ppermute(message, BOTH, swap(dyh=dyh, dyl=dyl))  9.46 us
    unnamed x28, local copies, waits for them, and re-layouts  8.81 us
    ppermute x3, starting transfers between devices, per_device(): lax.ppermute(message, BOTH, CORE)  8.41 us
    all_to_all x1, starting transfers between devices, exchange(): lax.all_to_all(value, BOTH, 0, 0, axis_index_groups=group, tiled=True)  8.19 us
  transfers between devices with their start and end apart: 26, of which 16 were waited for; matrix products, arithmetic and copies ran while one was open for 0% of the time, Pallas kernels for 13%

commit v1 on v0

--- a/solution.py
+++ b/solution.py
@@ -47,6 +47,7 @@
 CORE = swap(dcore=1)
 Y_STEPS = ((1, 1), (1, 0), (0, 1))
 GROUPS_Z = groups(lambda core, z, yh, x, yl: (core, yh, x, yl))
+GROUPS_ZC = groups(lambda core, z, yh, x, yl: (yh, x, yl))
 GROUPS_ZX = groups(lambda core, z, yh, x, yl: (core, yh, yl))
 
 
@@ -242,54 +243,60 @@
         out_ref[:, d * 512 : d * 512 + 512] = (scaled_ref[d] * scale).astype(BF16)
 
 
-WIDTH = 2048
+PARTS = 8
 
 
 def final_body(
-    where_ref, protos_ref, units_ref, cols_ref, mine_ref, other_ref, out_ref, wide_ref, in_ref, stage_ref, in_sems, out_sems
+    where_ref, near_ref, far_ref, units_ref, cols_ref, mine_ref, other_ref, out_ref, wide_ref, in_ref, stage_ref, in_sems, out_sems
 ):
-    parts = 16384 // WIDTH
-    lanes = [slice(n * WIDTH, n * WIDTH + WIDTH) for n in range(parts)]
-    ins = [pltpu.make_async_copy(protos_ref.at[:, lanes[n]], in_ref.at[n], in_sems.at[n]) for n in range(parts)]
-    outs = [pltpu.make_async_copy(stage_ref.at[n], out_ref.at[:, lanes[n]], out_sems.at[n]) for n in range(parts)]
+    yh, yl = where_ref[2], where_ref[4]
+    ins, outs, begins = [], [], []
+    for n in range(PARTS):
+        source = near_ref if n < PARTS // 2 else far_ref
+        part = n % (PARTS // 2)
+        begin = (yh if n < PARTS // 2 else 1 - yh) * 16 + part * 4
+        lanes = pl.ds(pl.multiple_of(begin * 512, 2048), 2048)
+        begins.append(begin)
+        ins.append(pltpu.make_async_copy(source.at[pl.ds(part * 4, 4)], in_ref.at[n], in_sems.at[n]))
+        outs.append(pltpu.make_async_copy(stage_ref.at[n], out_ref.at[:, lanes], out_sems.at[n]))
     for copy in ins:
         copy.start()
-    yl = where_ref[4]
     mine, other = mine_ref[:1], other_ref[:1]
     wide_ref[:128] = PROTOS / down(jnp.where(yl == 0, mine, other))
     wide_ref[128:] = PROTOS / down(jnp.where(yl == 0, other, mine))
-    for n in range(parts):
+    for n in range(PARTS):
         ins[n].wait()
-        for at in range(0, WIDTH, 256):
-            protos = in_ref[n, :, at : at + 256]
-            cols = cols_ref[n * (WIDTH // 512) + at // 512][:, at % 512 : at % 512 + 256]
-            dots = jnp.dot(units_ref[...], protos, preferred_element_type=F32)
-            value = jnp.exp2(dots * inv_norms(protos) - SLOPE) * cols
-            for q in (0, 128):
-                scaled = value[:, q : q + 128] * wide_ref[...]
-                stage_ref[n, :, at + q : at + q + 128] = scaled.astype(BF16)
+        for piece in range(4):
+            for at in (0, 256):
+                protos = in_ref[n, piece, :, at : at + 256]
+                cols = cols_ref[begins[n] + piece][:, at : at + 256]
+                dots = jnp.dot(units_ref[...], protos, preferred_element_type=F32)
+                value = jnp.exp2(dots * inv_norms(protos) - SLOPE) * cols
+                for q in (0, 128):
+                    scaled = value[:, q : q + 128] * wide_ref[...]
+                    to = piece * 512 + at + q
+                    stage_ref[n, :, to : to + 128] = scaled.astype(BF16)
         outs[n].start()
     for copy in outs:
         copy.wait()
 
 
-def final(where, protos, units, cols, mine, other):
-    parts = 16384 // WIDTH
+def final(where, near, far, units, cols, mine, other):
     return pl.pallas_call(
         final_body,
         out_shape=shape((256, 16384), BF16),
-        in_specs=[SM, HBM, VM, VM, VM, VM],
+        in_specs=[SM, HBM, HBM, VM, VM, VM, VM],
         out_specs=pl.BlockSpec(memory_space=pl.ANY),
         scratch_shapes=[
             pltpu.VMEM((256, 128), F32),
-            pltpu.VMEM((parts, 384, WIDTH), BF16),
-            pltpu.VMEM((parts, 256, WIDTH), BF16),
-            pltpu.SemaphoreType.DMA((parts,)),
-            pltpu.SemaphoreType.DMA((parts,)),
+            pltpu.VMEM((PARTS, 4, 384, 512), BF16),
+            pltpu.VMEM((PARTS, 256, 2048), BF16),
+            pltpu.SemaphoreType.DMA((PARTS,)),
+            pltpu.SemaphoreType.DMA((PARTS,)),
         ],
         compiler_params=pltpu.CompilerParams(vmem_limit_bytes=56 * MIB),
         name="final_scale",
-    )(where, protos, units, cols, mine, other)
+    )(where, near, far, units, cols, mine, other)
 
 
 def per_device(cls_features, patch_features, mask_index, cls_protos, patch_protos):
@@ -298,8 +305,6 @@
     x, yl = proto % NX, proto // NX
     where = jnp.stack([core, z, yh, x, yl]).astype(jnp.int32)
 
-    gathered = lax.all_gather(patch_protos, "dp", axis=1, tiled=True)
-
     cls_near = [lax.ppermute(cls_features, BOTH, swap(dcore=c, dyh=h)) for c, h in ((1, 0), (0, 1), (1, 1))]
 
     near = {(0, 0): patch_protos}
@@ -312,6 +317,10 @@
         units_body, (shape((256, 384), BF16), shape((NZ, 144, 384), BF16)), [SM] + [VM] * 6, "units"
     )(where, patch_features, mask_index, cls_features, *cls_near)
     rows = exchange(send, GROUPS_Z)
+
+    held = lax.optimization_barrier((patch_protos, rows, *pieces[1:4]))[0]
+    gathered = [lax.all_gather(held, BOTH, axis_index_groups=GROUPS_ZC)]
+    gathered.append(lax.all_gather(near[1, 0], BOTH, axis_index_groups=GROUPS_ZC))
 
     kern, col_sums = call(
         kernel_body, (pltpu.VMEM((1024, 4096), F32), shape((8, 512))), [VM] * 9, "patch_kernel"
@@ -349,7 +358,7 @@
     cls_scaled = lax.optimization_barrier((done[1], sums))[0]
     cls_scaled = lax.all_to_all(cls_scaled, "dp", 0, 0, tiled=True)
     other = lax.ppermute(sums, BOTH, swap(dyl=1))
-    patch_targets = final(where, gathered, units, cols, sums, other)
+    patch_targets = final(where, *gathered, units, cols, sums, other)
     cls_scaled, patch_targets = lax.optimization_barrier((cls_scaled, patch_targets))
     cls_targets = call(cls_final_body, shape((4, 16384), BF16), [SM, VM, VM], "cls_final")(where, cls_scaled, sums)
     return (cls_targets, patch_targets)

time: 189 us -> 208 us (1.10)
  waiting for transfers between devices: 38.9 us -> 59.9 us
    all_to_all x1, waiting for transfers between devices: 4.22 us -> 23.1 us  [exchange(): lax.all_to_all(value, BOTH, 0, 0, axis_index_groups=group, tiled=True)]
    ppermute x3, waiting for transfers between devices: 15.3 us -> 18.8 us  [per_device(): near[dyh, dyl] = lax.ppermute(patch_protos, BOTH, swap(dyh=dyh, dyl=dyl))]
    ppermute x9, waiting for transfers between devices: 9.46 us -> 6.45 us  [per_device(): lax.ppermute(message, BOTH, swap(dyh=dyh, dyl=dyl))]
    ppermute x4, starting transfers between devices: 4.47 us -> 1.9 us  [per_device(): pieces += [lax.ppermute(piece, BOTH, CORE) for piece in pieces]]
  transfers between devices with their start and end apart: 26 -> 27, of which waited for: 16 -> 21; matrix products, arithmetic and copies ran while one was open for 0% -> 0% of each run, Pallas kernels for 13% -> 12%
where the time goes in v1:
time: 208 us; the launch traced here: 207 us
  waiting for transfers between devices  59.9 us (29%)
  blocking collectives  51 us (25%)
  starting transfers between devices  47.3 us (23%)
  Pallas kernels  26.2 us (13%)
  between operations  14.2 us (7%)
  local copies, waits for them, and re-layouts  8.89 us (4%)
    all_to_all x3, blocking collectives, exchange(): lax.all_to_all(value, BOTH, 0, 0, axis_index_groups=group, tiled=True)  51 us
    all_to_all x1, waiting for transfers between devices, exchange(): lax.all_to_all(value, BOTH, 0, 0, axis_index_groups=group, tiled=True)  23.1 us
    ppermute x3, waiting for transfers between devices, per_device(): near[dyh, dyl] = lax.ppermute(patch_protos, BOTH, swap(dyh=dyh, dyl=dyl))  18.8 us
    pallas_call x1, Pallas kernels, final(): pl.pallas_call(final_body, out_shape=shape((256, 16384), BF16), in_specs=...  10.8 us
    ppermute x9, starting transfers between devices, per_device(): lax.ppermute(message, BOTH, swap(dyh=dyh, dyl=dyl))  9.76 us
    unnamed x28, local copies, waits for them, and re-layouts  8.8 us
    all_to_all x1, starting transfers between devices, per_device(): cls_scaled = lax.all_to_all(cls_scaled, 'dp', 0, 0, tiled=True)  8.64 us
    all_to_all x1, starting transfers between devices, exchange(): lax.all_to_all(value, BOTH, 0, 0, axis_index_groups=group, tiled=True)  8.19 us
  transfers between devices with their start and end apart: 27, of which 21 were waited for; matrix products, arithmetic and copies ran while one was open for 0% of the time, Pallas kernels for 12%

profile of v1, /device:TPU:1, one launch (start us, length us, event | category | flops | bytes accessed | tf_op | source)
XLA Modules:
  0.0 207.5 jit_solution(3871619607773435702)
XLA Ops:
  7.2 3.8 %collective-permute-start.4 = (bf16[384,512]{1,0:T(8,128)(2,1)}, bf16[384,512]{1,0:T(8,128)(2,1)S(1)}, u32[]{:S(2)}, u32[]{:S(2)}) collective-permute-start(bf16[384,512]{1,0:T(8,128)(2,1)} %refs_0_.1), channel_id=1, source_target_pairs={{0,128},{1,129},{2,130},{3,131},{4,132},{5,133},{6,134},{7,135},{8... | collective-permute-start | bytes 1179656 | tf_op jit(solution)/shard_map/ppermute | solution.py:312
  11.0 8.1 %collective-permute-done.4.refs_2_ = bf16[384,512]{1,0:T(8,128)(2,1)S(1)} collective-permute-done((bf16[384,512]{1,0:T(8,128)(2,1)}, bf16[384,512]{1,0:T(8,128)(2,1)S(1)}, u32[]{:S(2)}, u32[]{:S(2)}) %collective-permute-start.4) | collective-permute-done | bytes 393248 | tf_op jit(solution)/shard_map/ppermute | solution.py:312
  19.9 2.3 %collective-permute-start = (bf16[4,384]{1,0:T(4,128)(2,1)}, bf16[4,384]{1,0:T(4,128)(2,1)S(1)}, u32[]{:S(2)}, u32[]{:S(2)}) collective-permute-start(bf16[4,384]{1,0:T(4,128)(2,1)} %cls_ref.1), channel_id=1, source_target_pairs={{0,8},{1,9},{2,10},{3,11},{4,12},{5,13},{6,14},{7,15},{8,0},{9,1},... | collective-permute-start | bytes 9224 | tf_op jit(solution)/shard_map/ppermute | solution.py:308
  22.2 3.0 %collective-permute-start.1 = (bf16[4,384]{1,0:T(4,128)(2,1)}, bf16[4,384]{1,0:T(4,128)(2,1)S(1)}, u32[]{:S(2)}, u32[]{:S(2)}) collective-permute-start(bf16[4,384]{1,0:T(4,128)(2,1)} %cls_ref.1), channel_id=1, source_target_pairs={{0,128},{1,129},{2,130},{3,131},{4,132},{5,133},{6,134},{7,135},{8... | collective-permute-start | bytes 9224 | tf_op jit(solution)/shard_map/ppermute | solution.py:308
  26.4 3.5 %collective-permute-done.2.c_ref = bf16[4,384]{1,0:T(4,128)(2,1)S(1)} collective-permute-done((bf16[4,384]{1,0:T(4,128)(2,1)}, bf16[4,384]{1,0:T(4,128)(2,1)S(1)}, u32[]{:S(2)}, u32[]{:S(2)}) %collective-permute-start.2) | collective-permute-done | bytes 3104 | tf_op jit(solution)/shard_map/ppermute | solution.py:308
  29.9 1.1 copy-done.3
  32.4 1.9 units.1
  35.0 8.2 %all-to-all-start = ((bf16[8,144,384]{2,1,0:T(8,128)(2,1)}), bf16[8,144,384]{2,1,0:T(8,128)(2,1)S(1)}, u32[]{:S(2)}, u32[]{:S(2)}) async-start(bf16[8,144,384]{2,1,0:T(8,128)(2,1)} %get-tuple-element.16), calls=%async_computation | async-start | bytes 1769472 | tf_op jit(solution)/shard_map/all_to_all | solution.py:55
  44.2 9.5 %collective-permute-done.3.refs_1_ = bf16[384,512]{1,0:T(8,128)(2,1)S(1)} collective-permute-done((bf16[384,512]{1,0:T(8,128)(2,1)}, bf16[384,512]{1,0:T(8,128)(2,1)S(1)}, u32[]{:S(2)}, u32[]{:S(2)}) %collective-permute-start.3) | collective-permute-done | bytes 393248 | tf_op jit(solution)/shard_map/ppermute | solution.py:312
  53.6 1.3 collective-permute-done.5.refs_3_
  54.9 23.1 %all-to-all-done.units_ref = bf16[8,144,384]{2,1,0:T(8,128)(2,1)S(1)} async-done(((bf16[8,144,384]{2,1,0:T(8,128)(2,1)}), bf16[8,144,384]{2,1,0:T(8,128)(2,1)S(1)}, u32[]{:S(2)}, u32[]{:S(2)}) %all-to-all-start) | async-done | bytes 884768 | tf_op jit(solution)/shard_map/all_to_all | solution.py:55
  78.1 1.3 collective-permute-start.6
  84.6 4.7 %patch_kernel.1 = (f32[1024,4096]{1,0:T(8,128)S(1)}, f32[8,512]{1,0:T(8,128)S(1)}) custom-call(bf16[8,144,384]{2,1,0:T(8,128)(2,1)S(1)} %all-to-all-done.units_ref, bf16[384,512]{1,0:T(8,128)(2,1)S(1)} %copy-done, bf16[384,512]{1,0:T(8,128)(2,1)S(1)} %collective-permute-done.3.refs_1_, bf16[384,512]{1,0:T(8,128)(2,1)S(1)} %copy-done.2, ...), custom_call_target="tpu_custom_call" | custom-call | tf_op jit(solution)/shard_map/patch_kernel/pallas_call | solution.py:325
  92.8 1.5 collective-permute-start.12
  96.9 1.2 row_sums.3
  98.2 18.4 %all_to_all.25.got_ref = f32[32,16,128]{2,1,0:T(8,128)S(1)} all-to-all(f32[32,16,128]{2,1,0:T(8,128)S(1)} %row_sums.3), channel_id=1, replica_groups={{0,1,2,3,16,17,18,19,32,33,34,35,48,49,50,51,64,65,66,67,80,81,82,83,96..., dimensions={0} | all-to-all | bytes 524288 | tf_op jit(solution)/shard_map/all_to_all | solution.py:55
  116.5 1.4 column_sums.2.mine_ref
  117.9 3.9 %collective-permute-start.14 = (f32[8,640]{1,0:T(8,128)S(1)}, f32[8,640]{1,0:T(8,128)S(1)}, u32[]{:S(2)}, u32[]{:S(2)}) collective-permute-start(f32[8,640]{1,0:T(8,128)S(1)} %column_sums.2.mine_ref), channel_id=1, source_target_pairs={{0,8},{1,9},{2,10},{3,11},{4,12},{5,13},{6,14},{7,15},{8,0},{9,1},... | collective-permute-start | bytes 61448 | tf_op jit(solution)/shard_map/ppermute | solution.py:346
  122.6 1.8 collective-permute-start.15
  126.9 1.7 collective-permute-done.16.b_ref
  128.8 1.2 row_sums.4
  130.0 17.6 %all_to_all.26.got_ref = f32[32,16,128]{2,1,0:T(8,128)S(1)} all-to-all(f32[32,16,128]{2,1,0:T(8,128)S(1)} %row_sums.4), channel_id=1, replica_groups={{0,1,2,3,16,17,18,19,32,33,34,35,48,49,50,51,64,65,66,67,80,81,82,83,96..., dimensions={0} | all-to-all | bytes 524288 | tf_op jit(solution)/shard_map/all_to_all | solution.py:55
  147.6 1.4 column_sums.3
  149.0 3.1 %collective-permute-start.18 = (f32[8,640]{1,0:T(8,128)S(1)}, f32[8,640]{1,0:T(8,128)S(1)}, u32[]{:S(2)}, u32[]{:S(2)}) collective-permute-start(f32[8,640]{1,0:T(8,128)S(1)} %get-tuple-element.22.mine_ref), channel_id=1, source_target_pairs={{0,8},{1,9},{2,10},{3,11},{4,12},{5,13},{6,14},{7,15},{8,0},{9,1},... | collective-permute-start | bytes 61448 | tf_op jit(solution)/shard_map/ppermute | solution.py:346
  155.0 1.2 collective-permute-start.21
  156.8 1.3 collective-permute-done.20.b_ref
  158.1 1.2 row_sums.5
  159.4 15.1 %all_to_all.27.got_ref = f32[32,24,128]{2,1,0:T(8,128)S(1)} all-to-all(f32[32,24,128]{2,1,0:T(8,128)S(1)} %row_sums.5), channel_id=1, replica_groups={{0,1,2,3,16,17,18,19,32,33,34,35,48,49,50,51,64,65,66,67,80,81,82,83,96..., dimensions={0} | all-to-all | bytes 786432 | tf_op jit(solution)/shard_map/all_to_all | solution.py:55
  175.7 8.6 %all-to-all-start.4 = ((f32[32,4,512]{2,1,0:T(4,128)}), f32[32,4,512]{2,1,0:T(4,128)S(1)}, u32[]{:S(2)}, u32[]{:S(2)}) async-start(f32[32,4,512]{2,1,0:T(4,128)} %get-tuple-element.24), calls=%async_computation.4 | async-start | bytes 524288 | tf_op jit(solution)/shard_map/all_to_all | solution.py:359
  185.3 1.8 collective-permute-done.22.other_ref
  187.7 10.8 %final_scale.1 = bf16[256,16384]{1,0:T(8,128)(2,1)} custom-call(s32[5]{0:T(128)} %copy-done.9, bf16[16,384,512]{2,1,0:T(8,128)(2,1)} %bitcast.8, bf16[16,384,512]{2,1,0:T(8,128)(2,1)} %bitcast.7, bf16[256,384]{1,0:T(8,128)(2,1)} %copy-done.5, f32[32,1,512]{2,1,0:T(1,128)} %copy-done.6, f32[8,128]{1,0:T(8,128)} %copy-done.7, f32[8,128]{1,0:T(8,128)} %copy-done.13), custom_call_target="tpu_custom_call" | custom-call | tf_op jit(solution)/shard_map/final_scale/pallas_call | solution.py:285
  199.2 1.4 cls_final.1
  (70 shorter events, 27.0 us)
Async XLA Ops:
  7.2 180.0 %all-gather.7.cloned.1.call-start = ((), (), s32[]{:S(2)}) async-start(), calls=%async_computation.6 | async-start | bytes 6684672 | tf_op jit(solution)/shard_map/all_gather | solution.py:323
  7.2 11.9 %collective-permute-start.4 = (bf16[384,512]{1,0:T(8,128)(2,1)}, bf16[384,512]{1,0:T(8,128)(2,1)S(1)}, u32[]{:S(2)}, u32[]{:S(2)}) collective-permute-start(bf16[384,512]{1,0:T(8,128)(2,1)} %refs_0_.1), channel_id=1, source_target_pairs={{0,128},{1,129},{2,130},{3,131},{4,132},{5,133},{6,134},{7,135},{8... | collective-permute-start | bytes 1179656 | tf_op jit(solution)/shard_map/ppermute | solution.py:312
  19.9 5.6 %collective-permute-start = (bf16[4,384]{1,0:T(4,128)(2,1)}, bf16[4,384]{1,0:T(4,128)(2,1)S(1)}, u32[]{:S(2)}, u32[]{:S(2)}) collective-permute-start(bf16[4,384]{1,0:T(4,128)(2,1)} %cls_ref.1), channel_id=1, source_target_pairs={{0,8},{1,9},{2,10},{3,11},{4,12},{5,13},{6,14},{7,15},{8,0},{9,1},... | collective-permute-start | bytes 9224 | tf_op jit(solution)/shard_map/ppermute | solution.py:308
  22.2 4.2 %collective-permute-start.1 = (bf16[4,384]{1,0:T(4,128)(2,1)}, bf16[4,384]{1,0:T(4,128)(2,1)S(1)}, u32[]{:S(2)}, u32[]{:S(2)}) collective-permute-start(bf16[4,384]{1,0:T(4,128)(2,1)} %cls_ref.1), channel_id=1, source_target_pairs={{0,128},{1,129},{2,130},{3,131},{4,132},{5,133},{6,134},{7,135},{8... | collective-permute-start | bytes 9224 | tf_op jit(solution)/shard_map/ppermute | solution.py:308
  25.2 4.7 %collective-permute-start.2 = (bf16[4,384]{1,0:T(4,128)(2,1)}, bf16[4,384]{1,0:T(4,128)(2,1)S(1)}, u32[]{:S(2)}, u32[]{:S(2)}) collective-permute-start(bf16[4,384]{1,0:T(4,128)(2,1)} %cls_ref.1), channel_id=1, source_target_pairs={{0,136},{1,137},{2,138},{3,139},{4,140},{5,141},{6,142},{7,143},{8... | collective-permute-start | bytes 9224 | tf_op jit(solution)/shard_map/ppermute | solution.py:308
  25.5 148.9 %copy-start.9 = (s32[5]{0:T(128)}, s32[5]{0:T(128)S(1)}, u32[]{:S(2)}) copy-start(s32[5]{0:T(128)S(1)} %stack.23.where_ref) | copy-start | bytes 64
  29.9 1.1 copy-start.3
  35.0 43.0 %all-to-all-start = ((bf16[8,144,384]{2,1,0:T(8,128)(2,1)}), bf16[8,144,384]{2,1,0:T(8,128)(2,1)S(1)}, u32[]{:S(2)}, u32[]{:S(2)}) async-start(bf16[8,144,384]{2,1,0:T(8,128)(2,1)} %get-tuple-element.16), calls=%async_computation | async-start | bytes 1769472 | tf_op jit(solution)/shard_map/all_to_all | solution.py:55
  43.2 144.0 %all-gather.5.cloned.1.call-start = ((), (), s32[]{:S(2)}) async-start(), calls=%async_computation.5 | async-start | bytes 6684672 | tf_op jit(solution)/shard_map/all_gather | solution.py:322
  43.2 10.4 %collective-permute-start.3 = (bf16[384,512]{1,0:T(8,128)(2,1)}, bf16[384,512]{1,0:T(8,128)(2,1)S(1)}, u32[]{:S(2)}, u32[]{:S(2)}) collective-permute-start(bf16[384,512]{1,0:T(8,128)(2,1)} %refs_0_.1), channel_id=1, source_target_pairs={{0,4},{1,5},{2,6},{3,7},{4,0},{5,1},{6,2},{7,3},{8,12},{9,13},{10,... | collective-permute-start | bytes 1179656 | tf_op jit(solution)/shard_map/ppermute | solution.py:312
  43.7 11.2 %collective-permute-start.5 = (bf16[384,512]{1,0:T(8,128)(2,1)}, bf16[384,512]{1,0:T(8,128)(2,1)S(1)}, u32[]{:S(2)}, u32[]{:S(2)}) collective-permute-start(bf16[384,512]{1,0:T(8,128)(2,1)} %refs_0_.1), channel_id=1, source_target_pairs={{0,132},{1,133},{2,134},{3,135},{4,128},{5,129},{6,130},{7,131},{8... | collective-permute-start | bytes 1179656 | tf_op jit(solution)/shard_map/ppermute | solution.py:312
  78.1 2.8 %collective-permute-start.6 = (bf16[384,512]{1,0:T(8,128)(2,1)}, bf16[384,512]{1,0:T(8,128)(2,1)S(1)}, u32[]{:S(2)}, u32[]{:S(2)}) collective-permute-start(bf16[384,512]{1,0:T(8,128)(2,1)} %refs_0_.1), channel_id=1, source_target_pairs={{0,8},{1,9},{2,10},{3,11},{4,12},{5,13},{6,14},{7,15},{8,0},{9,1},... | collective-permute-start | bytes 1179656 | tf_op jit(solution)/shard_map/ppermute | solution.py:314
  79.3 2.6 %collective-permute-start.7 = (bf16[384,512]{1,0:T(8,128)(2,1)S(1)}, bf16[384,512]{1,0:T(8,128)(2,1)S(1)}, u32[]{:S(2)}, u32[]{:S(2)}) collective-permute-start(bf16[384,512]{1,0:T(8,128)(2,1)S(1)} %collective-permute-done.3.refs_1_), channel_id=1, source_target_pairs={{0,8},{1,9},{2,10},{3,11},{4,12},{5,13},{6,14},{7,15},{8,0},{9,1},... | collective-permute-start | bytes 1179656 | tf_op jit(solution)/shard_map/ppermute | solution.py:314
  79.4 2.7 %collective-permute-start.8 = (bf16[384,512]{1,0:T(8,128)(2,1)}, bf16[384,512]{1,0:T(8,128)(2,1)S(1)}, u32[]{:S(2)}, u32[]{:S(2)}) collective-permute-start(bf16[384,512]{1,0:T(8,128)(2,1)} %copy-done.1), channel_id=1, source_target_pairs={{0,8},{1,9},{2,10},{3,11},{4,12},{5,13},{6,14},{7,15},{8,0},{9,1},... | collective-permute-start | bytes 1179656 | tf_op jit(solution)/shard_map/ppermute | solution.py:314
  79.8 2.8 %collective-permute-start.9 = (bf16[384,512]{1,0:T(8,128)(2,1)S(1)}, bf16[384,512]{1,0:T(8,128)(2,1)S(1)}, u32[]{:S(2)}, u32[]{:S(2)}) collective-permute-start(bf16[384,512]{1,0:T(8,128)(2,1)S(1)} %collective-permute-done.5.refs_3_), channel_id=1, source_target_pairs={{0,8},{1,9},{2,10},{3,11},{4,12},{5,13},{6,14},{7,15},{8,0},{9,1},... | collective-permute-start | bytes 1179656 | tf_op jit(solution)/shard_map/ppermute | solution.py:314
  89.3 1.0 copy-start.4
  90.7 1.3 collective-permute-start.10
  92.0 3.8 %collective-permute-start.11 = (f32[8,640]{1,0:T(8,128)S(1)}, f32[8,640]{1,0:T(8,128)S(1)}, u32[]{:S(2)}, u32[]{:S(2)}) collective-permute-start(f32[8,640]{1,0:T(8,128)S(1)} %add_core.3.mine_ref), channel_id=1, source_target_pairs={{0,132},{1,133},{2,134},{3,135},{4,128},{5,129},{6,130},{7,131},{8... | collective-permute-start | bytes 61448 | tf_op jit(solution)/shard_map/ppermute | solution.py:347
  92.8 4.1 %collective-permute-start.12 = (f32[8,640]{1,0:T(8,128)S(1)}, f32[8,640]{1,0:T(8,128)S(1)}, u32[]{:S(2)}, u32[]{:S(2)}) collective-permute-start(f32[8,640]{1,0:T(8,128)S(1)} %add_core.3.mine_ref), channel_id=1, source_target_pairs={{0,128},{1,129},{2,130},{3,131},{4,132},{5,133},{6,134},{7,135},{8... | collective-permute-start | bytes 61448 | tf_op jit(solution)/shard_map/ppermute | solution.py:347
  94.3 2.7 %collective-permute-start.13 = (f32[8,640]{1,0:T(8,128)S(1)}, f32[8,640]{1,0:T(8,128)S(1)}, u32[]{:S(2)}, u32[]{:S(2)}) collective-permute-start(f32[8,640]{1,0:T(8,128)S(1)} %add_core.3.mine_ref), channel_id=1, source_target_pairs={{0,4},{1,5},{2,6},{3,7},{4,0},{5,1},{6,2},{7,3},{8,12},{9,13},{10,... | collective-permute-start | bytes 61448 | tf_op jit(solution)/shard_map/ppermute | solution.py:347
  117.9 4.7 %collective-permute-start.14 = (f32[8,640]{1,0:T(8,128)S(1)}, f32[8,640]{1,0:T(8,128)S(1)}, u32[]{:S(2)}, u32[]{:S(2)}) collective-permute-start(f32[8,640]{1,0:T(8,128)S(1)} %column_sums.2.mine_ref), channel_id=1, source_target_pairs={{0,8},{1,9},{2,10},{3,11},{4,12},{5,13},{6,14},{7,15},{8,0},{9,1},... | collective-permute-start | bytes 61448 | tf_op jit(solution)/shard_map/ppermute | solution.py:346
  122.6 4.2 %collective-permute-start.15 = (f32[8,640]{1,0:T(8,128)S(1)}, f32[8,640]{1,0:T(8,128)S(1)}, u32[]{:S(2)}, u32[]{:S(2)}) collective-permute-start(f32[8,640]{1,0:T(8,128)S(1)} %add_core.4.mine_ref), channel_id=1, source_target_pairs={{0,132},{1,133},{2,134},{3,135},{4,128},{5,129},{6,130},{7,131},{8... | collective-permute-start | bytes 61448 | tf_op jit(solution)/shard_map/ppermute | solution.py:347
  124.4 4.2 %collective-permute-start.16 = (f32[8,640]{1,0:T(8,128)S(1)}, f32[8,640]{1,0:T(8,128)S(1)}, u32[]{:S(2)}, u32[]{:S(2)}) collective-permute-start(f32[8,640]{1,0:T(8,128)S(1)} %add_core.4.mine_ref), channel_id=1, source_target_pairs={{0,128},{1,129},{2,130},{3,131},{4,132},{5,133},{6,134},{7,135},{8... | collective-permute-start | bytes 61448 | tf_op jit(solution)/shard_map/ppermute | solution.py:347
  125.6 3.2 %collective-permute-start.17 = (f32[8,640]{1,0:T(8,128)S(1)}, f32[8,640]{1,0:T(8,128)S(1)}, u32[]{:S(2)}, u32[]{:S(2)}) collective-permute-start(f32[8,640]{1,0:T(8,128)S(1)} %add_core.4.mine_ref), channel_id=1, source_target_pairs={{0,4},{1,5},{2,6},{3,7},{4,0},{5,1},{6,2},{7,3},{8,12},{9,13},{10,... | collective-permute-start | bytes 61448 | tf_op jit(solution)/shard_map/ppermute | solution.py:347
  149.0 4.0 %collective-permute-start.18 = (f32[8,640]{1,0:T(8,128)S(1)}, f32[8,640]{1,0:T(8,128)S(1)}, u32[]{:S(2)}, u32[]{:S(2)}) collective-permute-start(f32[8,640]{1,0:T(8,128)S(1)} %get-tuple-element.22.mine_ref), channel_id=1, source_target_pairs={{0,8},{1,9},{2,10},{3,11},{4,12},{5,13},{6,14},{7,15},{8,0},{9,1},... | collective-permute-start | bytes 61448 | tf_op jit(solution)/shard_map/ppermute | solution.py:346
  153.0 3.8 %collective-permute-start.19 = (f32[8,640]{1,0:T(8,128)S(1)}, f32[8,640]{1,0:T(8,128)S(1)}, u32[]{:S(2)}, u32[]{:S(2)}) collective-permute-start(f32[8,640]{1,0:T(8,128)S(1)} %add_core.5.mine_ref), channel_id=1, source_target_pairs={{0,132},{1,133},{2,134},{3,135},{4,128},{5,129},{6,130},{7,131},{8... | collective-permute-start | bytes 61448 | tf_op jit(solution)/shard_map/ppermute | solution.py:347
  154.0 4.1 %collective-permute-start.20 = (f32[8,640]{1,0:T(8,128)S(1)}, f32[8,640]{1,0:T(8,128)S(1)}, u32[]{:S(2)}, u32[]{:S(2)}) collective-permute-start(f32[8,640]{1,0:T(8,128)S(1)} %add_core.5.mine_ref), channel_id=1, source_target_pairs={{0,128},{1,129},{2,130},{3,131},{4,132},{5,133},{6,134},{7,135},{8... | collective-permute-start | bytes 61448 | tf_op jit(solution)/shard_map/ppermute | solution.py:347
  155.0 3.1 %collective-permute-start.21 = (f32[8,640]{1,0:T(8,128)S(1)}, f32[8,640]{1,0:T(8,128)S(1)}, u32[]{:S(2)}, u32[]{:S(2)}) collective-permute-start(f32[8,640]{1,0:T(8,128)S(1)} %add_core.5.mine_ref), channel_id=1, source_target_pairs={{0,4},{1,5},{2,6},{3,7},{4,0},{5,1},{6,2},{7,3},{8,12},{9,13},{10,... | collective-permute-start | bytes 61448 | tf_op jit(solution)/shard_map/ppermute | solution.py:347
  175.7 11.5 %copy-start.7 = (f32[8,128]{1,0:T(8,128)}, f32[8,128]{1,0:T(8,128)S(1)}, u32[]{:S(2)}) copy-start(f32[8,128]{1,0:T(8,128)S(1)} %get-tuple-element.23.mine_ref.sums_ref) | copy-start | bytes 12292
  175.7 22.8 %all-to-all-start.4 = ((f32[32,4,512]{2,1,0:T(4,128)}), f32[32,4,512]{2,1,0:T(4,128)S(1)}, u32[]{:S(2)}, u32[]{:S(2)}) async-start(f32[32,4,512]{2,1,0:T(4,128)} %get-tuple-element.24), calls=%async_computation.4 | async-start | bytes 524288 | tf_op jit(solution)/shard_map/all_to_all | solution.py:359
  184.3 2.8 %collective-permute-start.22 = (f32[8,128]{1,0:T(8,128)S(1)}, f32[8,128]{1,0:T(8,128)S(1)}, u32[]{:S(2)}, u32[]{:S(2)}) collective-permute-start(f32[8,128]{1,0:T(8,128)S(1)} %get-tuple-element.23.mine_ref.sums_ref), channel_id=1, source_target_pairs={{0,4},{1,5},{2,6},{3,7},{4,0},{5,1},{6,2},{7,3},{8,12},{9,13},{10,... | collective-permute-start | bytes 12296 | tf_op jit(solution)/shard_map/ppermute | solution.py:360
  187.7 10.8 %copy-start.10 = (s32[5]{0:T(128)S(1)}, s32[5]{0:T(128)}, u32[]{:S(2)}) copy-start(s32[5]{0:T(128)} %copy-done.9) | copy-start | bytes 64
  (9 other events, 6.7 us)
Sparse Core Ops, SparseCore 0:
  20.1 69.9 all-gather.6
  91.9 55.0 all-gather.4

commit v2 on v1

--- a/solution.py
+++ b/solution.py
@@ -97,14 +97,17 @@
     return (values * lax.rsqrt(jnp.sum(values * values, -1, keepdims=True) + 1e-06)).astype(BF16)
 
 
-def units_body(where_ref, feat_ref, mask_ref, cls_ref, a_ref, b_ref, c_ref, unit_ref, send_ref):
-    core, yh = where_ref[0], where_ref[2]
+def units_body(feat_ref, mask_ref, unit_ref):
     for image in range(4):
         pick = lax.broadcasted_iota(jnp.int32, (256, 64), 0) == mask_ref[image : image + 1, :]
         chosen = lax.dot_general(
             pick.astype(BF16), feat_ref[image], (((0,), (0,)), ((), ())), preferred_element_type=F32
         )
         unit_ref[image * 64 : image * 64 + 64, :] = unit(chosen)
+
+
+def send_body(where_ref, unit_ref, cls_ref, a_ref, b_ref, c_ref, send_ref):
+    core, yh = where_ref[0], where_ref[2]
     half = unit_ref[pl.ds(pl.multiple_of(where_ref[4] * 128, 128), 128), :]
     cls = [unit(ref[...].astype(F32)).astype(F32) for ref in (cls_ref, a_ref, b_ref, c_ref)]
     near = [jnp.where(core == 0, cls[0], cls[1]), jnp.where(core == 0, cls[1], cls[0])]
@@ -313,14 +316,12 @@
     pieces = [near[k // 2, k % 2] for k in range(4)]
     pieces += [lax.ppermute(piece, BOTH, CORE) for piece in pieces]
 
-    units, send = call(
-        units_body, (shape((256, 384), BF16), shape((NZ, 144, 384), BF16)), [SM] + [VM] * 6, "units"
-    )(where, patch_features, mask_index, cls_features, *cls_near)
+    units = call(units_body, shape((256, 384), BF16), [VM] * 2, "units")(patch_features, mask_index)
+    send = call(send_body, shape((NZ, 144, 384), BF16), [SM] + [VM] * 5, "send")(where, units, cls_features, *cls_near)
     rows = exchange(send, GROUPS_Z)
 
-    held = lax.optimization_barrier((patch_protos, rows, *pieces[1:4]))[0]
-    gathered = [lax.all_gather(held, BOTH, axis_index_groups=GROUPS_ZC)]
-    gathered.append(lax.all_gather(near[1, 0], BOTH, axis_index_groups=GROUPS_ZC))
+    held = lax.optimization_barrier((patch_protos, near[1, 0], rows, near[0, 1], near[1, 1]))[:2]
+    gathered = [lax.all_gather(piece, BOTH, axis_index_groups=GROUPS_ZC) for piece in held]
 
     kern, col_sums = call(
         kernel_body, (pltpu.VMEM((1024, 4096), F32), shape((8, 512))), [VM] * 9, "patch_kernel"

time: 208 us -> 186 us (0.89)
  waiting for transfers between devices: 59.9 us -> 37.3 us
  blocking collectives: 51 us -> 56.7 us
  starting transfers between devices: 47.3 us -> 44.8 us
  local copies, waits for them, and re-layouts: 8.89 us -> 6.47 us
    all_to_all x1, waiting for transfers between devices: 23.1 us -> 4.34 us  [exchange(): lax.all_to_all(value, BOTH, 0, 0, axis_index_groups=group, tiled=True)]
    all_to_all x3, blocking collectives: 51 us -> 56.7 us  [exchange(): lax.all_to_all(value, BOTH, 0, 0, axis_index_groups=group, tiled=True)]
    ppermute x3, waiting for transfers between devices: 4.39 us -> 0.4 us  [per_device(): lax.ppermute(cls_features, BOTH, swap(dcore=c, dyh=h))]
    unnamed x28, local copies, waits for them, and re-layouts: 8.8 us -> 6.38 us
  transfers between devices with their start and end apart: 27 -> 27, of which waited for: 21 -> 19; matrix products, arithmetic and copies ran while one was open for 0% -> 0% of each run, Pallas kernels for 12% -> 13%
where the time goes in v2:
time: 186 us
  blocking collectives  56.7 us (30%)
  starting transfers between devices  44.8 us (24%)
  waiting for transfers between devices  37.3 us (20%)
  Pallas kernels  26.2 us (14%)
  between operations  14.2 us (8%)
  local copies, waits for them, and re-layouts  6.47 us (3%)
    all_to_all x3, blocking collectives, exchange(): lax.all_to_all(value, BOTH, 0, 0, axis_index_groups=group, tiled=True)  56.7 us
    ppermute x3, waiting for transfers between devices, per_device(): near[dyh, dyl] = lax.ppermute(patch_protos, BOTH, swap(dyh=dyh, dyl=dyl))  17.4 us
    pallas_call x1, Pallas kernels, final(): pl.pallas_call(final_body, out_shape=shape((256, 16384), BF16), in_specs=...  10.8 us
    ppermute x9, starting transfers between devices, per_device(): lax.ppermute(message, BOTH, swap(dyh=dyh, dyl=dyl))  9.76 us
    all_to_all x1, starting transfers between devices, exchange(): lax.all_to_all(value, BOTH, 0, 0, axis_index_groups=group, tiled=True)  8.19 us
    all_to_all x1, starting transfers between devices, per_device(): cls_scaled = lax.all_to_all(cls_scaled, 'dp', 0, 0, tiled=True)  7.49 us
    ppermute x3, starting transfers between devices, per_device(): lax.ppermute(message, BOTH, CORE)  7.46 us
    ppermute x9, waiting for transfers between devices, per_device(): lax.ppermute(message, BOTH, swap(dyh=dyh, dyl=dyl))  6.65 us
  transfers between devices with their start and end apart: 27, of which 19 were waited for; matrix products, arithmetic and copies ran while one was open for 0% of the time, Pallas kernels for 13%

profile of v2, /device:TPU:1, one launch (start us, length us, event | category | flops | bytes accessed | tf_op | source)
XLA Modules:
  0.0 185.6 jit_solution(8729303080023014099)
XLA Ops:
  7.2 3.3 %collective-permute-start = (bf16[4,384]{1,0:T(4,128)(2,1)}, bf16[4,384]{1,0:T(4,128)(2,1)S(1)}, u32[]{:S(2)}, u32[]{:S(2)}) collective-permute-start(bf16[4,384]{1,0:T(4,128)(2,1)} %cls_ref.1), channel_id=1, source_target_pairs={{0,8},{1,9},{2,10},{3,11},{4,12},{5,13},{6,14},{7,15},{8,0},{9,1},... | collective-permute-start | bytes 9224 | tf_op jit(solution)/shard_map/ppermute | solution.py:311
  10.5 1.2 collective-permute-start.1
  11.7 2.0 %collective-permute-start.2 = (bf16[4,384]{1,0:T(4,128)(2,1)}, bf16[4,384]{1,0:T(4,128)(2,1)S(1)}, u32[]{:S(2)}, u32[]{:S(2)}) collective-permute-start(bf16[4,384]{1,0:T(4,128)(2,1)} %cls_ref.1), channel_id=1, source_target_pairs={{0,136},{1,137},{2,138},{3,139},{4,140},{5,141},{6,142},{7,143},{8... | collective-permute-start | bytes 9224 | tf_op jit(solution)/shard_map/ppermute | solution.py:311
  17.1 1.6 send.1
  18.7 8.2 %all-to-all-start = ((bf16[8,144,384]{2,1,0:T(8,128)(2,1)}), bf16[8,144,384]{2,1,0:T(8,128)(2,1)S(1)}, u32[]{:S(2)}, u32[]{:S(2)}) async-start(bf16[8,144,384]{2,1,0:T(8,128)(2,1)} %send.1), calls=%async_computation | async-start | bytes 1769472 | tf_op jit(solution)/shard_map/all_to_all | solution.py:55
  27.4 1.6 collective-permute-start.4
  28.9 1.9 %collective-permute-start.5 = (bf16[384,512]{1,0:T(8,128)(2,1)}, bf16[384,512]{1,0:T(8,128)(2,1)S(1)}, u32[]{:S(2)}, u32[]{:S(2)}) collective-permute-start(bf16[384,512]{1,0:T(8,128)(2,1)} %refs_0_.1), channel_id=1, source_target_pairs={{0,132},{1,133},{2,134},{3,135},{4,128},{5,129},{6,130},{7,131},{8... | collective-permute-start | bytes 1179656 | tf_op jit(solution)/shard_map/ppermute | solution.py:315
  30.9 6.4 %collective-permute-done.3.refs_1_ = bf16[384,512]{1,0:T(8,128)(2,1)S(1)} collective-permute-done((bf16[384,512]{1,0:T(8,128)(2,1)}, bf16[384,512]{1,0:T(8,128)(2,1)S(1)}, u32[]{:S(2)}, u32[]{:S(2)}) %collective-permute-start.3) | collective-permute-done | bytes 393248 | tf_op jit(solution)/shard_map/ppermute | solution.py:315
  37.2 9.0 %collective-permute-done.4.refs_2_ = bf16[384,512]{1,0:T(8,128)(2,1)S(1)} collective-permute-done((bf16[384,512]{1,0:T(8,128)(2,1)}, bf16[384,512]{1,0:T(8,128)(2,1)S(1)}, u32[]{:S(2)}, u32[]{:S(2)}) %collective-permute-start.4) | collective-permute-done | bytes 393248 | tf_op jit(solution)/shard_map/ppermute | solution.py:315
  46.2 2.0 %collective-permute-done.5.refs_3_ = bf16[384,512]{1,0:T(8,128)(2,1)S(1)} collective-permute-done((bf16[384,512]{1,0:T(8,128)(2,1)}, bf16[384,512]{1,0:T(8,128)(2,1)S(1)}, u32[]{:S(2)}, u32[]{:S(2)}) %collective-permute-start.5) | collective-permute-done | bytes 393248 | tf_op jit(solution)/shard_map/ppermute | solution.py:315
  48.2 4.3 %all-to-all-done.units_ref = bf16[8,144,384]{2,1,0:T(8,128)(2,1)S(1)} async-done(((bf16[8,144,384]{2,1,0:T(8,128)(2,1)}), bf16[8,144,384]{2,1,0:T(8,128)(2,1)S(1)}, u32[]{:S(2)}, u32[]{:S(2)}) %all-to-all-start) | async-done | bytes 884768 | tf_op jit(solution)/shard_map/all_to_all | solution.py:55
  59.0 4.7 %patch_kernel.1 = (f32[1024,4096]{1,0:T(8,128)S(1)}, f32[8,512]{1,0:T(8,128)S(1)}) custom-call(bf16[8,144,384]{2,1,0:T(8,128)(2,1)S(1)} %all-to-all-done.units_ref, bf16[384,512]{1,0:T(8,128)(2,1)S(1)} %copy-done.1, bf16[384,512]{1,0:T(8,128)(2,1)S(1)} %collective-permute-done.3.refs_1_, bf16[384,512]{1,0:T(8,128)(2,1)S(1)} %copy-done.3, ...), custom_call_target="tpu_custom_call" | custom-call | tf_op jit(solution)/shard_map/patch_kernel/pallas_call | solution.py:326
  66.1 1.4 collective-permute-start.12
  70.6 1.2 row_sums.3
  71.8 21.7 %all_to_all.25.got_ref = f32[32,16,128]{2,1,0:T(8,128)S(1)} all-to-all(f32[32,16,128]{2,1,0:T(8,128)S(1)} %row_sums.3), channel_id=1, replica_groups={{0,1,2,3,16,17,18,19,32,33,34,35,48,49,50,51,64,65,66,67,80,81,82,83,96..., dimensions={0} | all-to-all | bytes 524288 | tf_op jit(solution)/shard_map/all_to_all | solution.py:55
  93.5 1.4 column_sums.2.mine_ref
  94.9 3.3 %collective-permute-start.14 = (f32[8,640]{1,0:T(8,128)S(1)}, f32[8,640]{1,0:T(8,128)S(1)}, u32[]{:S(2)}, u32[]{:S(2)}) collective-permute-start(f32[8,640]{1,0:T(8,128)S(1)} %column_sums.2.mine_ref), channel_id=1, source_target_pairs={{0,8},{1,9},{2,10},{3,11},{4,12},{5,13},{6,14},{7,15},{8,0},{9,1},... | collective-permute-start | bytes 61448 | tf_op jit(solution)/shard_map/ppermute | solution.py:347
  99.9 1.1 collective-permute-start.16
  101.0 1.3 collective-permute-start.17
  102.9 1.1 collective-permute-done.16.b_ref
  104.0 1.2 row_sums.4
  105.2 13.6 %all_to_all.26.got_ref = f32[32,16,128]{2,1,0:T(8,128)S(1)} all-to-all(f32[32,16,128]{2,1,0:T(8,128)S(1)} %row_sums.4), channel_id=1, replica_groups={{0,1,2,3,16,17,18,19,32,33,34,35,48,49,50,51,64,65,66,67,80,81,82,83,96..., dimensions={0} | all-to-all | bytes 524288 | tf_op jit(solution)/shard_map/all_to_all | solution.py:55
  118.9 1.4 column_sums.3
  120.3 3.8 %collective-permute-start.18 = (f32[8,640]{1,0:T(8,128)S(1)}, f32[8,640]{1,0:T(8,128)S(1)}, u32[]{:S(2)}, u32[]{:S(2)}) collective-permute-start(f32[8,640]{1,0:T(8,128)S(1)} %get-tuple-element.20.mine_ref), channel_id=1, source_target_pairs={{0,8},{1,9},{2,10},{3,11},{4,12},{5,13},{6,14},{7,15},{8,0},{9,1},... | collective-permute-start | bytes 61448 | tf_op jit(solution)/shard_map/ppermute | solution.py:347
  125.0 2.0 %collective-permute-start.19 = (f32[8,640]{1,0:T(8,128)S(1)}, f32[8,640]{1,0:T(8,128)S(1)}, u32[]{:S(2)}, u32[]{:S(2)}) collective-permute-start(f32[8,640]{1,0:T(8,128)S(1)} %add_core.5.mine_ref), channel_id=1, source_target_pairs={{0,132},{1,133},{2,134},{3,135},{4,128},{5,129},{6,130},{7,131},{8... | collective-permute-start | bytes 61448 | tf_op jit(solution)/shard_map/ppermute | solution.py:348
  129.2 2.0 %collective-permute-done.20.b_ref = f32[8,640]{1,0:T(8,128)S(1)} collective-permute-done((f32[8,640]{1,0:T(8,128)S(1)}, f32[8,640]{1,0:T(8,128)S(1)}, u32[]{:S(2)}, u32[]{:S(2)}) %collective-permute-start.20) | collective-permute-done | bytes 20512 | tf_op jit(solution)/shard_map/ppermute | solution.py:348
  131.2 1.2 row_sums.5
  132.4 21.3 %all_to_all.27.got_ref = f32[32,24,128]{2,1,0:T(8,128)S(1)} all-to-all(f32[32,24,128]{2,1,0:T(8,128)S(1)} %row_sums.5), channel_id=1, replica_groups={{0,1,2,3,16,17,18,19,32,33,34,35,48,49,50,51,64,65,66,67,80,81,82,83,96..., dimensions={0} | all-to-all | bytes 786432 | tf_op jit(solution)/shard_map/all_to_all | solution.py:55
  155.0 7.5 %all-to-all-start.4 = ((f32[32,4,512]{2,1,0:T(4,128)}), f32[32,4,512]{2,1,0:T(4,128)S(1)}, u32[]{:S(2)}, u32[]{:S(2)}) async-start(f32[32,4,512]{2,1,0:T(4,128)} %get-tuple-element.22), calls=%async_computation.4 | async-start | bytes 524288 | tf_op jit(solution)/shard_map/all_to_all | solution.py:360
  162.6 2.7 %collective-permute-done.22.other_ref = f32[8,128]{1,0:T(8,128)S(1)} collective-permute-done((f32[8,128]{1,0:T(8,128)S(1)}, f32[8,128]{1,0:T(8,128)S(1)}, u32[]{:S(2)}, u32[]{:S(2)}) %collective-permute-start.22) | collective-permute-done | bytes 4128 | tf_op jit(solution)/shard_map/ppermute | solution.py:361
  165.9 10.8 %final_scale.1 = bf16[256,16384]{1,0:T(8,128)(2,1)} custom-call(s32[5]{0:T(128)} %copy-done.9, bf16[16,384,512]{2,1,0:T(8,128)(2,1)} %bitcast.7, bf16[16,384,512]{2,1,0:T(8,128)(2,1)} %bitcast.8, bf16[256,384]{1,0:T(8,128)(2,1)} %copy-done, f32[32,1,512]{2,1,0:T(1,128)} %copy-done.6, f32[8,128]{1,0:T(8,128)} %copy-done.7, f32[8,128]{1,0:T(8,128)} %copy-done.13), custom_call_target="tpu_custom_call" | custom-call | tf_op jit(solution)/shard_map/final_scale/pallas_call | solution.py:288
  177.4 1.4 cls_final.1
  (71 shorter events, 23.7 us)
Async XLA Ops:
  7.2 8.9 %collective-permute-start = (bf16[4,384]{1,0:T(4,128)(2,1)}, bf16[4,384]{1,0:T(4,128)(2,1)S(1)}, u32[]{:S(2)}, u32[]{:S(2)}) collective-permute-start(bf16[4,384]{1,0:T(4,128)(2,1)} %cls_ref.1), channel_id=1, source_target_pairs={{0,8},{1,9},{2,10},{3,11},{4,12},{5,13},{6,14},{7,15},{8,0},{9,1},... | collective-permute-start | bytes 9224 | tf_op jit(solution)/shard_map/ppermute | solution.py:311
  10.5 5.5 %collective-permute-start.1 = (bf16[4,384]{1,0:T(4,128)(2,1)}, bf16[4,384]{1,0:T(4,128)(2,1)S(1)}, u32[]{:S(2)}, u32[]{:S(2)}) collective-permute-start(bf16[4,384]{1,0:T(4,128)(2,1)} %cls_ref.1), channel_id=1, source_target_pairs={{0,128},{1,129},{2,130},{3,131},{4,132},{5,133},{6,134},{7,135},{8... | collective-permute-start | bytes 9224 | tf_op jit(solution)/shard_map/ppermute | solution.py:311
  11.7 4.7 %collective-permute-start.2 = (bf16[4,384]{1,0:T(4,128)(2,1)}, bf16[4,384]{1,0:T(4,128)(2,1)S(1)}, u32[]{:S(2)}, u32[]{:S(2)}) collective-permute-start(bf16[4,384]{1,0:T(4,128)(2,1)} %cls_ref.1), channel_id=1, source_target_pairs={{0,136},{1,137},{2,138},{3,139},{4,140},{5,141},{6,142},{7,143},{8... | collective-permute-start | bytes 9224 | tf_op jit(solution)/shard_map/ppermute | solution.py:311
  15.5 48.1 %copy-start.5 = (bf16[384,512]{1,0:T(8,128)(2,1)S(1)}, bf16[384,512]{1,0:T(8,128)(2,1)}, u32[]{:S(2)}) copy-start(bf16[384,512]{1,0:T(8,128)(2,1)} %protos_ref.1) | copy-start | bytes 1179652
  15.9 55.9 %copy-start = (bf16[256,384]{1,0:T(8,128)(2,1)}, bf16[256,384]{1,0:T(8,128)(2,1)S(1)}, u32[]{:S(2)}) copy-start(bf16[256,384]{1,0:T(8,128)(2,1)S(1)} %units.1.unit_ref.units_ref) | copy-start | bytes 589828
  16.0 137.7 %copy-start.9 = (s32[5]{0:T(128)}, s32[5]{0:T(128)S(1)}, u32[]{:S(2)}) copy-start(s32[5]{0:T(128)S(1)} %stack.23.where_ref) | copy-start | bytes 64
  18.7 33.9 %all-to-all-start = ((bf16[8,144,384]{2,1,0:T(8,128)(2,1)}), bf16[8,144,384]{2,1,0:T(8,128)(2,1)S(1)}, u32[]{:S(2)}, u32[]{:S(2)}) async-start(bf16[8,144,384]{2,1,0:T(8,128)(2,1)} %send.1), calls=%async_computation | async-start | bytes 1769472 | tf_op jit(solution)/shard_map/all_to_all | solution.py:55
  26.9 138.4 %all-gather.5.cloned.1.call-start = ((), (), s32[]{:S(2)}) async-start(), calls=%async_computation.5 | async-start | bytes 6684672 | tf_op jit(solution)/shard_map/all_gather | solution.py:324
  26.9 10.3 %collective-permute-start.3 = (bf16[384,512]{1,0:T(8,128)(2,1)}, bf16[384,512]{1,0:T(8,128)(2,1)S(1)}, u32[]{:S(2)}, u32[]{:S(2)}) collective-permute-start(bf16[384,512]{1,0:T(8,128)(2,1)} %refs_0_.1), channel_id=1, source_target_pairs={{0,4},{1,5},{2,6},{3,7},{4,0},{5,1},{6,2},{7,3},{8,12},{9,13},{10,... | collective-permute-start | bytes 1179656 | tf_op jit(solution)/shard_map/ppermute | solution.py:315
  27.4 18.8 %collective-permute-start.4 = (bf16[384,512]{1,0:T(8,128)(2,1)}, bf16[384,512]{1,0:T(8,128)(2,1)S(1)}, u32[]{:S(2)}, u32[]{:S(2)}) collective-permute-start(bf16[384,512]{1,0:T(8,128)(2,1)} %refs_0_.1), channel_id=1, source_target_pairs={{0,128},{1,129},{2,130},{3,131},{4,132},{5,133},{6,134},{7,135},{8... | collective-permute-start | bytes 1179656 | tf_op jit(solution)/shard_map/ppermute | solution.py:315
  28.9 19.3 %collective-permute-start.5 = (bf16[384,512]{1,0:T(8,128)(2,1)}, bf16[384,512]{1,0:T(8,128)(2,1)S(1)}, u32[]{:S(2)}, u32[]{:S(2)}) collective-permute-start(bf16[384,512]{1,0:T(8,128)(2,1)} %refs_0_.1), channel_id=1, source_target_pairs={{0,132},{1,133},{2,134},{3,135},{4,128},{5,129},{6,130},{7,131},{8... | collective-permute-start | bytes 1179656 | tf_op jit(solution)/shard_map/ppermute | solution.py:315
  52.6 112.7 %all-gather.7.cloned.1.call-start = ((), (), s32[]{:S(2)}) async-start(), calls=%async_computation.6 | async-start | bytes 6684672 | tf_op jit(solution)/shard_map/all_gather | solution.py:324
  53.3 2.1 %collective-permute-start.6 = (bf16[384,512]{1,0:T(8,128)(2,1)}, bf16[384,512]{1,0:T(8,128)(2,1)S(1)}, u32[]{:S(2)}, u32[]{:S(2)}) collective-permute-start(bf16[384,512]{1,0:T(8,128)(2,1)} %refs_0_.1), channel_id=1, source_target_pairs={{0,8},{1,9},{2,10},{3,11},{4,12},{5,13},{6,14},{7,15},{8,0},{9,1},... | collective-permute-start | bytes 1179656 | tf_op jit(solution)/shard_map/ppermute | solution.py:317
  53.9 2.5 %collective-permute-start.7 = (bf16[384,512]{1,0:T(8,128)(2,1)S(1)}, bf16[384,512]{1,0:T(8,128)(2,1)S(1)}, u32[]{:S(2)}, u32[]{:S(2)}) collective-permute-start(bf16[384,512]{1,0:T(8,128)(2,1)S(1)} %collective-permute-done.3.refs_1_), channel_id=1, source_target_pairs={{0,8},{1,9},{2,10},{3,11},{4,12},{5,13},{6,14},{7,15},{8,0},{9,1},... | collective-permute-start | bytes 1179656 | tf_op jit(solution)/shard_map/ppermute | solution.py:317
  54.0 3.0 %collective-permute-start.8 = (bf16[384,512]{1,0:T(8,128)(2,1)}, bf16[384,512]{1,0:T(8,128)(2,1)S(1)}, u32[]{:S(2)}, u32[]{:S(2)}) collective-permute-start(bf16[384,512]{1,0:T(8,128)(2,1)} %copy-done.2), channel_id=1, source_target_pairs={{0,8},{1,9},{2,10},{3,11},{4,12},{5,13},{6,14},{7,15},{8,0},{9,1},... | collective-permute-start | bytes 1179656 | tf_op jit(solution)/shard_map/ppermute | solution.py:317
  54.4 2.6 %collective-permute-start.9 = (bf16[384,512]{1,0:T(8,128)(2,1)S(1)}, bf16[384,512]{1,0:T(8,128)(2,1)S(1)}, u32[]{:S(2)}, u32[]{:S(2)}) collective-permute-start(bf16[384,512]{1,0:T(8,128)(2,1)S(1)} %collective-permute-done.5.refs_3_), channel_id=1, source_target_pairs={{0,8},{1,9},{2,10},{3,11},{4,12},{5,13},{6,14},{7,15},{8,0},{9,1},... | collective-permute-start | bytes 1179656 | tf_op jit(solution)/shard_map/ppermute | solution.py:317
  64.1 1.3 collective-permute-start.10
  65.3 4.2 %collective-permute-start.11 = (f32[8,640]{1,0:T(8,128)S(1)}, f32[8,640]{1,0:T(8,128)S(1)}, u32[]{:S(2)}, u32[]{:S(2)}) collective-permute-start(f32[8,640]{1,0:T(8,128)S(1)} %add_core.3.mine_ref), channel_id=1, source_target_pairs={{0,132},{1,133},{2,134},{3,135},{4,128},{5,129},{6,130},{7,131},{8... | collective-permute-start | bytes 61448 | tf_op jit(solution)/shard_map/ppermute | solution.py:348
  66.1 4.1 %collective-permute-start.12 = (f32[8,640]{1,0:T(8,128)S(1)}, f32[8,640]{1,0:T(8,128)S(1)}, u32[]{:S(2)}, u32[]{:S(2)}) collective-permute-start(f32[8,640]{1,0:T(8,128)S(1)} %add_core.3.mine_ref), channel_id=1, source_target_pairs={{0,128},{1,129},{2,130},{3,131},{4,132},{5,133},{6,134},{7,135},{8... | collective-permute-start | bytes 61448 | tf_op jit(solution)/shard_map/ppermute | solution.py:348
  67.5 3.0 %collective-permute-start.13 = (f32[8,640]{1,0:T(8,128)S(1)}, f32[8,640]{1,0:T(8,128)S(1)}, u32[]{:S(2)}, u32[]{:S(2)}) collective-permute-start(f32[8,640]{1,0:T(8,128)S(1)} %add_core.3.mine_ref), channel_id=1, source_target_pairs={{0,4},{1,5},{2,6},{3,7},{4,0},{5,1},{6,2},{7,3},{8,12},{9,13},{10,... | collective-permute-start | bytes 61448 | tf_op jit(solution)/shard_map/ppermute | solution.py:348
  94.9 4.1 %collective-permute-start.14 = (f32[8,640]{1,0:T(8,128)S(1)}, f32[8,640]{1,0:T(8,128)S(1)}, u32[]{:S(2)}, u32[]{:S(2)}) collective-permute-start(f32[8,640]{1,0:T(8,128)S(1)} %column_sums.2.mine_ref), channel_id=1, source_target_pairs={{0,8},{1,9},{2,10},{3,11},{4,12},{5,13},{6,14},{7,15},{8,0},{9,1},... | collective-permute-start | bytes 61448 | tf_op jit(solution)/shard_map/ppermute | solution.py:347
  99.0 3.8 %collective-permute-start.15 = (f32[8,640]{1,0:T(8,128)S(1)}, f32[8,640]{1,0:T(8,128)S(1)}, u32[]{:S(2)}, u32[]{:S(2)}) collective-permute-start(f32[8,640]{1,0:T(8,128)S(1)} %add_core.4.mine_ref), channel_id=1, source_target_pairs={{0,132},{1,133},{2,134},{3,135},{4,128},{5,129},{6,130},{7,131},{8... | collective-permute-start | bytes 61448 | tf_op jit(solution)/shard_map/ppermute | solution.py:348
  99.9 4.1 %collective-permute-start.16 = (f32[8,640]{1,0:T(8,128)S(1)}, f32[8,640]{1,0:T(8,128)S(1)}, u32[]{:S(2)}, u32[]{:S(2)}) collective-permute-start(f32[8,640]{1,0:T(8,128)S(1)} %add_core.4.mine_ref), channel_id=1, source_target_pairs={{0,128},{1,129},{2,130},{3,131},{4,132},{5,133},{6,134},{7,135},{8... | collective-permute-start | bytes 61448 | tf_op jit(solution)/shard_map/ppermute | solution.py:348
  101.0 3.0 %collective-permute-start.17 = (f32[8,640]{1,0:T(8,128)S(1)}, f32[8,640]{1,0:T(8,128)S(1)}, u32[]{:S(2)}, u32[]{:S(2)}) collective-permute-start(f32[8,640]{1,0:T(8,128)S(1)} %add_core.4.mine_ref), channel_id=1, source_target_pairs={{0,4},{1,5},{2,6},{3,7},{4,0},{5,1},{6,2},{7,3},{8,12},{9,13},{10,... | collective-permute-start | bytes 61448 | tf_op jit(solution)/shard_map/ppermute | solution.py:348
  120.3 4.7 %collective-permute-start.18 = (f32[8,640]{1,0:T(8,128)S(1)}, f32[8,640]{1,0:T(8,128)S(1)}, u32[]{:S(2)}, u32[]{:S(2)}) collective-permute-start(f32[8,640]{1,0:T(8,128)S(1)} %get-tuple-element.20.mine_ref), channel_id=1, source_target_pairs={{0,8},{1,9},{2,10},{3,11},{4,12},{5,13},{6,14},{7,15},{8,0},{9,1},... | collective-permute-start | bytes 61448 | tf_op jit(solution)/shard_map/ppermute | solution.py:347
  125.0 4.2 %collective-permute-start.19 = (f32[8,640]{1,0:T(8,128)S(1)}, f32[8,640]{1,0:T(8,128)S(1)}, u32[]{:S(2)}, u32[]{:S(2)}) collective-permute-start(f32[8,640]{1,0:T(8,128)S(1)} %add_core.5.mine_ref), channel_id=1, source_target_pairs={{0,132},{1,133},{2,134},{3,135},{4,128},{5,129},{6,130},{7,131},{8... | collective-permute-start | bytes 61448 | tf_op jit(solution)/shard_map/ppermute | solution.py:348
  127.0 4.2 %collective-permute-start.20 = (f32[8,640]{1,0:T(8,128)S(1)}, f32[8,640]{1,0:T(8,128)S(1)}, u32[]{:S(2)}, u32[]{:S(2)}) collective-permute-start(f32[8,640]{1,0:T(8,128)S(1)} %add_core.5.mine_ref), channel_id=1, source_target_pairs={{0,128},{1,129},{2,130},{3,131},{4,132},{5,133},{6,134},{7,135},{8... | collective-permute-start | bytes 61448 | tf_op jit(solution)/shard_map/ppermute | solution.py:348
  127.9 3.3 %collective-permute-start.21 = (f32[8,640]{1,0:T(8,128)S(1)}, f32[8,640]{1,0:T(8,128)S(1)}, u32[]{:S(2)}, u32[]{:S(2)}) collective-permute-start(f32[8,640]{1,0:T(8,128)S(1)} %add_core.5.mine_ref), channel_id=1, source_target_pairs={{0,4},{1,5},{2,6},{3,7},{4,0},{5,1},{6,2},{7,3},{8,12},{9,13},{10,... | collective-permute-start | bytes 61448 | tf_op jit(solution)/shard_map/ppermute | solution.py:348
  155.0 10.3 %copy-start.7 = (f32[8,128]{1,0:T(8,128)}, f32[8,128]{1,0:T(8,128)S(1)}, u32[]{:S(2)}) copy-start(f32[8,128]{1,0:T(8,128)S(1)} %get-tuple-element.21.mine_ref.sums_ref) | copy-start | bytes 12292
  155.0 21.7 %all-to-all-start.4 = ((f32[32,4,512]{2,1,0:T(4,128)}), f32[32,4,512]{2,1,0:T(4,128)S(1)}, u32[]{:S(2)}, u32[]{:S(2)}) async-start(f32[32,4,512]{2,1,0:T(4,128)} %get-tuple-element.22), calls=%async_computation.4 | async-start | bytes 524288 | tf_op jit(solution)/shard_map/all_to_all | solution.py:360
  162.5 2.8 %collective-permute-start.22 = (f32[8,128]{1,0:T(8,128)S(1)}, f32[8,128]{1,0:T(8,128)S(1)}, u32[]{:S(2)}, u32[]{:S(2)}) collective-permute-start(f32[8,128]{1,0:T(8,128)S(1)} %get-tuple-element.21.mine_ref.sums_ref), channel_id=1, source_target_pairs={{0,4},{1,5},{2,6},{3,7},{4,0},{5,1},{6,2},{7,3},{8,12},{9,13},{10,... | collective-permute-start | bytes 12296 | tf_op jit(solution)/shard_map/ppermute | solution.py:361
  165.9 10.8 %copy-start.10 = (s32[5]{0:T(128)S(1)}, s32[5]{0:T(128)}, u32[]{:S(2)}) copy-start(s32[5]{0:T(128)} %copy-done.9) | copy-start | bytes 64
  (9 other events, 12.8 us)
Sparse Core Ops, SparseCore 0:
  52.7 49.4 all-gather.4
  104.0 54.1 all-gather.6

commit v3 on v2

--- a/solution.py
+++ b/solution.py
@@ -120,24 +120,6 @@
         send_ref[z, 128:, :] = tail
 
 
-def kernel_body(units_ref, *refs):
-    pieces, (kern_ref, sums_ref) = refs[:8], refs[8:]
-    for k in range(8):
-        for half in range(2):
-            lanes = slice(half * 256, half * 256 + 256)
-            protos = pieces[k][:, lanes]
-            scale = inv_norms(protos)
-            total = jnp.zeros((8, 256), F32)
-            for part in range(2):
-                units = units_ref[part * 4 : part * 4 + 4, :128, :].reshape(512, 384)
-                dots = jnp.dot(units, protos, preferred_element_type=F32)
-                value = jnp.exp2(dots * scale - SLOPE)
-                at = k * 512 + half * 256
-                kern_ref[part * 512 : part * 512 + 512, at : at + 256] = value
-                total = total + jnp.sum(value.reshape(64, 8, 256), axis=0)
-            sums_ref[k : k + 1, lanes] = jnp.sum(total, axis=0, keepdims=True)
-
-
 def cls_step(cls_kern, row_scale):
     wide = down(row_scale)
     cols = [
@@ -150,13 +132,34 @@
     return cols, across(total)
 
 
-def cls_body(units_ref, protos_ref, sums_ref, kern_ref, message_ref):
+def kernel_body(rows_ref, cls_ref, *refs):
+    pieces, (kern_ref, cls_kern_ref, message_ref, units_ref, held_ref, sems) = refs[:8], refs[8:]
+    copies = [pltpu.make_async_copy(rows_ref, units_ref, sems.at[9])]
+    copies += [pltpu.make_async_copy(ref, held_ref.at[k], sems.at[k]) for k, ref in enumerate((*pieces, cls_ref))]
+    for copy in copies:
+        copy.start()
+    copies[0].wait()
+    for k in range(8):
+        copies[k + 1].wait()
+        for half in range(2):
+            lanes = slice(half * 256, half * 256 + 256)
+            protos = held_ref[k, :, lanes]
+            scale = inv_norms(protos)
+            total = jnp.zeros((8, 256), F32)
+            for part in range(2):
+                units = units_ref[part * 4 : part * 4 + 4, :128, :].reshape(512, 384)
+                dots = jnp.dot(units, protos, preferred_element_type=F32)
+                value = jnp.exp2(dots * scale - SLOPE)
+                at = k * 512 + half * 256
+                kern_ref[part * 512 : part * 512 + 512, at : at + 256] = value
+                total = total + jnp.sum(value.reshape(64, 8, 256), axis=0)
+            message_ref[k : k + 1, lanes] = jnp.sum(total, axis=0, keepdims=True)
+    copies[9].wait()
     units = jnp.concatenate([units_ref[z, 128:, :] for z in range(NZ)], axis=0)
-    protos = protos_ref[...]
+    protos = held_ref[8]
     dots = jnp.dot(units, protos, preferred_element_type=F32)
-    kern_ref[...] = jnp.exp2(dots * inv_norms(protos) - SLOPE)
-    _, sums = cls_step(kern_ref[...], jnp.ones((1, 128), F32))
-    message_ref[:, :512] = sums_ref[...]
+    cls_kern_ref[...] = jnp.exp2(dots * inv_norms(protos) - SLOPE)
+    _, sums = cls_step(cls_kern_ref[...], jnp.ones((1, 128), F32))
     message_ref[:, 512:] = jnp.broadcast_to(sums, (8, 128))
 
 
@@ -297,7 +300,7 @@
             pltpu.SemaphoreType.DMA((PARTS,)),
             pltpu.SemaphoreType.DMA((PARTS,)),
         ],
-        compiler_params=pltpu.CompilerParams(vmem_limit_bytes=56 * MIB),
+        compiler_params=pltpu.CompilerParams(vmem_limit_bytes=50 * MIB),
         name="final_scale",
     )(where, near, far, units, cols, mine, other)
 
@@ -320,15 +323,21 @@
     send = call(send_body, shape((NZ, 144, 384), BF16), [SM] + [VM] * 5, "send")(where, units, cls_features, *cls_near)
     rows = exchange(send, GROUPS_Z)
 
-    held = lax.optimization_barrier((patch_protos, near[1, 0], rows, near[0, 1], near[1, 1]))[:2]
+    held = lax.optimization_barrier((patch_protos, near[1, 0], rows, *pieces[1:2], *pieces[3:]))[:2]
     gathered = [lax.all_gather(piece, BOTH, axis_index_groups=GROUPS_ZC) for piece in held]
 
-    kern, col_sums = call(
-        kernel_body, (pltpu.VMEM((1024, 4096), F32), shape((8, 512))), [VM] * 9, "patch_kernel"
-    )(rows, *pieces)
-    cls_kern, message = call(cls_body, (shape((128, 512)), shape((8, 640))), [VM] * 3, "cls_kernel")(
-        rows, cls_protos, col_sums
-    )
+    kern, cls_kern, message = call(
+        kernel_body,
+        (pltpu.VMEM((1024, 4096), F32), shape((128, 512)), shape((8, 640))),
+        [HBM] * 10,
+        "patch_kernel",
+        [
+            pltpu.VMEM((NZ, 144, 384), BF16),
+            pltpu.VMEM((9, 384, 512), BF16),
+            pltpu.SemaphoreType.DMA((10,)),
+        ],
+        limit=43,
+    )(rows, cls_protos, *pieces)
 
     for step in range(ITERS):
         last = step == ITERS - 1

time: 186 us -> 184 us (0.989)
  waiting for transfers between devices: 37.3 us -> 26.4 us
  starting transfers between devices: 44.8 us -> 51.7 us
  Pallas kernels: 26.2 us -> 28.9 us
  local copies, waits for them, and re-layouts: 6.47 us -> 4.23 us
    ppermute x4, starting transfers between devices: 1.19 us -> 7.79 us  [per_device(): pieces += [lax.ppermute(piece, BOTH, CORE) for piece in pieces]]
    ppermute x3, waiting for transfers between devices: 17.4 us -> 11.7 us  [per_device(): near[dyh, dyl] = lax.ppermute(patch_protos, BOTH, swap(dyh=dyh, dyl=dyl))]
    all_to_all x1, waiting for transfers between devices: 4.34 us -> 0.73 us  [exchange(): lax.all_to_all(value, BOTH, 0, 0, axis_index_groups=group, tiled=True)]
    pallas_call x2 -> x1, Pallas kernels: 5.02 us -> 8.18 us  [per_device(): call(kernel_body, (pltpu.VMEM((1024, 4096), F32), shape((128, 512)), shap...]
    unnamed x28 -> x24, local copies, waits for them, and re-layouts: 6.38 us -> 4.15 us
    ppermute x4, waiting for transfers between devices: 2.51 us -> 0.64 us  [per_device(): pieces += [lax.ppermute(piece, BOTH, CORE) for piece in pieces]]
  transfers between devices with their start and end apart: 27 -> 27, of which waited for: 19 -> 17; matrix products, arithmetic and copies ran while one was open for 0% -> 0% of each run, Pallas kernels for 13% -> 14%
where the time goes in v3:
time: 184 us
  blocking collectives  58.4 us (32%)
  starting transfers between devices  51.7 us (28%)
  Pallas kernels  28.9 us (16%)
  waiting for transfers between devices  26.4 us (14%)
  between operations  14.2 us (8%)
  local copies, waits for them, and re-layouts  4.23 us (2%)
    all_to_all x3, blocking collectives, exchange(): lax.all_to_all(value, BOTH, 0, 0, axis_index_groups=group, tiled=True)  58.4 us
    ppermute x3, waiting for transfers between devices, per_device(): near[dyh, dyl] = lax.ppermute(patch_protos, BOTH, swap(dyh=dyh, dyl=dyl))  11.7 us
    pallas_call x1, Pallas kernels, final(): pl.pallas_call(final_body, out_shape=shape((256, 16384), BF16), in_specs=...  10.3 us
    ppermute x9, starting transfers between devices, per_device(): lax.ppermute(message, BOTH, swap(dyh=dyh, dyl=dyl))  9.76 us
    all_to_all x1, starting transfers between devices, exchange(): lax.all_to_all(value, BOTH, 0, 0, axis_index_groups=group, tiled=True)  8.19 us
    pallas_call x1, Pallas kernels, per_device(): call(kernel_body, (pltpu.VMEM((1024, 4096), F32), shape((128, 512)), shap...  8.18 us
    ppermute x4, starting transfers between devices, per_device(): pieces += [lax.ppermute(piece, BOTH, CORE) for piece in pieces]  7.79 us
    ppermute x3, starting transfers between devices, per_device(): lax.ppermute(message, BOTH, CORE)  7.69 us
  transfers between devices with their start and end apart: 27, of which 17 were waited for; matrix products, arithmetic and copies ran while one was open for 0% of the time, Pallas kernels for 14%

profile of v3, /device:TPU:1, one launch (start us, length us, event | category | flops | bytes accessed | tf_op | source)
XLA Modules:
  0.0 183.9 jit_solution(12390032640679684743)
XLA Ops:
  7.2 3.3 %collective-permute-start = (bf16[4,384]{1,0:T(4,128)(2,1)}, bf16[4,384]{1,0:T(4,128)(2,1)S(1)}, u32[]{:S(2)}, u32[]{:S(2)}) collective-permute-start(bf16[4,384]{1,0:T(4,128)(2,1)} %cls_ref.2), channel_id=1, source_target_pairs={{0,8},{1,9},{2,10},{3,11},{4,12},{5,13},{6,14},{7,15},{8,0},{9,1},... | collective-permute-start | bytes 9224 | tf_op jit(solution)/shard_map/ppermute | solution.py:314
  10.5 1.2 collective-permute-start.1
  11.7 2.0 %collective-permute-start.2 = (bf16[4,384]{1,0:T(4,128)(2,1)}, bf16[4,384]{1,0:T(4,128)(2,1)S(1)}, u32[]{:S(2)}, u32[]{:S(2)}) collective-permute-start(bf16[4,384]{1,0:T(4,128)(2,1)} %cls_ref.2), channel_id=1, source_target_pairs={{0,136},{1,137},{2,138},{3,139},{4,140},{5,141},{6,142},{7,143},{8... | collective-permute-start | bytes 9224 | tf_op jit(solution)/shard_map/ppermute | solution.py:314
  17.1 1.6 send.1
  18.7 8.2 %all-to-all-start = ((bf16[8,144,384]{2,1,0:T(8,128)(2,1)}), bf16[8,144,384]{2,1,0:T(8,128)(2,1)S(1)}, u32[]{:S(2)}, u32[]{:S(2)}) async-start(bf16[8,144,384]{2,1,0:T(8,128)(2,1)} %send.1), calls=%async_computation | async-start | bytes 1769472 | tf_op jit(solution)/shard_map/all_to_all | solution.py:55
  27.4 1.6 collective-permute-start.4
  28.9 1.9 %collective-permute-start.5 = (bf16[384,512]{1,0:T(8,128)(2,1)}, bf16[384,512]{1,0:T(8,128)(2,1)S(1)}, u32[]{:S(2)}, u32[]{:S(2)}) collective-permute-start(bf16[384,512]{1,0:T(8,128)(2,1)} %refs_0_.1), channel_id=1, source_target_pairs={{0,132},{1,133},{2,134},{3,135},{4,128},{5,129},{6,130},{7,131},{8... | collective-permute-start | bytes 1179656 | tf_op jit(solution)/shard_map/ppermute | solution.py:318
  30.9 1.5 collective-permute-start.6
  32.3 4.9 %collective-permute-done.3.refs_1_ = bf16[384,512]{1,0:T(8,128)(2,1)S(1)} collective-permute-done((bf16[384,512]{1,0:T(8,128)(2,1)}, bf16[384,512]{1,0:T(8,128)(2,1)S(1)}, u32[]{:S(2)}, u32[]{:S(2)}) %collective-permute-start.3) | collective-permute-done | bytes 393248 | tf_op jit(solution)/shard_map/ppermute | solution.py:318
  37.2 2.6 %collective-permute-start.7 = (bf16[384,512]{1,0:T(8,128)(2,1)S(1)}, bf16[384,512]{1,0:T(8,128)(2,1)S(1)}, u32[]{:S(2)}, u32[]{:S(2)}) collective-permute-start(bf16[384,512]{1,0:T(8,128)(2,1)S(1)} %collective-permute-done.3.refs_1_), channel_id=1, source_target_pairs={{0,8},{1,9},{2,10},{3,11},{4,12},{5,13},{6,14},{7,15},{8,0},{9,1},... | collective-permute-start | bytes 1179656 | tf_op jit(solution)/shard_map/ppermute | solution.py:320
  39.8 6.3 %collective-permute-done.4.refs_2_ = bf16[384,512]{1,0:T(8,128)(2,1)S(1)} collective-permute-done((bf16[384,512]{1,0:T(8,128)(2,1)}, bf16[384,512]{1,0:T(8,128)(2,1)S(1)}, u32[]{:S(2)}, u32[]{:S(2)}) %collective-permute-start.4) | collective-permute-done | bytes 393248 | tf_op jit(solution)/shard_map/ppermute | solution.py:318
  46.2 1.6 collective-permute-start.8
  48.2 2.1 %collective-permute-start.9 = (bf16[384,512]{1,0:T(8,128)(2,1)S(1)}, bf16[384,512]{1,0:T(8,128)(2,1)}, u32[]{:S(2)}, u32[]{:S(2)}) collective-permute-start(bf16[384,512]{1,0:T(8,128)(2,1)S(1)} %collective-permute-done.5.refs_3_), channel_id=1, source_target_pairs={{0,8},{1,9},{2,10},{3,11},{4,12},{5,13},{6,14},{7,15},{8,0},{9,1},... | collective-permute-start | bytes 1179656 | tf_op jit(solution)/shard_map/ppermute | solution.py:320
  53.5 8.2 %patch_kernel.1 = (f32[1024,4096]{1,0:T(8,128)S(1)}, f32[128,512]{1,0:T(8,128)}, f32[8,640]{1,0:T(8,128)}) custom-call(bf16[8,144,384]{2,1,0:T(8,128)(2,1)} %copy-done.5, bf16[384,512]{1,0:T(8,128)(2,1)} %cls_ref.3, bf16[384,512]{1,0:T(8,128)(2,1)} %refs_0_.1, bf16[384,512]{1,0:T(8,128)(2,1)} %copy-done.7, bf16[384,512]{1,0:T(8,128)(2,1)} %copy-done.6, ...), custom_call_target="tpu_custom_call" | custom-call | tf_op jit(solution)/shard_map/patch_kernel/pallas_call | solution.py:329
  69.3 1.2 row_sums.3
  70.5 23.7 %all_to_all.25.got_ref = f32[32,16,128]{2,1,0:T(8,128)S(1)} all-to-all(f32[32,16,128]{2,1,0:T(8,128)S(1)} %row_sums.3), channel_id=1, replica_groups={{0,1,2,3,16,17,18,19,32,33,34,35,48,49,50,51,64,65,66,67,80,81,82,83,96..., dimensions={0} | all-to-all | bytes 524288 | tf_op jit(solution)/shard_map/all_to_all | solution.py:55
  94.1 1.4 column_sums.2.mine_ref
  95.5 3.2 %collective-permute-start.14 = (f32[8,640]{1,0:T(8,128)S(1)}, f32[8,640]{1,0:T(8,128)S(1)}, u32[]{:S(2)}, u32[]{:S(2)}) collective-permute-start(f32[8,640]{1,0:T(8,128)S(1)} %column_sums.2.mine_ref), channel_id=1, source_target_pairs={{0,8},{1,9},{2,10},{3,11},{4,12},{5,13},{6,14},{7,15},{8,0},{9,1},... | collective-permute-start | bytes 61448 | tf_op jit(solution)/shard_map/ppermute | solution.py:356
  100.5 1.1 collective-permute-start.16
  101.6 1.3 collective-permute-start.17
  104.6 1.2 row_sums.4
  105.8 13.7 %all_to_all.26.got_ref = f32[32,16,128]{2,1,0:T(8,128)S(1)} all-to-all(f32[32,16,128]{2,1,0:T(8,128)S(1)} %row_sums.4), channel_id=1, replica_groups={{0,1,2,3,16,17,18,19,32,33,34,35,48,49,50,51,64,65,66,67,80,81,82,83,96..., dimensions={0} | all-to-all | bytes 524288 | tf_op jit(solution)/shard_map/all_to_all | solution.py:55
  119.5 1.4 column_sums.3
  120.9 3.9 %collective-permute-start.18 = (f32[8,640]{1,0:T(8,128)S(1)}, f32[8,640]{1,0:T(8,128)S(1)}, u32[]{:S(2)}, u32[]{:S(2)}) collective-permute-start(f32[8,640]{1,0:T(8,128)S(1)} %get-tuple-element.18.mine_ref), channel_id=1, source_target_pairs={{0,8},{1,9},{2,10},{3,11},{4,12},{5,13},{6,14},{7,15},{8,0},{9,1},... | collective-permute-start | bytes 61448 | tf_op jit(solution)/shard_map/ppermute | solution.py:356
  125.6 1.9 %collective-permute-start.19 = (f32[8,640]{1,0:T(8,128)S(1)}, f32[8,640]{1,0:T(8,128)S(1)}, u32[]{:S(2)}, u32[]{:S(2)}) collective-permute-start(f32[8,640]{1,0:T(8,128)S(1)} %add_core.5.mine_ref), channel_id=1, source_target_pairs={{0,132},{1,133},{2,134},{3,135},{4,128},{5,129},{6,130},{7,131},{8... | collective-permute-start | bytes 61448 | tf_op jit(solution)/shard_map/ppermute | solution.py:357
  129.9 1.8 %collective-permute-done.20.b_ref = f32[8,640]{1,0:T(8,128)S(1)} collective-permute-done((f32[8,640]{1,0:T(8,128)S(1)}, f32[8,640]{1,0:T(8,128)S(1)}, u32[]{:S(2)}, u32[]{:S(2)}) %collective-permute-start.20) | collective-permute-done | bytes 20512 | tf_op jit(solution)/shard_map/ppermute | solution.py:357
  131.7 1.2 row_sums.5
  133.0 21.1 %all_to_all.27.got_ref = f32[32,24,128]{2,1,0:T(8,128)S(1)} all-to-all(f32[32,24,128]{2,1,0:T(8,128)S(1)} %row_sums.5), channel_id=1, replica_groups={{0,1,2,3,16,17,18,19,32,33,34,35,48,49,50,51,64,65,66,67,80,81,82,83,96..., dimensions={0} | all-to-all | bytes 786432 | tf_op jit(solution)/shard_map/all_to_all | solution.py:55
  154.7 7.6 %all-to-all-start.4 = ((f32[32,4,512]{2,1,0:T(4,128)}), f32[32,4,512]{2,1,0:T(4,128)S(1)}, u32[]{:S(2)}, u32[]{:S(2)}) async-start(f32[32,4,512]{2,1,0:T(4,128)} %get-tuple-element.20), calls=%async_computation.4 | async-start | bytes 524288 | tf_op jit(solution)/shard_map/all_to_all | solution.py:369
  162.4 2.7 %collective-permute-done.22.other_ref = f32[8,128]{1,0:T(8,128)S(1)} collective-permute-done((f32[8,128]{1,0:T(8,128)S(1)}, f32[8,128]{1,0:T(8,128)S(1)}, u32[]{:S(2)}, u32[]{:S(2)}) %collective-permute-start.22) | collective-permute-done | bytes 4128 | tf_op jit(solution)/shard_map/ppermute | solution.py:370
  165.1 10.3 %final_scale.1 = bf16[256,16384]{1,0:T(8,128)(2,1)} custom-call(s32[5]{0:T(128)S(1)} %stack.23.where_ref, bf16[16,384,512]{2,1,0:T(8,128)(2,1)} %bitcast.7, bf16[16,384,512]{2,1,0:T(8,128)(2,1)} %bitcast.8, bf16[256,384]{1,0:T(8,128)(2,1)S(1)} %units.1.unit_ref.units_ref, f32[32,1,512]{2,1,0:T(1,128)S(1)} %get-tuple-element.23.cols_ref, ...), custom_call_target="tpu_custom_call" | custom-call | tf_op jit(solution)/shard_map/final_scale/pallas_call | solution.py:291
  175.7 1.4 cls_final.1
  (66 shorter events, 22.5 us)
Async XLA Ops:
  7.2 8.9 %collective-permute-start = (bf16[4,384]{1,0:T(4,128)(2,1)}, bf16[4,384]{1,0:T(4,128)(2,1)S(1)}, u32[]{:S(2)}, u32[]{:S(2)}) collective-permute-start(bf16[4,384]{1,0:T(4,128)(2,1)} %cls_ref.2), channel_id=1, source_target_pairs={{0,8},{1,9},{2,10},{3,11},{4,12},{5,13},{6,14},{7,15},{8,0},{9,1},... | collective-permute-start | bytes 9224 | tf_op jit(solution)/shard_map/ppermute | solution.py:314
  10.5 5.5 %collective-permute-start.1 = (bf16[4,384]{1,0:T(4,128)(2,1)}, bf16[4,384]{1,0:T(4,128)(2,1)S(1)}, u32[]{:S(2)}, u32[]{:S(2)}) collective-permute-start(bf16[4,384]{1,0:T(4,128)(2,1)} %cls_ref.2), channel_id=1, source_target_pairs={{0,128},{1,129},{2,130},{3,131},{4,132},{5,133},{6,134},{7,135},{8... | collective-permute-start | bytes 9224 | tf_op jit(solution)/shard_map/ppermute | solution.py:314
  11.7 4.7 %collective-permute-start.2 = (bf16[4,384]{1,0:T(4,128)(2,1)}, bf16[4,384]{1,0:T(4,128)(2,1)S(1)}, u32[]{:S(2)}, u32[]{:S(2)}) collective-permute-start(bf16[4,384]{1,0:T(4,128)(2,1)} %cls_ref.2), channel_id=1, source_target_pairs={{0,136},{1,137},{2,138},{3,139},{4,140},{5,141},{6,142},{7,143},{8... | collective-permute-start | bytes 9224 | tf_op jit(solution)/shard_map/ppermute | solution.py:314
  18.7 33.9 %all-to-all-start = ((bf16[8,144,384]{2,1,0:T(8,128)(2,1)}), bf16[8,144,384]{2,1,0:T(8,128)(2,1)S(1)}, u32[]{:S(2)}, u32[]{:S(2)}) async-start(bf16[8,144,384]{2,1,0:T(8,128)(2,1)} %send.1), calls=%async_computation | async-start | bytes 1769472 | tf_op jit(solution)/shard_map/all_to_all | solution.py:55
  26.9 138.2 %all-gather.5.cloned.1.call-start = ((), (), s32[]{:S(2)}) async-start(), calls=%async_computation.5 | async-start | bytes 6684672 | tf_op jit(solution)/shard_map/all_gather | solution.py:327
  26.9 10.3 %collective-permute-start.3 = (bf16[384,512]{1,0:T(8,128)(2,1)}, bf16[384,512]{1,0:T(8,128)(2,1)S(1)}, u32[]{:S(2)}, u32[]{:S(2)}) collective-permute-start(bf16[384,512]{1,0:T(8,128)(2,1)} %refs_0_.1), channel_id=1, source_target_pairs={{0,4},{1,5},{2,6},{3,7},{4,0},{5,1},{6,2},{7,3},{8,12},{9,13},{10,... | collective-permute-start | bytes 1179656 | tf_op jit(solution)/shard_map/ppermute | solution.py:318
  27.4 18.8 %collective-permute-start.4 = (bf16[384,512]{1,0:T(8,128)(2,1)}, bf16[384,512]{1,0:T(8,128)(2,1)S(1)}, u32[]{:S(2)}, u32[]{:S(2)}) collective-permute-start(bf16[384,512]{1,0:T(8,128)(2,1)} %refs_0_.1), channel_id=1, source_target_pairs={{0,128},{1,129},{2,130},{3,131},{4,132},{5,133},{6,134},{7,135},{8... | collective-permute-start | bytes 1179656 | tf_op jit(solution)/shard_map/ppermute | solution.py:318
  28.9 19.3 %collective-permute-start.5 = (bf16[384,512]{1,0:T(8,128)(2,1)}, bf16[384,512]{1,0:T(8,128)(2,1)S(1)}, u32[]{:S(2)}, u32[]{:S(2)}) collective-permute-start(bf16[384,512]{1,0:T(8,128)(2,1)} %refs_0_.1), channel_id=1, source_target_pairs={{0,132},{1,133},{2,134},{3,135},{4,128},{5,129},{6,130},{7,131},{8... | collective-permute-start | bytes 1179656 | tf_op jit(solution)/shard_map/ppermute | solution.py:318
  30.9 19.5 %collective-permute-start.6 = (bf16[384,512]{1,0:T(8,128)(2,1)}, bf16[384,512]{1,0:T(8,128)(2,1)S(1)}, u32[]{:S(2)}, u32[]{:S(2)}) collective-permute-start(bf16[384,512]{1,0:T(8,128)(2,1)} %refs_0_.1), channel_id=1, source_target_pairs={{0,8},{1,9},{2,10},{3,11},{4,12},{5,13},{6,14},{7,15},{8,0},{9,1},... | collective-permute-start | bytes 1179656 | tf_op jit(solution)/shard_map/ppermute | solution.py:320
  37.2 16.1 %copy-start.7 = (bf16[384,512]{1,0:T(8,128)(2,1)}, bf16[384,512]{1,0:T(8,128)(2,1)S(1)}, u32[]{:S(2)}) copy-start(bf16[384,512]{1,0:T(8,128)(2,1)S(1)} %collective-permute-done.3.refs_1_) | copy-start | bytes 1179652
  37.2 13.1 %collective-permute-start.7 = (bf16[384,512]{1,0:T(8,128)(2,1)S(1)}, bf16[384,512]{1,0:T(8,128)(2,1)S(1)}, u32[]{:S(2)}, u32[]{:S(2)}) collective-permute-start(bf16[384,512]{1,0:T(8,128)(2,1)S(1)} %collective-permute-done.3.refs_1_), channel_id=1, source_target_pairs={{0,8},{1,9},{2,10},{3,11},{4,12},{5,13},{6,14},{7,15},{8,0},{9,1},... | collective-permute-start | bytes 1179656 | tf_op jit(solution)/shard_map/ppermute | solution.py:320
  46.2 6.4 %copy-start.6 = (bf16[384,512]{1,0:T(8,128)(2,1)}, bf16[384,512]{1,0:T(8,128)(2,1)S(1)}, u32[]{:S(2)}) copy-start(bf16[384,512]{1,0:T(8,128)(2,1)S(1)} %collective-permute-done.4.refs_2_) | copy-start | bytes 1179652
  46.2 4.2 %collective-permute-start.8 = (bf16[384,512]{1,0:T(8,128)(2,1)S(1)}, bf16[384,512]{1,0:T(8,128)(2,1)S(1)}, u32[]{:S(2)}, u32[]{:S(2)}) collective-permute-start(bf16[384,512]{1,0:T(8,128)(2,1)S(1)} %collective-permute-done.4.refs_2_), channel_id=1, source_target_pairs={{0,8},{1,9},{2,10},{3,11},{4,12},{5,13},{6,14},{7,15},{8,0},{9,1},... | collective-permute-start | bytes 1179656 | tf_op jit(solution)/shard_map/ppermute | solution.py:320
  48.2 5.1 %copy-start.8 = (bf16[384,512]{1,0:T(8,128)(2,1)}, bf16[384,512]{1,0:T(8,128)(2,1)S(1)}, u32[]{:S(2)}) copy-start(bf16[384,512]{1,0:T(8,128)(2,1)S(1)} %collective-permute-done.5.refs_3_) | copy-start | bytes 1179652
  48.2 3.6 %collective-permute-start.9 = (bf16[384,512]{1,0:T(8,128)(2,1)S(1)}, bf16[384,512]{1,0:T(8,128)(2,1)}, u32[]{:S(2)}, u32[]{:S(2)}) collective-permute-start(bf16[384,512]{1,0:T(8,128)(2,1)S(1)} %collective-permute-done.5.refs_3_), channel_id=1, source_target_pairs={{0,8},{1,9},{2,10},{3,11},{4,12},{5,13},{6,14},{7,15},{8,0},{9,1},... | collective-permute-start | bytes 1179656 | tf_op jit(solution)/shard_map/ppermute | solution.py:320
  50.3 3.0 %copy-start.10 = (bf16[384,512]{1,0:T(8,128)(2,1)}, bf16[384,512]{1,0:T(8,128)(2,1)S(1)}, u32[]{:S(2)}) copy-start(bf16[384,512]{1,0:T(8,128)(2,1)S(1)} %collective-permute-done.7.refs_5_) | copy-start | bytes 1179652
  52.6 112.5 %all-gather.7.cloned.1.call-start = ((), (), s32[]{:S(2)}) async-start(), calls=%async_computation.6 | async-start | bytes 6684672 | tf_op jit(solution)/shard_map/all_gather | solution.py:327
  61.6 1.6 collective-permute-start.10
  64.0 4.2 %collective-permute-start.11 = (f32[8,640]{1,0:T(8,128)S(1)}, f32[8,640]{1,0:T(8,128)S(1)}, u32[]{:S(2)}, u32[]{:S(2)}) collective-permute-start(f32[8,640]{1,0:T(8,128)S(1)} %add_core.3.mine_ref), channel_id=1, source_target_pairs={{0,132},{1,133},{2,134},{3,135},{4,128},{5,129},{6,130},{7,131},{8... | collective-permute-start | bytes 61448 | tf_op jit(solution)/shard_map/ppermute | solution.py:357
  65.1 4.2 %collective-permute-start.12 = (f32[8,640]{1,0:T(8,128)S(1)}, f32[8,640]{1,0:T(8,128)S(1)}, u32[]{:S(2)}, u32[]{:S(2)}) collective-permute-start(f32[8,640]{1,0:T(8,128)S(1)} %add_core.3.mine_ref), channel_id=1, source_target_pairs={{0,128},{1,129},{2,130},{3,131},{4,132},{5,133},{6,134},{7,135},{8... | collective-permute-start | bytes 61448 | tf_op jit(solution)/shard_map/ppermute | solution.py:357
  66.2 3.1 %collective-permute-start.13 = (f32[8,640]{1,0:T(8,128)S(1)}, f32[8,640]{1,0:T(8,128)S(1)}, u32[]{:S(2)}, u32[]{:S(2)}) collective-permute-start(f32[8,640]{1,0:T(8,128)S(1)} %add_core.3.mine_ref), channel_id=1, source_target_pairs={{0,4},{1,5},{2,6},{3,7},{4,0},{5,1},{6,2},{7,3},{8,12},{9,13},{10,... | collective-permute-start | bytes 61448 | tf_op jit(solution)/shard_map/ppermute | solution.py:357
  69.3 24.9 %copy-start = (f32[128,512]{1,0:T(8,128)S(1)}, f32[128,512]{1,0:T(8,128)}, u32[]{:S(2)}) copy-start(f32[128,512]{1,0:T(8,128)} %get-tuple-element.16.cls_kern_ref) | copy-start | bytes 786436
  95.5 4.1 %collective-permute-start.14 = (f32[8,640]{1,0:T(8,128)S(1)}, f32[8,640]{1,0:T(8,128)S(1)}, u32[]{:S(2)}, u32[]{:S(2)}) collective-permute-start(f32[8,640]{1,0:T(8,128)S(1)} %column_sums.2.mine_ref), channel_id=1, source_target_pairs={{0,8},{1,9},{2,10},{3,11},{4,12},{5,13},{6,14},{7,15},{8,0},{9,1},... | collective-permute-start | bytes 61448 | tf_op jit(solution)/shard_map/ppermute | solution.py:356
  99.6 3.8 %collective-permute-start.15 = (f32[8,640]{1,0:T(8,128)S(1)}, f32[8,640]{1,0:T(8,128)S(1)}, u32[]{:S(2)}, u32[]{:S(2)}) collective-permute-start(f32[8,640]{1,0:T(8,128)S(1)} %add_core.4.mine_ref), channel_id=1, source_target_pairs={{0,132},{1,133},{2,134},{3,135},{4,128},{5,129},{6,130},{7,131},{8... | collective-permute-start | bytes 61448 | tf_op jit(solution)/shard_map/ppermute | solution.py:357
  100.5 4.1 %collective-permute-start.16 = (f32[8,640]{1,0:T(8,128)S(1)}, f32[8,640]{1,0:T(8,128)S(1)}, u32[]{:S(2)}, u32[]{:S(2)}) collective-permute-start(f32[8,640]{1,0:T(8,128)S(1)} %add_core.4.mine_ref), channel_id=1, source_target_pairs={{0,128},{1,129},{2,130},{3,131},{4,132},{5,133},{6,134},{7,135},{8... | collective-permute-start | bytes 61448 | tf_op jit(solution)/shard_map/ppermute | solution.py:357
  101.6 3.0 %collective-permute-start.17 = (f32[8,640]{1,0:T(8,128)S(1)}, f32[8,640]{1,0:T(8,128)S(1)}, u32[]{:S(2)}, u32[]{:S(2)}) collective-permute-start(f32[8,640]{1,0:T(8,128)S(1)} %add_core.4.mine_ref), channel_id=1, source_target_pairs={{0,4},{1,5},{2,6},{3,7},{4,0},{5,1},{6,2},{7,3},{8,12},{9,13},{10,... | collective-permute-start | bytes 61448 | tf_op jit(solution)/shard_map/ppermute | solution.py:357
  120.9 4.7 %collective-permute-start.18 = (f32[8,640]{1,0:T(8,128)S(1)}, f32[8,640]{1,0:T(8,128)S(1)}, u32[]{:S(2)}, u32[]{:S(2)}) collective-permute-start(f32[8,640]{1,0:T(8,128)S(1)} %get-tuple-element.18.mine_ref), channel_id=1, source_target_pairs={{0,8},{1,9},{2,10},{3,11},{4,12},{5,13},{6,14},{7,15},{8,0},{9,1},... | collective-permute-start | bytes 61448 | tf_op jit(solution)/shard_map/ppermute | solution.py:356
  125.6 4.2 %collective-permute-start.19 = (f32[8,640]{1,0:T(8,128)S(1)}, f32[8,640]{1,0:T(8,128)S(1)}, u32[]{:S(2)}, u32[]{:S(2)}) collective-permute-start(f32[8,640]{1,0:T(8,128)S(1)} %add_core.5.mine_ref), channel_id=1, source_target_pairs={{0,132},{1,133},{2,134},{3,135},{4,128},{5,129},{6,130},{7,131},{8... | collective-permute-start | bytes 61448 | tf_op jit(solution)/shard_map/ppermute | solution.py:357
  127.5 4.2 %collective-permute-start.20 = (f32[8,640]{1,0:T(8,128)S(1)}, f32[8,640]{1,0:T(8,128)S(1)}, u32[]{:S(2)}, u32[]{:S(2)}) collective-permute-start(f32[8,640]{1,0:T(8,128)S(1)} %add_core.5.mine_ref), channel_id=1, source_target_pairs={{0,128},{1,129},{2,130},{3,131},{4,132},{5,133},{6,134},{7,135},{8... | collective-permute-start | bytes 61448 | tf_op jit(solution)/shard_map/ppermute | solution.py:357
  128.7 3.1 %collective-permute-start.21 = (f32[8,640]{1,0:T(8,128)S(1)}, f32[8,640]{1,0:T(8,128)S(1)}, u32[]{:S(2)}, u32[]{:S(2)}) collective-permute-start(f32[8,640]{1,0:T(8,128)S(1)} %add_core.5.mine_ref), channel_id=1, source_target_pairs={{0,4},{1,5},{2,6},{3,7},{4,0},{5,1},{6,2},{7,3},{8,12},{9,13},{10,... | collective-permute-start | bytes 61448 | tf_op jit(solution)/shard_map/ppermute | solution.py:357
  154.7 21.0 %all-to-all-start.4 = ((f32[32,4,512]{2,1,0:T(4,128)}), f32[32,4,512]{2,1,0:T(4,128)S(1)}, u32[]{:S(2)}, u32[]{:S(2)}) async-start(f32[32,4,512]{2,1,0:T(4,128)} %get-tuple-element.20), calls=%async_computation.4 | async-start | bytes 524288 | tf_op jit(solution)/shard_map/all_to_all | solution.py:369
  162.3 2.8 %collective-permute-start.22 = (f32[8,128]{1,0:T(8,128)S(1)}, f32[8,128]{1,0:T(8,128)S(1)}, u32[]{:S(2)}, u32[]{:S(2)}) collective-permute-start(f32[8,128]{1,0:T(8,128)S(1)} %get-tuple-element.19.mine_ref.sums_ref), channel_id=1, source_target_pairs={{0,4},{1,5},{2,6},{3,7},{4,0},{5,1},{6,2},{7,3},{8,12},{9,13},{10,... | collective-permute-start | bytes 12296 | tf_op jit(solution)/shard_map/ppermute | solution.py:370
  (7 other events, 8.0 us)
Sparse Core Ops, SparseCore 0:
  52.7 51.3 all-gather.4
  105.9 53.4 all-gather.6

commit v4 on v3

--- a/solution.py
+++ b/solution.py
@@ -115,9 +115,8 @@
     first = [jnp.where(yh == 0, n, f) for n, f in zip(near, far)]
     second = [jnp.where(yh == 0, f, n) for n, f in zip(near, far)]
     tail = jnp.concatenate(first + second, axis=0).astype(BF16)
-    for z in range(NZ):
-        send_ref[z, :128, :] = half
-        send_ref[z, 128:, :] = tail
+    send_ref[:128, :] = half
+    send_ref[128:, :] = tail
 
 
 def cls_step(cls_kern, row_scale):
@@ -132,18 +131,12 @@
     return cols, across(total)
 
 
-def kernel_body(rows_ref, cls_ref, *refs):
-    pieces, (kern_ref, cls_kern_ref, message_ref, units_ref, held_ref, sems) = refs[:8], refs[8:]
-    copies = [pltpu.make_async_copy(rows_ref, units_ref, sems.at[9])]
-    copies += [pltpu.make_async_copy(ref, held_ref.at[k], sems.at[k]) for k, ref in enumerate((*pieces, cls_ref))]
-    for copy in copies:
-        copy.start()
-    copies[0].wait()
+def kernel_body(units_ref, cls_ref, *refs):
+    pieces, (kern_ref, cls_kern_ref, message_ref) = refs[:8], refs[8:]
     for k in range(8):
-        copies[k + 1].wait()
         for half in range(2):
             lanes = slice(half * 256, half * 256 + 256)
-            protos = held_ref[k, :, lanes]
+            protos = pieces[k][:, lanes]
             scale = inv_norms(protos)
             total = jnp.zeros((8, 256), F32)
             for part in range(2):
@@ -154,9 +147,8 @@
                 kern_ref[part * 512 : part * 512 + 512, at : at + 256] = value
                 total = total + jnp.sum(value.reshape(64, 8, 256), axis=0)
             message_ref[k : k + 1, lanes] = jnp.sum(total, axis=0, keepdims=True)
-    copies[9].wait()
     units = jnp.concatenate([units_ref[z, 128:, :] for z in range(NZ)], axis=0)
-    protos = held_ref[8]
+    protos = cls_ref[...]
     dots = jnp.dot(units, protos, preferred_element_type=F32)
     cls_kern_ref[...] = jnp.exp2(dots * inv_norms(protos) - SLOPE)
     _, sums = cls_step(cls_kern_ref[...], jnp.ones((1, 128), F32))
@@ -316,27 +308,23 @@
     near = {(0, 0): patch_protos}
     for dyh, dyl in Y_STEPS:
         near[dyh, dyl] = lax.ppermute(patch_protos, BOTH, swap(dyh=dyh, dyl=dyl))
+
+    units = call(units_body, shape((256, 384), BF16), [VM] * 2, "units")(patch_features, mask_index)
+    send = call(send_body, shape((144, 384), BF16), [SM] + [VM] * 5, "send")(where, units, cls_features, *cls_near)
+    rows = lax.all_gather(send, BOTH, axis_index_groups=GROUPS_Z)
+
     pieces = [near[k // 2, k % 2] for k in range(4)]
+    pieces[1:] = lax.optimization_barrier((*pieces[1:], rows))[:3]
     pieces += [lax.ppermute(piece, BOTH, CORE) for piece in pieces]
 
-    units = call(units_body, shape((256, 384), BF16), [VM] * 2, "units")(patch_features, mask_index)
-    send = call(send_body, shape((NZ, 144, 384), BF16), [SM] + [VM] * 5, "send")(where, units, cls_features, *cls_near)
-    rows = exchange(send, GROUPS_Z)
-
-    held = lax.optimization_barrier((patch_protos, near[1, 0], rows, *pieces[1:2], *pieces[3:]))[:2]
+    held = lax.optimization_barrier((patch_protos, pieces[2], rows, *pieces[1:2], *pieces[3:]))[:2]
     gathered = [lax.all_gather(piece, BOTH, axis_index_groups=GROUPS_ZC) for piece in held]
 
     kern, cls_kern, message = call(
         kernel_body,
         (pltpu.VMEM((1024, 4096), F32), shape((128, 512)), shape((8, 640))),
-        [HBM] * 10,
+        [VM] * 10,
         "patch_kernel",
-        [
-            pltpu.VMEM((NZ, 144, 384), BF16),
-            pltpu.VMEM((9, 384, 512), BF16),
-            pltpu.SemaphoreType.DMA((10,)),
-        ],
-        limit=43,
     )(rows, cls_protos, *pieces)
 
     for step in range(ITERS):

time: 184 us -> 197 us (1.071)
  blocking collectives: 58.4 us -> 81.4 us
  starting transfers between devices: 51.7 us -> 43.7 us
  Pallas kernels: 28.9 us -> 25.7 us
  local copies, waits for them, and re-layouts: 4.23 us -> 7.34 us
  waiting for transfers between devices: 26.4 us -> 23.8 us
    all_gather x0 -> x1, blocking collectives: none -> 24.8 us  [per_device(): rows = lax.all_gather(send, BOTH, axis_index_groups=GROUPS_Z)]
    ppermute x3, waiting for transfers between devices: 11.7 us -> 0.01 us  [per_device(): near[dyh, dyl] = lax.ppermute(patch_protos, BOTH, swap(dyh=dyh, dyl=dyl))]
    ppermute x3, waiting for transfers between devices: 0.42 us -> 9.92 us  [per_device(): lax.ppermute(cls_features, BOTH, swap(dcore=c, dyh=h))]
    all_to_all x1 -> x0, starting transfers between devices: 8.19 us -> none  [exchange(): lax.all_to_all(value, BOTH, 0, 0, axis_index_groups=group, tiled=True)]
    pallas_call x1, Pallas kernels: 8.18 us -> 4.9 us  [per_device(): call(kernel_body, (pltpu.VMEM((1024, 4096), F32), shape((128, 512)), shap...]
    unnamed x24 -> x18, local copies, waits for them, and re-layouts: 4.15 us -> 7.26 us
  transfers between devices with their start and end apart: 27 -> 26, of which waited for: 17 -> 15; matrix products, arithmetic and copies ran while one was open for 0% -> 0% of each run, Pallas kernels for 14% -> 12%
where the time goes in v4:
time: 197 us; the launch traced here: 196 us
  blocking collectives  81.4 us (41%)
  starting transfers between devices  43.7 us (22%)
  Pallas kernels  25.7 us (13%)
  waiting for transfers between devices  23.8 us (12%)
  between operations  14.2 us (7%)
  local copies, waits for them, and re-layouts  7.34 us (4%)
    all_to_all x3, blocking collectives, exchange(): lax.all_to_all(value, BOTH, 0, 0, axis_index_groups=group, tiled=True)  56.6 us
    all_gather x1, blocking collectives, per_device(): rows = lax.all_gather(send, BOTH, axis_index_groups=GROUPS_Z)  24.8 us
    pallas_call x1, Pallas kernels, final(): pl.pallas_call(final_body, out_shape=shape((256, 16384), BF16), in_specs=...  10.3 us
    ppermute x3, waiting for transfers between devices, per_device(): lax.ppermute(cls_features, BOTH, swap(dcore=c, dyh=h))  9.92 us
    ppermute x9, starting transfers between devices, per_device(): lax.ppermute(message, BOTH, swap(dyh=dyh, dyl=dyl))  9.76 us
    all_to_all x1, starting transfers between devices, per_device(): cls_scaled = lax.all_to_all(cls_scaled, 'dp', 0, 0, tiled=True)  7.48 us
    ppermute x3, starting transfers between devices, per_device(): lax.ppermute(message, BOTH, CORE)  7.43 us
    ppermute x3, starting transfers between devices, per_device(): lax.ppermute(cls_features, BOTH, swap(dcore=c, dyh=h))  7.38 us
  transfers between devices with their start and end apart: 26, of which 15 were waited for; matrix products, arithmetic and copies ran while one was open for 0% of the time, Pallas kernels for 12%

profile of v4, /device:TPU:1, one launch (start us, length us, event | category | flops | bytes accessed | tf_op | source)
XLA Modules:
  0.0 196.1 jit_solution(5309750429383927433)
XLA Ops:
  7.2 3.3 %collective-permute-start = (bf16[4,384]{1,0:T(4,128)(2,1)}, bf16[4,384]{1,0:T(4,128)(2,1)S(1)}, u32[]{:S(2)}, u32[]{:S(2)}) collective-permute-start(bf16[4,384]{1,0:T(4,128)(2,1)} %cls_ref.2), channel_id=1, source_target_pairs={{0,8},{1,9},{2,10},{3,11},{4,12},{5,13},{6,14},{7,15},{8,0},{9,1},... | collective-permute-start | bytes 9224 | tf_op jit(solution)/shard_map/ppermute | solution.py:306
  10.5 2.2 %collective-permute-start.4 = (bf16[384,512]{1,0:T(8,128)(2,1)}, bf16[384,512]{1,0:T(8,128)(2,1)S(1)}, u32[]{:S(2)}, u32[]{:S(2)}) collective-permute-start(bf16[384,512]{1,0:T(8,128)(2,1)} %refs_0_.1), channel_id=1, source_target_pairs={{0,128},{1,129},{2,130},{3,131},{4,132},{5,133},{6,134},{7,135},{8... | collective-permute-start | bytes 1179656 | tf_op jit(solution)/shard_map/ppermute | solution.py:310
  12.7 1.7 collective-permute-start.5
  14.4 4.1 %collective-permute-start.2 = (bf16[4,384]{1,0:T(4,128)(2,1)}, bf16[4,384]{1,0:T(4,128)(2,1)S(1)}, u32[]{:S(2)}, u32[]{:S(2)}) collective-permute-start(bf16[4,384]{1,0:T(4,128)(2,1)} %cls_ref.2), channel_id=1, source_target_pairs={{0,136},{1,137},{2,138},{3,139},{4,140},{5,141},{6,142},{7,143},{8... | collective-permute-start | bytes 9224 | tf_op jit(solution)/shard_map/ppermute | solution.py:306
  18.5 1.1 copy-done.3
  20.8 9.9 %collective-permute-done.1.b_ref = bf16[4,384]{1,0:T(4,128)(2,1)S(1)} collective-permute-done((bf16[4,384]{1,0:T(4,128)(2,1)}, bf16[4,384]{1,0:T(4,128)(2,1)S(1)}, u32[]{:S(2)}, u32[]{:S(2)}) %collective-permute-start.1) | collective-permute-done | bytes 3104 | tf_op jit(solution)/shard_map/ppermute | solution.py:306
  33.0 24.8 %all-gather = bf16[1152,384]{1,0:T(8,128)(2,1)S(1)} all-gather(bf16[144,384]{1,0:T(8,128)(2,1)S(1)} %send.1), channel_id=2, replica_groups={{0,16,32,48,64,80,96,112},{4,20,36,52,68,84,100,116},{1,17,33,49,65,81,..., dimensions={0}, use_global_device_ids=true | all-gather | bytes 995328 | tf_op jit(solution)/shard_map/all_gather | solution.py:314
  57.8 5.3 %collective-permute-start.7 = (bf16[384,512]{1,0:T(8,128)(2,1)S(1)}, bf16[384,512]{1,0:T(8,128)(2,1)S(1)}, u32[]{:S(2)}, u32[]{:S(2)}) collective-permute-start(bf16[384,512]{1,0:T(8,128)(2,1)S(1)} %collective-permute-done.3.refs_1_), channel_id=1, source_target_pairs={{0,8},{1,9},{2,10},{3,11},{4,12},{5,13},{6,14},{7,15},{8,0},{9,1},... | collective-permute-start | bytes 1179656 | tf_op jit(solution)/shard_map/ppermute | solution.py:318
  68.2 1.0 copy-done.2
  69.2 1.0 copy-done.4
  71.2 4.9 %patch_kernel.1 = (f32[1024,4096]{1,0:T(8,128)S(1)}, f32[128,512]{1,0:T(8,128)S(1)}, f32[8,640]{1,0:T(8,128)S(1)}) custom-call(bf16[8,144,384]{2,1,0:T(8,128)(2,1)S(1)} %bitcast.8, bf16[384,512]{1,0:T(8,128)(2,1)S(1)} %copy-done.4, bf16[384,512]{1,0:T(8,128)(2,1)S(1)} %copy-done, bf16[384,512]{1,0:T(8,128)(2,1)S(1)} %collective-permute-done.3.refs_1_, ...), custom_call_target="tpu_custom_call" | custom-call | tf_op jit(solution)/shard_map/patch_kernel/pallas_call | solution.py:323
  77.4 1.6 collective-permute-start.12
  79.0 1.6 collective-permute-start.13
  82.4 1.3 row_sums.3
  83.8 21.7 %all_to_all.20.got_ref = f32[32,16,128]{2,1,0:T(8,128)S(1)} all-to-all(f32[32,16,128]{2,1,0:T(8,128)S(1)} %row_sums.3), channel_id=1, replica_groups={{0,1,2,3,16,17,18,19,32,33,34,35,48,49,50,51,64,65,66,67,80,81,82,83,96..., dimensions={0} | all-to-all | bytes 524288 | tf_op jit(solution)/shard_map/all_to_all | solution.py:55
  105.5 1.6 column_sums.2.mine_ref
  107.1 3.1 %collective-permute-start.14 = (f32[8,640]{1,0:T(8,128)S(1)}, f32[8,640]{1,0:T(8,128)S(1)}, u32[]{:S(2)}, u32[]{:S(2)}) collective-permute-start(f32[8,640]{1,0:T(8,128)S(1)} %column_sums.2.mine_ref), channel_id=1, source_target_pairs={{0,8},{1,9},{2,10},{3,11},{4,12},{5,13},{6,14},{7,15},{8,0},{9,1},... | collective-permute-start | bytes 61448 | tf_op jit(solution)/shard_map/ppermute | solution.py:344
  111.1 2.0 %collective-permute-start.15 = (f32[8,640]{1,0:T(8,128)S(1)}, f32[8,640]{1,0:T(8,128)S(1)}, u32[]{:S(2)}, u32[]{:S(2)}) collective-permute-start(f32[8,640]{1,0:T(8,128)S(1)} %add_core.4.mine_ref), channel_id=1, source_target_pairs={{0,132},{1,133},{2,134},{3,135},{4,128},{5,129},{6,130},{7,131},{8... | collective-permute-start | bytes 61448 | tf_op jit(solution)/shard_map/ppermute | solution.py:345
  113.1 1.2 collective-permute-start.16
  114.9 2.3 %collective-permute-done.16.b_ref = f32[8,640]{1,0:T(8,128)S(1)} collective-permute-done((f32[8,640]{1,0:T(8,128)S(1)}, f32[8,640]{1,0:T(8,128)S(1)}, u32[]{:S(2)}, u32[]{:S(2)}) %collective-permute-start.16) | collective-permute-done | bytes 20512 | tf_op jit(solution)/shard_map/ppermute | solution.py:345
  117.2 1.3 row_sums.4
  118.5 13.6 %all_to_all.21.got_ref = f32[32,16,128]{2,1,0:T(8,128)S(1)} all-to-all(f32[32,16,128]{2,1,0:T(8,128)S(1)} %row_sums.4), channel_id=1, replica_groups={{0,1,2,3,16,17,18,19,32,33,34,35,48,49,50,51,64,65,66,67,80,81,82,83,96..., dimensions={0} | all-to-all | bytes 524288 | tf_op jit(solution)/shard_map/all_to_all | solution.py:55
  132.2 1.6 column_sums.3
  133.8 3.9 %collective-permute-start.18 = (f32[8,640]{1,0:T(8,128)S(1)}, f32[8,640]{1,0:T(8,128)S(1)}, u32[]{:S(2)}, u32[]{:S(2)}) collective-permute-start(f32[8,640]{1,0:T(8,128)S(1)} %get-tuple-element.24.mine_ref), channel_id=1, source_target_pairs={{0,8},{1,9},{2,10},{3,11},{4,12},{5,13},{6,14},{7,15},{8,0},{9,1},... | collective-permute-start | bytes 61448 | tf_op jit(solution)/shard_map/ppermute | solution.py:344
  139.4 1.2 collective-permute-start.20
  140.6 1.2 collective-permute-start.21
  143.6 1.5 row_sums.5
  145.1 21.2 %all_to_all.22.got_ref = f32[32,24,128]{2,1,0:T(8,128)S(1)} all-to-all(f32[32,24,128]{2,1,0:T(8,128)S(1)} %row_sums.5), channel_id=1, replica_groups={{0,1,2,3,16,17,18,19,32,33,34,35,48,49,50,51,64,65,66,67,80,81,82,83,96..., dimensions={0} | all-to-all | bytes 786432 | tf_op jit(solution)/shard_map/all_to_all | solution.py:55
  166.9 7.5 %all-to-all-start.3 = ((f32[32,4,512]{2,1,0:T(4,128)}), f32[32,4,512]{2,1,0:T(4,128)S(1)}, u32[]{:S(2)}, u32[]{:S(2)}) async-start(f32[32,4,512]{2,1,0:T(4,128)} %get-tuple-element.26), calls=%async_computation.3 | async-start | bytes 524288 | tf_op jit(solution)/shard_map/all_to_all | solution.py:357
  175.3 1.9 collective-permute-done.22.other_ref
  177.3 10.3 %final_scale.1 = bf16[256,16384]{1,0:T(8,128)(2,1)} custom-call(s32[5]{0:T(128)S(1)} %stack.23.where_ref, bf16[16,384,512]{2,1,0:T(8,128)(2,1)} %bitcast.9, bf16[16,384,512]{2,1,0:T(8,128)(2,1)} %bitcast.10, bf16[256,384]{1,0:T(8,128)(2,1)S(1)} %units.1.unit_ref.units_ref, f32[32,1,512]{2,1,0:T(1,128)S(1)} %get-tuple-element.29.cols_ref, ...), custom_call_target="tpu_custom_call" | custom-call | tf_op jit(solution)/shard_map/final_scale/pallas_call | solution.py:283
  187.9 1.4 cls_final.1
  (59 shorter events, 19.4 us)
Async XLA Ops:
  7.2 170.1 %all-gather.6.cloned.1.call-start = ((), (), s32[]{:S(2)}) async-start(), calls=%async_computation.4 | async-start | bytes 6684672 | tf_op jit(solution)/shard_map/all_gather | solution.py:321
  7.2 7.2 %collective-permute-start = (bf16[4,384]{1,0:T(4,128)(2,1)}, bf16[4,384]{1,0:T(4,128)(2,1)S(1)}, u32[]{:S(2)}, u32[]{:S(2)}) collective-permute-start(bf16[4,384]{1,0:T(4,128)(2,1)} %cls_ref.2), channel_id=1, source_target_pairs={{0,8},{1,9},{2,10},{3,11},{4,12},{5,13},{6,14},{7,15},{8,0},{9,1},... | collective-permute-start | bytes 9224 | tf_op jit(solution)/shard_map/ppermute | solution.py:306
  10.5 47.3 %collective-permute-start.3 = (bf16[384,512]{1,0:T(8,128)(2,1)}, bf16[384,512]{1,0:T(8,128)(2,1)S(1)}, u32[]{:S(2)}, u32[]{:S(2)}) collective-permute-start(bf16[384,512]{1,0:T(8,128)(2,1)} %refs_0_.1), channel_id=1, source_target_pairs={{0,4},{1,5},{2,6},{3,7},{4,0},{5,1},{6,2},{7,3},{8,12},{9,13},{10,... | collective-permute-start | bytes 1179656 | tf_op jit(solution)/shard_map/ppermute | solution.py:310
  10.5 47.3 %collective-permute-start.4 = (bf16[384,512]{1,0:T(8,128)(2,1)}, bf16[384,512]{1,0:T(8,128)(2,1)S(1)}, u32[]{:S(2)}, u32[]{:S(2)}) collective-permute-start(bf16[384,512]{1,0:T(8,128)(2,1)} %refs_0_.1), channel_id=1, source_target_pairs={{0,128},{1,129},{2,130},{3,131},{4,132},{5,133},{6,134},{7,135},{8... | collective-permute-start | bytes 1179656 | tf_op jit(solution)/shard_map/ppermute | solution.py:310
  12.7 45.1 %collective-permute-start.5 = (bf16[384,512]{1,0:T(8,128)(2,1)}, bf16[384,512]{1,0:T(8,128)(2,1)S(1)}, u32[]{:S(2)}, u32[]{:S(2)}) collective-permute-start(bf16[384,512]{1,0:T(8,128)(2,1)} %refs_0_.1), channel_id=1, source_target_pairs={{0,132},{1,133},{2,134},{3,135},{4,128},{5,129},{6,130},{7,131},{8... | collective-permute-start | bytes 1179656 | tf_op jit(solution)/shard_map/ppermute | solution.py:310
  14.4 16.3 %collective-permute-start.1 = (bf16[4,384]{1,0:T(4,128)(2,1)}, bf16[4,384]{1,0:T(4,128)(2,1)S(1)}, u32[]{:S(2)}, u32[]{:S(2)}) collective-permute-start(bf16[4,384]{1,0:T(4,128)(2,1)} %cls_ref.2), channel_id=1, source_target_pairs={{0,128},{1,129},{2,130},{3,131},{4,132},{5,133},{6,134},{7,135},{8... | collective-permute-start | bytes 9224 | tf_op jit(solution)/shard_map/ppermute | solution.py:306
  14.4 17.2 %collective-permute-start.2 = (bf16[4,384]{1,0:T(4,128)(2,1)}, bf16[4,384]{1,0:T(4,128)(2,1)S(1)}, u32[]{:S(2)}, u32[]{:S(2)}) collective-permute-start(bf16[4,384]{1,0:T(4,128)(2,1)} %cls_ref.2), channel_id=1, source_target_pairs={{0,136},{1,137},{2,138},{3,139},{4,140},{5,141},{6,142},{7,143},{8... | collective-permute-start | bytes 9224 | tf_op jit(solution)/shard_map/ppermute | solution.py:306
  18.5 1.1 copy-start.3
  30.7 33.0 %collective-permute-start.6 = (bf16[384,512]{1,0:T(8,128)(2,1)}, bf16[384,512]{1,0:T(8,128)(2,1)S(1)}, u32[]{:S(2)}, u32[]{:S(2)}) collective-permute-start(bf16[384,512]{1,0:T(8,128)(2,1)} %refs_0_.1), channel_id=1, source_target_pairs={{0,8},{1,9},{2,10},{3,11},{4,12},{5,13},{6,14},{7,15},{8,0},{9,1},... | collective-permute-start | bytes 1179656 | tf_op jit(solution)/shard_map/ppermute | solution.py:318
  57.8 8.7 %copy-start.1 = (bf16[384,512]{1,0:T(8,128)(2,1)}, bf16[384,512]{1,0:T(8,128)(2,1)S(1)}, u32[]{:S(2)}) copy-start(bf16[384,512]{1,0:T(8,128)(2,1)S(1)} %collective-permute-done.4.refs_2_) | copy-start | bytes 1179652
  57.8 6.7 %collective-permute-start.7 = (bf16[384,512]{1,0:T(8,128)(2,1)S(1)}, bf16[384,512]{1,0:T(8,128)(2,1)S(1)}, u32[]{:S(2)}, u32[]{:S(2)}) collective-permute-start(bf16[384,512]{1,0:T(8,128)(2,1)S(1)} %collective-permute-done.3.refs_1_), channel_id=1, source_target_pairs={{0,8},{1,9},{2,10},{3,11},{4,12},{5,13},{6,14},{7,15},{8,0},{9,1},... | collective-permute-start | bytes 1179656 | tf_op jit(solution)/shard_map/ppermute | solution.py:318
  63.1 1.9 collective-permute-start.8
  63.2 2.4 %collective-permute-start.9 = (bf16[384,512]{1,0:T(8,128)(2,1)S(1)}, bf16[384,512]{1,0:T(8,128)(2,1)S(1)}, u32[]{:S(2)}, u32[]{:S(2)}) collective-permute-start(bf16[384,512]{1,0:T(8,128)(2,1)S(1)} %collective-permute-done.5.refs_3_), channel_id=1, source_target_pairs={{0,8},{1,9},{2,10},{3,11},{4,12},{5,13},{6,14},{7,15},{8,0},{9,1},... | collective-permute-start | bytes 1179656 | tf_op jit(solution)/shard_map/ppermute | solution.py:318
  66.4 110.8 %all-gather.8.cloned.1.call-start = ((), (), s32[]{:S(2)}) async-start(), calls=%async_computation.5 | async-start | bytes 6684672 | tf_op jit(solution)/shard_map/all_gather | solution.py:321
  67.2 1.0 copy-start
  68.2 1.0 copy-start.2
  69.2 1.0 copy-start.4
  70.2 1.0 copy-start.6
  76.1 1.3 collective-permute-start.10
  77.4 4.2 %collective-permute-start.11 = (f32[8,640]{1,0:T(8,128)S(1)}, f32[8,640]{1,0:T(8,128)S(1)}, u32[]{:S(2)}, u32[]{:S(2)}) collective-permute-start(f32[8,640]{1,0:T(8,128)S(1)} %add_core.3.mine_ref), channel_id=1, source_target_pairs={{0,132},{1,133},{2,134},{3,135},{4,128},{5,129},{6,130},{7,131},{8... | collective-permute-start | bytes 61448 | tf_op jit(solution)/shard_map/ppermute | solution.py:345
  77.4 4.3 %collective-permute-start.12 = (f32[8,640]{1,0:T(8,128)S(1)}, f32[8,640]{1,0:T(8,128)S(1)}, u32[]{:S(2)}, u32[]{:S(2)}) collective-permute-start(f32[8,640]{1,0:T(8,128)S(1)} %add_core.3.mine_ref), channel_id=1, source_target_pairs={{0,128},{1,129},{2,130},{3,131},{4,132},{5,133},{6,134},{7,135},{8... | collective-permute-start | bytes 61448 | tf_op jit(solution)/shard_map/ppermute | solution.py:345
  79.0 3.4 %collective-permute-start.13 = (f32[8,640]{1,0:T(8,128)S(1)}, f32[8,640]{1,0:T(8,128)S(1)}, u32[]{:S(2)}, u32[]{:S(2)}) collective-permute-start(f32[8,640]{1,0:T(8,128)S(1)} %add_core.3.mine_ref), channel_id=1, source_target_pairs={{0,4},{1,5},{2,6},{3,7},{4,0},{5,1},{6,2},{7,3},{8,12},{9,13},{10,... | collective-permute-start | bytes 61448 | tf_op jit(solution)/shard_map/ppermute | solution.py:345
  107.1 4.0 %collective-permute-start.14 = (f32[8,640]{1,0:T(8,128)S(1)}, f32[8,640]{1,0:T(8,128)S(1)}, u32[]{:S(2)}, u32[]{:S(2)}) collective-permute-start(f32[8,640]{1,0:T(8,128)S(1)} %column_sums.2.mine_ref), channel_id=1, source_target_pairs={{0,8},{1,9},{2,10},{3,11},{4,12},{5,13},{6,14},{7,15},{8,0},{9,1},... | collective-permute-start | bytes 61448 | tf_op jit(solution)/shard_map/ppermute | solution.py:344
  111.1 3.8 %collective-permute-start.15 = (f32[8,640]{1,0:T(8,128)S(1)}, f32[8,640]{1,0:T(8,128)S(1)}, u32[]{:S(2)}, u32[]{:S(2)}) collective-permute-start(f32[8,640]{1,0:T(8,128)S(1)} %add_core.4.mine_ref), channel_id=1, source_target_pairs={{0,132},{1,133},{2,134},{3,135},{4,128},{5,129},{6,130},{7,131},{8... | collective-permute-start | bytes 61448 | tf_op jit(solution)/shard_map/ppermute | solution.py:345
  113.1 4.1 %collective-permute-start.16 = (f32[8,640]{1,0:T(8,128)S(1)}, f32[8,640]{1,0:T(8,128)S(1)}, u32[]{:S(2)}, u32[]{:S(2)}) collective-permute-start(f32[8,640]{1,0:T(8,128)S(1)} %add_core.4.mine_ref), channel_id=1, source_target_pairs={{0,128},{1,129},{2,130},{3,131},{4,132},{5,133},{6,134},{7,135},{8... | collective-permute-start | bytes 61448 | tf_op jit(solution)/shard_map/ppermute | solution.py:345
  114.2 3.0 %collective-permute-start.17 = (f32[8,640]{1,0:T(8,128)S(1)}, f32[8,640]{1,0:T(8,128)S(1)}, u32[]{:S(2)}, u32[]{:S(2)}) collective-permute-start(f32[8,640]{1,0:T(8,128)S(1)} %add_core.4.mine_ref), channel_id=1, source_target_pairs={{0,4},{1,5},{2,6},{3,7},{4,0},{5,1},{6,2},{7,3},{8,12},{9,13},{10,... | collective-permute-start | bytes 61448 | tf_op jit(solution)/shard_map/ppermute | solution.py:345
  133.8 4.7 %collective-permute-start.18 = (f32[8,640]{1,0:T(8,128)S(1)}, f32[8,640]{1,0:T(8,128)S(1)}, u32[]{:S(2)}, u32[]{:S(2)}) collective-permute-start(f32[8,640]{1,0:T(8,128)S(1)} %get-tuple-element.24.mine_ref), channel_id=1, source_target_pairs={{0,8},{1,9},{2,10},{3,11},{4,12},{5,13},{6,14},{7,15},{8,0},{9,1},... | collective-permute-start | bytes 61448 | tf_op jit(solution)/shard_map/ppermute | solution.py:344
  138.5 4.2 %collective-permute-start.19 = (f32[8,640]{1,0:T(8,128)S(1)}, f32[8,640]{1,0:T(8,128)S(1)}, u32[]{:S(2)}, u32[]{:S(2)}) collective-permute-start(f32[8,640]{1,0:T(8,128)S(1)} %add_core.5.mine_ref), channel_id=1, source_target_pairs={{0,132},{1,133},{2,134},{3,135},{4,128},{5,129},{6,130},{7,131},{8... | collective-permute-start | bytes 61448 | tf_op jit(solution)/shard_map/ppermute | solution.py:345
  139.4 4.2 %collective-permute-start.20 = (f32[8,640]{1,0:T(8,128)S(1)}, f32[8,640]{1,0:T(8,128)S(1)}, u32[]{:S(2)}, u32[]{:S(2)}) collective-permute-start(f32[8,640]{1,0:T(8,128)S(1)} %add_core.5.mine_ref), channel_id=1, source_target_pairs={{0,128},{1,129},{2,130},{3,131},{4,132},{5,133},{6,134},{7,135},{8... | collective-permute-start | bytes 61448 | tf_op jit(solution)/shard_map/ppermute | solution.py:345
  140.6 3.0 %collective-permute-start.21 = (f32[8,640]{1,0:T(8,128)S(1)}, f32[8,640]{1,0:T(8,128)S(1)}, u32[]{:S(2)}, u32[]{:S(2)}) collective-permute-start(f32[8,640]{1,0:T(8,128)S(1)} %add_core.5.mine_ref), channel_id=1, source_target_pairs={{0,4},{1,5},{2,6},{3,7},{4,0},{5,1},{6,2},{7,3},{8,12},{9,13},{10,... | collective-permute-start | bytes 61448 | tf_op jit(solution)/shard_map/ppermute | solution.py:345
  166.9 20.9 %all-to-all-start.3 = ((f32[32,4,512]{2,1,0:T(4,128)}), f32[32,4,512]{2,1,0:T(4,128)S(1)}, u32[]{:S(2)}, u32[]{:S(2)}) async-start(f32[32,4,512]{2,1,0:T(4,128)} %get-tuple-element.26), calls=%async_computation.3 | async-start | bytes 524288 | tf_op jit(solution)/shard_map/all_to_all | solution.py:357
  174.4 2.8 %collective-permute-start.22 = (f32[8,128]{1,0:T(8,128)S(1)}, f32[8,128]{1,0:T(8,128)S(1)}, u32[]{:S(2)}, u32[]{:S(2)}) collective-permute-start(f32[8,128]{1,0:T(8,128)S(1)} %get-tuple-element.25.mine_ref.sums_ref), channel_id=1, source_target_pairs={{0,4},{1,5},{2,6},{3,7},{4,0},{5,1},{6,2},{7,3},{8,12},{9,13},{10,... | collective-permute-start | bytes 12296 | tf_op jit(solution)/shard_map/ppermute | solution.py:358
  (3 other events, 2.1 us)
Sparse Core Ops, SparseCore 0:
  66.5 48.6 all-gather.5
  117.6 53.8 all-gather.7

commit v5 on v3

--- a/solution.py
+++ b/solution.py
@@ -82,6 +82,13 @@
 
 def across(block):
     return jnp.sum(jnp.transpose(block), axis=0, keepdims=True)
+
+
+def summed(got_ref, row):
+    total = got_ref[0, row]
+    for k in range(1, 32):
+        total = total + got_ref[k, row]
+    return total
 
 
 def swapped(rows, step):
@@ -164,12 +171,9 @@
 
 
 def columns_body(last, got_ref, kern_ref, cls_kern_ref, message_ref, *more):
-    total = got_ref[0]
-    for k in range(1, 32):
-        total = total + got_ref[k]
-    row_scale = 1.0 / total[:9]
+    row_scale = [1.0 / summed(got_ref, row) for row in range(9)]
     cls_kern = cls_kern_ref[...]
-    cols, sums = cls_step(cls_kern, row_scale[8:9])
+    cols, sums = cls_step(cls_kern, row_scale[8])
     if last:
         for q in range(4):
             scaled = cls_kern[:, q * 128 : q * 128 + 128] * cols[q]
@@ -178,7 +182,7 @@
                 more[0][(yh * NZ + z) * 2 + core, :, q * 128 : q * 128 + 128] = scaled[n * 4 : n * 4 + 4]
     acc = more[-1]
     for z in range(NZ):
-        wide = down(row_scale[z : z + 1]).reshape(16, 8, 128)
+        wide = down(row_scale[z]).reshape(16, 8, 128)
         for t in range(32):
             block = kern_ref[z * 128 : z * 128 + 128, t * 128 : t * 128 + 128]
             part = jnp.sum(block.reshape(16, 8, 128) * wide, axis=0)
@@ -210,33 +214,23 @@
             block = kern_ref[z * 128 : z * 128 + 128, t * 128 : t * 128 + 128]
             acc = acc + block.reshape(16, 8, 128) * wide_ref[:, t * 128 : t * 128 + 128][None]
         sums.append(across(acc.reshape(128, 128)))
-    if last:
-        own = [cols[k : k + 1, q * 128 : q * 128 + 128] for k in (0, 2, 4, 6) for q in range(4)]
-        own = jnp.concatenate(own, axis=0)
-        rest = jnp.zeros((6, 128), F32)
-        for z in range(NZ):
-            block = jnp.concatenate([own, sums[z], cls, rest], axis=0)
-            for x in range(NX):
-                send_ref[z * NX + x] = block
-    else:
-        block = jnp.concatenate(sums + [cls, jnp.zeros((7, 128), F32)], axis=0)
-        for k in range(32):
-            send_ref[k] = block
+    own = [cols[k : k + 1, q * 128 : q * 128 + 128] for k in (0, 2, 4, 6) for q in range(4)]
+    for k in range(32):
+        block = own + [sums[k // NX], cls] if last else sums + [cls]
+        for at, row in enumerate(block):
+            send_ref[k, at] = row
 
 
 def settle_body(where_ref, got_ref, cols_ref, sums_ref):
     core, yh, x = where_ref[0], where_ref[2], where_ref[3]
-    total = got_ref[0, 16:24, :]
-    for k in range(1, 32):
-        total = total + got_ref[k, 16:24, :]
-    sums_ref[...] = total
+    sums_ref[...] = jnp.concatenate([summed(got_ref, 16), summed(got_ref, 17), jnp.zeros((6, 128), F32)], axis=0)
     for z in range(NZ):
         for cr in range(2):
             for yr in range(2):
                 row = (jnp.bitwise_xor(yh, yr) * NZ + z) * 2 + jnp.bitwise_xor(core, cr)
                 for q in range(4):
                     at = (cr * 2 + yr) * 4 + q
-                    cols_ref[row, :, q * 128 : q * 128 + 128] = got_ref[z * NX + x, at : at + 1, :]
+                    cols_ref[row, :, q * 128 : q * 128 + 128] = got_ref[z * NX + x, at]
 
 
 def cls_final_body(where_ref, scaled_ref, sums_ref, out_ref):
@@ -357,7 +351,7 @@
         parts = [lax.ppermute(message, BOTH, swap(dyh=dyh, dyl=dyl)) for dyh, dyl in Y_STEPS]
         send = call(
             functools.partial(rows_body, last),
-            shape((32, 24 if last else 16, 128)),
+            shape((32, 18 if last else 9, 1, 128)),
             [VM] * 5,
             "row_sums",
             [pltpu.VMEM((8, 4096), F32)],

time: 184 us -> 177 us (0.962)
  blocking collectives: 58.4 us -> 51.1 us
    all_to_all x3, blocking collectives: 58.4 us -> 51.1 us  [exchange(): lax.all_to_all(value, BOTH, 0, 0, axis_index_groups=group, tiled=True)]
  transfers between devices with their start and end apart: 27 -> 27, of which waited for: 17 -> 18; matrix products, arithmetic and copies ran while one was open for 0% -> 0% of each run, Pallas kernels for 14% -> 15%
where the time goes in v5:
time: 177 us; the launch traced here: 176 us
  blocking collectives  51.1 us (29%)
  starting transfers between devices  51 us (29%)
  Pallas kernels  29 us (16%)
  waiting for transfers between devices  26.4 us (15%)
  between operations  14.2 us (8%)
  local copies, waits for them, and re-layouts  4.23 us (2%)
    all_to_all x3, blocking collectives, exchange(): lax.all_to_all(value, BOTH, 0, 0, axis_index_groups=group, tiled=True)  51.1 us
    ppermute x3, waiting for transfers between devices, per_device(): near[dyh, dyl] = lax.ppermute(patch_protos, BOTH, swap(dyh=dyh, dyl=dyl))  11.7 us
    pallas_call x1, Pallas kernels, final(): pl.pallas_call(final_body, out_shape=shape((256, 16384), BF16), in_specs=...  10.3 us
    ppermute x9, starting transfers between devices, per_device(): lax.ppermute(message, BOTH, swap(dyh=dyh, dyl=dyl))  9.76 us
    all_to_all x1, starting transfers between devices, exchange(): lax.all_to_all(value, BOTH, 0, 0, axis_index_groups=group, tiled=True)  8.19 us
    pallas_call x1, Pallas kernels, per_device(): call(kernel_body, (pltpu.VMEM((1024, 4096), F32), shape((128, 512)), shap...  8.18 us
    ppermute x4, starting transfers between devices, per_device(): pieces += [lax.ppermute(piece, BOTH, CORE) for piece in pieces]  7.79 us
    all_to_all x1, starting transfers between devices, per_device(): cls_scaled = lax.all_to_all(cls_scaled, 'dp', 0, 0, tiled=True)  7.32 us
  transfers between devices with their start and end apart: 27, of which 18 were waited for; matrix products, arithmetic and copies ran while one was open for 0% of the time, Pallas kernels for 15%

profile of v5, /device:TPU:1, one launch (start us, length us, event | category | flops | bytes accessed | tf_op | source)
XLA Modules:
  0.0 176.0 jit_solution(1294637444494596607)
XLA Ops:
  7.2 3.3 %collective-permute-start = (bf16[4,384]{1,0:T(4,128)(2,1)}, bf16[4,384]{1,0:T(4,128)(2,1)S(1)}, u32[]{:S(2)}, u32[]{:S(2)}) collective-permute-start(bf16[4,384]{1,0:T(4,128)(2,1)} %cls_ref.2), channel_id=1, source_target_pairs={{0,8},{1,9},{2,10},{3,11},{4,12},{5,13},{6,14},{7,15},{8,0},{9,1},... | collective-permute-start | bytes 9224 | tf_op jit(solution)/shard_map/ppermute | solution.py:308
  10.5 1.2 collective-permute-start.1
  11.7 2.0 %collective-permute-start.2 = (bf16[4,384]{1,0:T(4,128)(2,1)}, bf16[4,384]{1,0:T(4,128)(2,1)S(1)}, u32[]{:S(2)}, u32[]{:S(2)}) collective-permute-start(bf16[4,384]{1,0:T(4,128)(2,1)} %cls_ref.2), channel_id=1, source_target_pairs={{0,136},{1,137},{2,138},{3,139},{4,140},{5,141},{6,142},{7,143},{8... | collective-permute-start | bytes 9224 | tf_op jit(solution)/shard_map/ppermute | solution.py:308
  17.1 1.6 send.1
  18.7 8.2 %all-to-all-start = ((bf16[8,144,384]{2,1,0:T(8,128)(2,1)}), bf16[8,144,384]{2,1,0:T(8,128)(2,1)S(1)}, u32[]{:S(2)}, u32[]{:S(2)}) async-start(bf16[8,144,384]{2,1,0:T(8,128)(2,1)} %send.1), calls=%async_computation | async-start | bytes 1769472 | tf_op jit(solution)/shard_map/all_to_all | solution.py:55
  27.4 1.6 collective-permute-start.4
  28.9 1.9 %collective-permute-start.5 = (bf16[384,512]{1,0:T(8,128)(2,1)}, bf16[384,512]{1,0:T(8,128)(2,1)S(1)}, u32[]{:S(2)}, u32[]{:S(2)}) collective-permute-start(bf16[384,512]{1,0:T(8,128)(2,1)} %refs_0_.1), channel_id=1, source_target_pairs={{0,132},{1,133},{2,134},{3,135},{4,128},{5,129},{6,130},{7,131},{8... | collective-permute-start | bytes 1179656 | tf_op jit(solution)/shard_map/ppermute | solution.py:312
  30.9 1.5 collective-permute-start.6
  32.3 4.9 %collective-permute-done.3.refs_1_ = bf16[384,512]{1,0:T(8,128)(2,1)S(1)} collective-permute-done((bf16[384,512]{1,0:T(8,128)(2,1)}, bf16[384,512]{1,0:T(8,128)(2,1)S(1)}, u32[]{:S(2)}, u32[]{:S(2)}) %collective-permute-start.3) | collective-permute-done | bytes 393248 | tf_op jit(solution)/shard_map/ppermute | solution.py:312
  37.2 2.6 %collective-permute-start.7 = (bf16[384,512]{1,0:T(8,128)(2,1)S(1)}, bf16[384,512]{1,0:T(8,128)(2,1)S(1)}, u32[]{:S(2)}, u32[]{:S(2)}) collective-permute-start(bf16[384,512]{1,0:T(8,128)(2,1)S(1)} %collective-permute-done.3.refs_1_), channel_id=1, source_target_pairs={{0,8},{1,9},{2,10},{3,11},{4,12},{5,13},{6,14},{7,15},{8,0},{9,1},... | collective-permute-start | bytes 1179656 | tf_op jit(solution)/shard_map/ppermute | solution.py:314
  39.8 6.3 %collective-permute-done.4.refs_2_ = bf16[384,512]{1,0:T(8,128)(2,1)S(1)} collective-permute-done((bf16[384,512]{1,0:T(8,128)(2,1)}, bf16[384,512]{1,0:T(8,128)(2,1)S(1)}, u32[]{:S(2)}, u32[]{:S(2)}) %collective-permute-start.4) | collective-permute-done | bytes 393248 | tf_op jit(solution)/shard_map/ppermute | solution.py:312
  46.2 1.6 collective-permute-start.8
  48.2 2.1 %collective-permute-start.9 = (bf16[384,512]{1,0:T(8,128)(2,1)S(1)}, bf16[384,512]{1,0:T(8,128)(2,1)}, u32[]{:S(2)}, u32[]{:S(2)}) collective-permute-start(bf16[384,512]{1,0:T(8,128)(2,1)S(1)} %collective-permute-done.5.refs_3_), channel_id=1, source_target_pairs={{0,8},{1,9},{2,10},{3,11},{4,12},{5,13},{6,14},{7,15},{8,0},{9,1},... | collective-permute-start | bytes 1179656 | tf_op jit(solution)/shard_map/ppermute | solution.py:314
  53.5 8.2 %patch_kernel.1 = (f32[1024,4096]{1,0:T(8,128)S(1)}, f32[128,512]{1,0:T(8,128)}, f32[8,640]{1,0:T(8,128)}) custom-call(bf16[8,144,384]{2,1,0:T(8,128)(2,1)} %copy-done.5, bf16[384,512]{1,0:T(8,128)(2,1)} %cls_ref.3, bf16[384,512]{1,0:T(8,128)(2,1)} %refs_0_.1, bf16[384,512]{1,0:T(8,128)(2,1)} %copy-done.7, bf16[384,512]{1,0:T(8,128)(2,1)} %copy-done.6, ...), custom_call_target="tpu_custom_call" | custom-call | tf_op jit(solution)/shard_map/patch_kernel/pallas_call | solution.py:323
  69.3 1.2 row_sums.3
  70.5 20.3 %all_to_all.25.got_ref = f32[32,9,1,128]{3,2,1,0:T(1,128)S(1)} all-to-all(f32[32,9,1,128]{3,2,1,0:T(1,128)S(1)} %row_sums.3), channel_id=1, replica_groups={{0,1,2,3,16,17,18,19,32,33,34,35,48,49,50,51,64,65,66,67,80,81,82,83,96..., dimensions={0} | all-to-all | bytes 294912 | tf_op jit(solution)/shard_map/all_to_all | solution.py:55
  90.8 1.4 column_sums.2.mine_ref
  92.2 3.3 %collective-permute-start.14 = (f32[8,640]{1,0:T(8,128)S(1)}, f32[8,640]{1,0:T(8,128)S(1)}, u32[]{:S(2)}, u32[]{:S(2)}) collective-permute-start(f32[8,640]{1,0:T(8,128)S(1)} %column_sums.2.mine_ref), channel_id=1, source_target_pairs={{0,8},{1,9},{2,10},{3,11},{4,12},{5,13},{6,14},{7,15},{8,0},{9,1},... | collective-permute-start | bytes 61448 | tf_op jit(solution)/shard_map/ppermute | solution.py:350
  98.3 1.3 collective-permute-start.17
  101.3 1.2 row_sums.4
  102.6 12.6 %all_to_all.26.got_ref = f32[32,9,1,128]{3,2,1,0:T(1,128)S(1)} all-to-all(f32[32,9,1,128]{3,2,1,0:T(1,128)S(1)} %row_sums.4), channel_id=1, replica_groups={{0,1,2,3,16,17,18,19,32,33,34,35,48,49,50,51,64,65,66,67,80,81,82,83,96..., dimensions={0} | all-to-all | bytes 294912 | tf_op jit(solution)/shard_map/all_to_all | solution.py:55
  115.1 1.4 column_sums.3
  116.6 3.4 %collective-permute-start.18 = (f32[8,640]{1,0:T(8,128)S(1)}, f32[8,640]{1,0:T(8,128)S(1)}, u32[]{:S(2)}, u32[]{:S(2)}) collective-permute-start(f32[8,640]{1,0:T(8,128)S(1)} %get-tuple-element.18.mine_ref), channel_id=1, source_target_pairs={{0,8},{1,9},{2,10},{3,11},{4,12},{5,13},{6,14},{7,15},{8,0},{9,1},... | collective-permute-start | bytes 61448 | tf_op jit(solution)/shard_map/ppermute | solution.py:350
  120.8 1.8 %collective-permute-start.19 = (f32[8,640]{1,0:T(8,128)S(1)}, f32[8,640]{1,0:T(8,128)S(1)}, u32[]{:S(2)}, u32[]{:S(2)}) collective-permute-start(f32[8,640]{1,0:T(8,128)S(1)} %add_core.5.mine_ref), channel_id=1, source_target_pairs={{0,132},{1,133},{2,134},{3,135},{4,128},{5,129},{6,130},{7,131},{8... | collective-permute-start | bytes 61448 | tf_op jit(solution)/shard_map/ppermute | solution.py:351
  122.6 1.1 collective-permute-start.20
  125.0 1.7 collective-permute-done.20.b_ref
  126.9 1.3 row_sums.5
  128.2 18.2 %all_to_all.27.got_ref = f32[32,18,1,128]{3,2,1,0:T(1,128)S(1)} all-to-all(f32[32,18,1,128]{3,2,1,0:T(1,128)S(1)} %row_sums.5), channel_id=1, replica_groups={{0,1,2,3,16,17,18,19,32,33,34,35,48,49,50,51,64,65,66,67,80,81,82,83,96..., dimensions={0} | all-to-all | bytes 589824 | tf_op jit(solution)/shard_map/all_to_all | solution.py:55
  147.1 7.3 %all-to-all-start.4 = ((f32[32,4,512]{2,1,0:T(4,128)}), f32[32,4,512]{2,1,0:T(4,128)S(1)}, u32[]{:S(2)}, u32[]{:S(2)}) async-start(f32[32,4,512]{2,1,0:T(4,128)} %get-tuple-element.20), calls=%async_computation.4 | async-start | bytes 524288 | tf_op jit(solution)/shard_map/all_to_all | solution.py:363
  154.5 2.7 %collective-permute-done.22.other_ref = f32[8,128]{1,0:T(8,128)S(1)} collective-permute-done((f32[8,128]{1,0:T(8,128)S(1)}, f32[8,128]{1,0:T(8,128)S(1)}, u32[]{:S(2)}, u32[]{:S(2)}) %collective-permute-start.22) | collective-permute-done | bytes 4128 | tf_op jit(solution)/shard_map/ppermute | solution.py:364
  157.2 10.3 %final_scale.1 = bf16[256,16384]{1,0:T(8,128)(2,1)} custom-call(s32[5]{0:T(128)S(1)} %stack.23.where_ref, bf16[16,384,512]{2,1,0:T(8,128)(2,1)} %bitcast.7, bf16[16,384,512]{2,1,0:T(8,128)(2,1)} %bitcast.8, bf16[256,384]{1,0:T(8,128)(2,1)S(1)} %units.1.unit_ref.units_ref, f32[32,1,512]{2,1,0:T(1,128)S(1)} %get-tuple-element.23.cols_ref, ...), custom_call_target="tpu_custom_call" | custom-call | tf_op jit(solution)/shard_map/final_scale/pallas_call | solution.py:285
  167.8 1.4 cls_final.1
  (66 shorter events, 22.8 us)
Async XLA Ops:
  7.2 8.9 %collective-permute-start = (bf16[4,384]{1,0:T(4,128)(2,1)}, bf16[4,384]{1,0:T(4,128)(2,1)S(1)}, u32[]{:S(2)}, u32[]{:S(2)}) collective-permute-start(bf16[4,384]{1,0:T(4,128)(2,1)} %cls_ref.2), channel_id=1, source_target_pairs={{0,8},{1,9},{2,10},{3,11},{4,12},{5,13},{6,14},{7,15},{8,0},{9,1},... | collective-permute-start | bytes 9224 | tf_op jit(solution)/shard_map/ppermute | solution.py:308
  10.5 5.5 %collective-permute-start.1 = (bf16[4,384]{1,0:T(4,128)(2,1)}, bf16[4,384]{1,0:T(4,128)(2,1)S(1)}, u32[]{:S(2)}, u32[]{:S(2)}) collective-permute-start(bf16[4,384]{1,0:T(4,128)(2,1)} %cls_ref.2), channel_id=1, source_target_pairs={{0,128},{1,129},{2,130},{3,131},{4,132},{5,133},{6,134},{7,135},{8... | collective-permute-start | bytes 9224 | tf_op jit(solution)/shard_map/ppermute | solution.py:308
  11.7 4.7 %collective-permute-start.2 = (bf16[4,384]{1,0:T(4,128)(2,1)}, bf16[4,384]{1,0:T(4,128)(2,1)S(1)}, u32[]{:S(2)}, u32[]{:S(2)}) collective-permute-start(bf16[4,384]{1,0:T(4,128)(2,1)} %cls_ref.2), channel_id=1, source_target_pairs={{0,136},{1,137},{2,138},{3,139},{4,140},{5,141},{6,142},{7,143},{8... | collective-permute-start | bytes 9224 | tf_op jit(solution)/shard_map/ppermute | solution.py:308
  18.7 33.9 %all-to-all-start = ((bf16[8,144,384]{2,1,0:T(8,128)(2,1)}), bf16[8,144,384]{2,1,0:T(8,128)(2,1)S(1)}, u32[]{:S(2)}, u32[]{:S(2)}) async-start(bf16[8,144,384]{2,1,0:T(8,128)(2,1)} %send.1), calls=%async_computation | async-start | bytes 1769472 | tf_op jit(solution)/shard_map/all_to_all | solution.py:55
  26.9 130.3 %all-gather.5.cloned.1.call-start = ((), (), s32[]{:S(2)}) async-start(), calls=%async_computation.5 | async-start | bytes 6684672 | tf_op jit(solution)/shard_map/all_gather | solution.py:321
  26.9 10.3 %collective-permute-start.3 = (bf16[384,512]{1,0:T(8,128)(2,1)}, bf16[384,512]{1,0:T(8,128)(2,1)S(1)}, u32[]{:S(2)}, u32[]{:S(2)}) collective-permute-start(bf16[384,512]{1,0:T(8,128)(2,1)} %refs_0_.1), channel_id=1, source_target_pairs={{0,4},{1,5},{2,6},{3,7},{4,0},{5,1},{6,2},{7,3},{8,12},{9,13},{10,... | collective-permute-start | bytes 1179656 | tf_op jit(solution)/shard_map/ppermute | solution.py:312
  27.4 18.8 %collective-permute-start.4 = (bf16[384,512]{1,0:T(8,128)(2,1)}, bf16[384,512]{1,0:T(8,128)(2,1)S(1)}, u32[]{:S(2)}, u32[]{:S(2)}) collective-permute-start(bf16[384,512]{1,0:T(8,128)(2,1)} %refs_0_.1), channel_id=1, source_target_pairs={{0,128},{1,129},{2,130},{3,131},{4,132},{5,133},{6,134},{7,135},{8... | collective-permute-start | bytes 1179656 | tf_op jit(solution)/shard_map/ppermute | solution.py:312
  28.9 19.3 %collective-permute-start.5 = (bf16[384,512]{1,0:T(8,128)(2,1)}, bf16[384,512]{1,0:T(8,128)(2,1)S(1)}, u32[]{:S(2)}, u32[]{:S(2)}) collective-permute-start(bf16[384,512]{1,0:T(8,128)(2,1)} %refs_0_.1), channel_id=1, source_target_pairs={{0,132},{1,133},{2,134},{3,135},{4,128},{5,129},{6,130},{7,131},{8... | collective-permute-start | bytes 1179656 | tf_op jit(solution)/shard_map/ppermute | solution.py:312
  30.9 19.5 %collective-permute-start.6 = (bf16[384,512]{1,0:T(8,128)(2,1)}, bf16[384,512]{1,0:T(8,128)(2,1)S(1)}, u32[]{:S(2)}, u32[]{:S(2)}) collective-permute-start(bf16[384,512]{1,0:T(8,128)(2,1)} %refs_0_.1), channel_id=1, source_target_pairs={{0,8},{1,9},{2,10},{3,11},{4,12},{5,13},{6,14},{7,15},{8,0},{9,1},... | collective-permute-start | bytes 1179656 | tf_op jit(solution)/shard_map/ppermute | solution.py:314
  37.2 16.1 %copy-start.7 = (bf16[384,512]{1,0:T(8,128)(2,1)}, bf16[384,512]{1,0:T(8,128)(2,1)S(1)}, u32[]{:S(2)}) copy-start(bf16[384,512]{1,0:T(8,128)(2,1)S(1)} %collective-permute-done.3.refs_1_) | copy-start | bytes 1179652
  37.2 13.1 %collective-permute-start.7 = (bf16[384,512]{1,0:T(8,128)(2,1)S(1)}, bf16[384,512]{1,0:T(8,128)(2,1)S(1)}, u32[]{:S(2)}, u32[]{:S(2)}) collective-permute-start(bf16[384,512]{1,0:T(8,128)(2,1)S(1)} %collective-permute-done.3.refs_1_), channel_id=1, source_target_pairs={{0,8},{1,9},{2,10},{3,11},{4,12},{5,13},{6,14},{7,15},{8,0},{9,1},... | collective-permute-start | bytes 1179656 | tf_op jit(solution)/shard_map/ppermute | solution.py:314
  46.2 6.4 %copy-start.6 = (bf16[384,512]{1,0:T(8,128)(2,1)}, bf16[384,512]{1,0:T(8,128)(2,1)S(1)}, u32[]{:S(2)}) copy-start(bf16[384,512]{1,0:T(8,128)(2,1)S(1)} %collective-permute-done.4.refs_2_) | copy-start | bytes 1179652
  46.2 4.2 %collective-permute-start.8 = (bf16[384,512]{1,0:T(8,128)(2,1)S(1)}, bf16[384,512]{1,0:T(8,128)(2,1)S(1)}, u32[]{:S(2)}, u32[]{:S(2)}) collective-permute-start(bf16[384,512]{1,0:T(8,128)(2,1)S(1)} %collective-permute-done.4.refs_2_), channel_id=1, source_target_pairs={{0,8},{1,9},{2,10},{3,11},{4,12},{5,13},{6,14},{7,15},{8,0},{9,1},... | collective-permute-start | bytes 1179656 | tf_op jit(solution)/shard_map/ppermute | solution.py:314
  48.2 5.1 %copy-start.8 = (bf16[384,512]{1,0:T(8,128)(2,1)}, bf16[384,512]{1,0:T(8,128)(2,1)S(1)}, u32[]{:S(2)}) copy-start(bf16[384,512]{1,0:T(8,128)(2,1)S(1)} %collective-permute-done.5.refs_3_) | copy-start | bytes 1179652
  48.2 3.6 %collective-permute-start.9 = (bf16[384,512]{1,0:T(8,128)(2,1)S(1)}, bf16[384,512]{1,0:T(8,128)(2,1)}, u32[]{:S(2)}, u32[]{:S(2)}) collective-permute-start(bf16[384,512]{1,0:T(8,128)(2,1)S(1)} %collective-permute-done.5.refs_3_), channel_id=1, source_target_pairs={{0,8},{1,9},{2,10},{3,11},{4,12},{5,13},{6,14},{7,15},{8,0},{9,1},... | collective-permute-start | bytes 1179656 | tf_op jit(solution)/shard_map/ppermute | solution.py:314
  50.3 3.0 %copy-start.10 = (bf16[384,512]{1,0:T(8,128)(2,1)}, bf16[384,512]{1,0:T(8,128)(2,1)S(1)}, u32[]{:S(2)}) copy-start(bf16[384,512]{1,0:T(8,128)(2,1)S(1)} %collective-permute-done.7.refs_5_) | copy-start | bytes 1179652
  52.6 104.6 %all-gather.7.cloned.1.call-start = ((), (), s32[]{:S(2)}) async-start(), calls=%async_computation.6 | async-start | bytes 6684672 | tf_op jit(solution)/shard_map/all_gather | solution.py:321
  61.6 1.6 collective-permute-start.10
  64.0 4.2 %collective-permute-start.11 = (f32[8,640]{1,0:T(8,128)S(1)}, f32[8,640]{1,0:T(8,128)S(1)}, u32[]{:S(2)}, u32[]{:S(2)}) collective-permute-start(f32[8,640]{1,0:T(8,128)S(1)} %add_core.3.mine_ref), channel_id=1, source_target_pairs={{0,132},{1,133},{2,134},{3,135},{4,128},{5,129},{6,130},{7,131},{8... | collective-permute-start | bytes 61448 | tf_op jit(solution)/shard_map/ppermute | solution.py:351
  65.1 4.2 %collective-permute-start.12 = (f32[8,640]{1,0:T(8,128)S(1)}, f32[8,640]{1,0:T(8,128)S(1)}, u32[]{:S(2)}, u32[]{:S(2)}) collective-permute-start(f32[8,640]{1,0:T(8,128)S(1)} %add_core.3.mine_ref), channel_id=1, source_target_pairs={{0,128},{1,129},{2,130},{3,131},{4,132},{5,133},{6,134},{7,135},{8... | collective-permute-start | bytes 61448 | tf_op jit(solution)/shard_map/ppermute | solution.py:351
  66.2 3.1 %collective-permute-start.13 = (f32[8,640]{1,0:T(8,128)S(1)}, f32[8,640]{1,0:T(8,128)S(1)}, u32[]{:S(2)}, u32[]{:S(2)}) collective-permute-start(f32[8,640]{1,0:T(8,128)S(1)} %add_core.3.mine_ref), channel_id=1, source_target_pairs={{0,4},{1,5},{2,6},{3,7},{4,0},{5,1},{6,2},{7,3},{8,12},{9,13},{10,... | collective-permute-start | bytes 61448 | tf_op jit(solution)/shard_map/ppermute | solution.py:351
  69.3 21.5 %copy-start = (f32[128,512]{1,0:T(8,128)S(1)}, f32[128,512]{1,0:T(8,128)}, u32[]{:S(2)}) copy-start(f32[128,512]{1,0:T(8,128)} %get-tuple-element.16.cls_kern_ref) | copy-start | bytes 786436
  92.2 4.2 %collective-permute-start.14 = (f32[8,640]{1,0:T(8,128)S(1)}, f32[8,640]{1,0:T(8,128)S(1)}, u32[]{:S(2)}, u32[]{:S(2)}) collective-permute-start(f32[8,640]{1,0:T(8,128)S(1)} %column_sums.2.mine_ref), channel_id=1, source_target_pairs={{0,8},{1,9},{2,10},{3,11},{4,12},{5,13},{6,14},{7,15},{8,0},{9,1},... | collective-permute-start | bytes 61448 | tf_op jit(solution)/shard_map/ppermute | solution.py:350
  96.4 3.8 %collective-permute-start.15 = (f32[8,640]{1,0:T(8,128)S(1)}, f32[8,640]{1,0:T(8,128)S(1)}, u32[]{:S(2)}, u32[]{:S(2)}) collective-permute-start(f32[8,640]{1,0:T(8,128)S(1)} %add_core.4.mine_ref), channel_id=1, source_target_pairs={{0,132},{1,133},{2,134},{3,135},{4,128},{5,129},{6,130},{7,131},{8... | collective-permute-start | bytes 61448 | tf_op jit(solution)/shard_map/ppermute | solution.py:351
  97.2 4.1 %collective-permute-start.16 = (f32[8,640]{1,0:T(8,128)S(1)}, f32[8,640]{1,0:T(8,128)S(1)}, u32[]{:S(2)}, u32[]{:S(2)}) collective-permute-start(f32[8,640]{1,0:T(8,128)S(1)} %add_core.4.mine_ref), channel_id=1, source_target_pairs={{0,128},{1,129},{2,130},{3,131},{4,132},{5,133},{6,134},{7,135},{8... | collective-permute-start | bytes 61448 | tf_op jit(solution)/shard_map/ppermute | solution.py:351
  98.3 3.0 %collective-permute-start.17 = (f32[8,640]{1,0:T(8,128)S(1)}, f32[8,640]{1,0:T(8,128)S(1)}, u32[]{:S(2)}, u32[]{:S(2)}) collective-permute-start(f32[8,640]{1,0:T(8,128)S(1)} %add_core.4.mine_ref), channel_id=1, source_target_pairs={{0,4},{1,5},{2,6},{3,7},{4,0},{5,1},{6,2},{7,3},{8,12},{9,13},{10,... | collective-permute-start | bytes 61448 | tf_op jit(solution)/shard_map/ppermute | solution.py:351
  116.6 4.2 %collective-permute-start.18 = (f32[8,640]{1,0:T(8,128)S(1)}, f32[8,640]{1,0:T(8,128)S(1)}, u32[]{:S(2)}, u32[]{:S(2)}) collective-permute-start(f32[8,640]{1,0:T(8,128)S(1)} %get-tuple-element.18.mine_ref), channel_id=1, source_target_pairs={{0,8},{1,9},{2,10},{3,11},{4,12},{5,13},{6,14},{7,15},{8,0},{9,1},... | collective-permute-start | bytes 61448 | tf_op jit(solution)/shard_map/ppermute | solution.py:350
  120.8 4.2 %collective-permute-start.19 = (f32[8,640]{1,0:T(8,128)S(1)}, f32[8,640]{1,0:T(8,128)S(1)}, u32[]{:S(2)}, u32[]{:S(2)}) collective-permute-start(f32[8,640]{1,0:T(8,128)S(1)} %add_core.5.mine_ref), channel_id=1, source_target_pairs={{0,132},{1,133},{2,134},{3,135},{4,128},{5,129},{6,130},{7,131},{8... | collective-permute-start | bytes 61448 | tf_op jit(solution)/shard_map/ppermute | solution.py:351
  122.6 4.2 %collective-permute-start.20 = (f32[8,640]{1,0:T(8,128)S(1)}, f32[8,640]{1,0:T(8,128)S(1)}, u32[]{:S(2)}, u32[]{:S(2)}) collective-permute-start(f32[8,640]{1,0:T(8,128)S(1)} %add_core.5.mine_ref), channel_id=1, source_target_pairs={{0,128},{1,129},{2,130},{3,131},{4,132},{5,133},{6,134},{7,135},{8... | collective-permute-start | bytes 61448 | tf_op jit(solution)/shard_map/ppermute | solution.py:351
  123.7 3.2 %collective-permute-start.21 = (f32[8,640]{1,0:T(8,128)S(1)}, f32[8,640]{1,0:T(8,128)S(1)}, u32[]{:S(2)}, u32[]{:S(2)}) collective-permute-start(f32[8,640]{1,0:T(8,128)S(1)} %add_core.5.mine_ref), channel_id=1, source_target_pairs={{0,4},{1,5},{2,6},{3,7},{4,0},{5,1},{6,2},{7,3},{8,12},{9,13},{10,... | collective-permute-start | bytes 61448 | tf_op jit(solution)/shard_map/ppermute | solution.py:351
  147.1 20.7 %all-to-all-start.4 = ((f32[32,4,512]{2,1,0:T(4,128)}), f32[32,4,512]{2,1,0:T(4,128)S(1)}, u32[]{:S(2)}, u32[]{:S(2)}) async-start(f32[32,4,512]{2,1,0:T(4,128)} %get-tuple-element.20), calls=%async_computation.4 | async-start | bytes 524288 | tf_op jit(solution)/shard_map/all_to_all | solution.py:363
  154.4 2.8 %collective-permute-start.22 = (f32[8,128]{1,0:T(8,128)S(1)}, f32[8,128]{1,0:T(8,128)S(1)}, u32[]{:S(2)}, u32[]{:S(2)}) collective-permute-start(f32[8,128]{1,0:T(8,128)S(1)} %get-tuple-element.19.mine_ref.sums_ref), channel_id=1, source_target_pairs={{0,4},{1,5},{2,6},{3,7},{4,0},{5,1},{6,2},{7,3},{8,12},{9,13},{10,... | collective-permute-start | bytes 12296 | tf_op jit(solution)/shard_map/ppermute | solution.py:364
  (7 other events, 8.0 us)
Sparse Core Ops, SparseCore 0:
  52.7 48.8 all-gather.4
  103.4 50.9 all-gather.6

commit v6 on v5

--- a/solution.py
+++ b/solution.py
@@ -295,6 +295,7 @@
             pltpu.SemaphoreType.DMA((PARTS,)),
         ],
         compiler_params=pltpu.CompilerParams(vmem_limit_bytes=50 * MIB),
+        cost_estimate=pl.CostEstimate(flops=64*256*384*16384, bytes_accessed=512*MIB, transcendentals=1 << 22),
         name="final_scale",
     )(where, near, far, units, cols, mine, other)
 

time: 177 us -> 177 us (level)
    all_to_all x1, waiting for transfers between devices: 0.26 us -> 2.99 us  [per_device(): cls_scaled = lax.all_to_all(cls_scaled, 'dp', 0, 0, tiled=True)]
    ppermute x1, waiting for transfers between devices: 2.71 us -> 0.01 us  [per_device(): other = lax.ppermute(sums, BOTH, swap(dyl=1))]
  transfers between devices with their start and end apart: 27 -> 27, of which waited for: 18 -> 17; matrix products, arithmetic and copies ran while one was open for 0% -> 0% of each run, Pallas kernels for 15% -> 15%
where the time goes in v6:
time: 177 us
  starting transfers between devices  51.5 us (29%)
  blocking collectives  51.1 us (29%)
  Pallas kernels  29.1 us (16%)
  waiting for transfers between devices  26.5 us (15%)
  between operations  14.2 us (8%)
  local copies, waits for them, and re-layouts  4.23 us (2%)
    all_to_all x3, blocking collectives, exchange(): lax.all_to_all(value, BOTH, 0, 0, axis_index_groups=group, tiled=True)  51.1 us
    ppermute x3, waiting for transfers between devices, per_device(): near[dyh, dyl] = lax.ppermute(patch_protos, BOTH, swap(dyh=dyh, dyl=dyl))  11.7 us
    pallas_call x1, Pallas kernels, final(): pl.pallas_call(final_body, out_shape=shape((256, 16384), BF16), in_specs=...  10.4 us
    ppermute x9, starting transfers between devices, per_device(): lax.ppermute(message, BOTH, swap(dyh=dyh, dyl=dyl))  9.76 us
    all_to_all x1, starting transfers between devices, exchange(): lax.all_to_all(value, BOTH, 0, 0, axis_index_groups=group, tiled=True)  8.19 us
    pallas_call x1, Pallas kernels, per_device(): call(kernel_body, (pltpu.VMEM((1024, 4096), F32), shape((128, 512)), shap...  8.18 us
    ppermute x4, starting transfers between devices, per_device(): pieces += [lax.ppermute(piece, BOTH, CORE) for piece in pieces]  7.79 us
    all_to_all x1, starting transfers between devices, per_device(): cls_scaled = lax.all_to_all(cls_scaled, 'dp', 0, 0, tiled=True)  7.65 us
  transfers between devices with their start and end apart: 27, of which 17 were waited for; matrix products, arithmetic and copies ran while one was open for 0% of the time, Pallas kernels for 15%

profile of v6, /device:TPU:1, one launch (start us, length us, event | category | flops | bytes accessed | tf_op | source)
XLA Modules:
  0.0 176.6 jit_solution(1293020857279036303)
XLA Ops:
  7.2 3.3 %collective-permute-start = (bf16[4,384]{1,0:T(4,128)(2,1)}, bf16[4,384]{1,0:T(4,128)(2,1)S(1)}, u32[]{:S(2)}, u32[]{:S(2)}) collective-permute-start(bf16[4,384]{1,0:T(4,128)(2,1)} %cls_ref.2), channel_id=1, source_target_pairs={{0,8},{1,9},{2,10},{3,11},{4,12},{5,13},{6,14},{7,15},{8,0},{9,1},... | collective-permute-start | bytes 9224 | tf_op jit(solution)/shard_map/ppermute | solution.py:309
  10.5 1.2 collective-permute-start.1
  11.7 2.0 %collective-permute-start.2 = (bf16[4,384]{1,0:T(4,128)(2,1)}, bf16[4,384]{1,0:T(4,128)(2,1)S(1)}, u32[]{:S(2)}, u32[]{:S(2)}) collective-permute-start(bf16[4,384]{1,0:T(4,128)(2,1)} %cls_ref.2), channel_id=1, source_target_pairs={{0,136},{1,137},{2,138},{3,139},{4,140},{5,141},{6,142},{7,143},{8... | collective-permute-start | bytes 9224 | tf_op jit(solution)/shard_map/ppermute | solution.py:309
  17.1 1.6 send.1
  18.7 8.2 %all-to-all-start = ((bf16[8,144,384]{2,1,0:T(8,128)(2,1)}), bf16[8,144,384]{2,1,0:T(8,128)(2,1)S(1)}, u32[]{:S(2)}, u32[]{:S(2)}) async-start(bf16[8,144,384]{2,1,0:T(8,128)(2,1)} %send.1), calls=%async_computation | async-start | bytes 1769472 | tf_op jit(solution)/shard_map/all_to_all | solution.py:55
  27.4 1.6 collective-permute-start.4
  28.9 1.9 %collective-permute-start.5 = (bf16[384,512]{1,0:T(8,128)(2,1)}, bf16[384,512]{1,0:T(8,128)(2,1)S(1)}, u32[]{:S(2)}, u32[]{:S(2)}) collective-permute-start(bf16[384,512]{1,0:T(8,128)(2,1)} %refs_0_.1), channel_id=1, source_target_pairs={{0,132},{1,133},{2,134},{3,135},{4,128},{5,129},{6,130},{7,131},{8... | collective-permute-start | bytes 1179656 | tf_op jit(solution)/shard_map/ppermute | solution.py:313
  30.9 1.5 collective-permute-start.6
  32.3 4.9 %collective-permute-done.3.refs_1_ = bf16[384,512]{1,0:T(8,128)(2,1)S(1)} collective-permute-done((bf16[384,512]{1,0:T(8,128)(2,1)}, bf16[384,512]{1,0:T(8,128)(2,1)S(1)}, u32[]{:S(2)}, u32[]{:S(2)}) %collective-permute-start.3) | collective-permute-done | bytes 393248 | tf_op jit(solution)/shard_map/ppermute | solution.py:313
  37.2 2.6 %collective-permute-start.7 = (bf16[384,512]{1,0:T(8,128)(2,1)S(1)}, bf16[384,512]{1,0:T(8,128)(2,1)S(1)}, u32[]{:S(2)}, u32[]{:S(2)}) collective-permute-start(bf16[384,512]{1,0:T(8,128)(2,1)S(1)} %collective-permute-done.3.refs_1_), channel_id=1, source_target_pairs={{0,8},{1,9},{2,10},{3,11},{4,12},{5,13},{6,14},{7,15},{8,0},{9,1},... | collective-permute-start | bytes 1179656 | tf_op jit(solution)/shard_map/ppermute | solution.py:315
  39.8 6.3 %collective-permute-done.4.refs_2_ = bf16[384,512]{1,0:T(8,128)(2,1)S(1)} collective-permute-done((bf16[384,512]{1,0:T(8,128)(2,1)}, bf16[384,512]{1,0:T(8,128)(2,1)S(1)}, u32[]{:S(2)}, u32[]{:S(2)}) %collective-permute-start.4) | collective-permute-done | bytes 393248 | tf_op jit(solution)/shard_map/ppermute | solution.py:313
  46.2 1.6 collective-permute-start.8
  48.2 2.1 %collective-permute-start.9 = (bf16[384,512]{1,0:T(8,128)(2,1)S(1)}, bf16[384,512]{1,0:T(8,128)(2,1)}, u32[]{:S(2)}, u32[]{:S(2)}) collective-permute-start(bf16[384,512]{1,0:T(8,128)(2,1)S(1)} %collective-permute-done.5.refs_3_), channel_id=1, source_target_pairs={{0,8},{1,9},{2,10},{3,11},{4,12},{5,13},{6,14},{7,15},{8,0},{9,1},... | collective-permute-start | bytes 1179656 | tf_op jit(solution)/shard_map/ppermute | solution.py:315
  53.5 8.2 %patch_kernel.1 = (f32[1024,4096]{1,0:T(8,128)S(1)}, f32[128,512]{1,0:T(8,128)}, f32[8,640]{1,0:T(8,128)}) custom-call(bf16[8,144,384]{2,1,0:T(8,128)(2,1)} %copy-done.5, bf16[384,512]{1,0:T(8,128)(2,1)} %cls_ref.3, bf16[384,512]{1,0:T(8,128)(2,1)} %refs_0_.1, bf16[384,512]{1,0:T(8,128)(2,1)} %copy-done.7, bf16[384,512]{1,0:T(8,128)(2,1)} %copy-done.6, ...), custom_call_target="tpu_custom_call" | custom-call | tf_op jit(solution)/shard_map/patch_kernel/pallas_call | solution.py:324
  69.3 1.2 row_sums.3
  70.5 20.3 %all_to_all.25.got_ref = f32[32,9,1,128]{3,2,1,0:T(1,128)S(1)} all-to-all(f32[32,9,1,128]{3,2,1,0:T(1,128)S(1)} %row_sums.3), channel_id=1, replica_groups={{0,1,2,3,16,17,18,19,32,33,34,35,48,49,50,51,64,65,66,67,80,81,82,83,96..., dimensions={0} | all-to-all | bytes 294912 | tf_op jit(solution)/shard_map/all_to_all | solution.py:55
  90.8 1.4 column_sums.2.mine_ref
  92.2 3.3 %collective-permute-start.14 = (f32[8,640]{1,0:T(8,128)S(1)}, f32[8,640]{1,0:T(8,128)S(1)}, u32[]{:S(2)}, u32[]{:S(2)}) collective-permute-start(f32[8,640]{1,0:T(8,128)S(1)} %column_sums.2.mine_ref), channel_id=1, source_target_pairs={{0,8},{1,9},{2,10},{3,11},{4,12},{5,13},{6,14},{7,15},{8,0},{9,1},... | collective-permute-start | bytes 61448 | tf_op jit(solution)/shard_map/ppermute | solution.py:351
  98.3 1.3 collective-permute-start.17
  101.4 1.2 row_sums.4
  102.6 12.6 %all_to_all.26.got_ref = f32[32,9,1,128]{3,2,1,0:T(1,128)S(1)} all-to-all(f32[32,9,1,128]{3,2,1,0:T(1,128)S(1)} %row_sums.4), channel_id=1, replica_groups={{0,1,2,3,16,17,18,19,32,33,34,35,48,49,50,51,64,65,66,67,80,81,82,83,96..., dimensions={0} | all-to-all | bytes 294912 | tf_op jit(solution)/shard_map/all_to_all | solution.py:55
  115.1 1.5 column_sums.3
  116.6 3.4 %collective-permute-start.18 = (f32[8,640]{1,0:T(8,128)S(1)}, f32[8,640]{1,0:T(8,128)S(1)}, u32[]{:S(2)}, u32[]{:S(2)}) collective-permute-start(f32[8,640]{1,0:T(8,128)S(1)} %get-tuple-element.18.mine_ref), channel_id=1, source_target_pairs={{0,8},{1,9},{2,10},{3,11},{4,12},{5,13},{6,14},{7,15},{8,0},{9,1},... | collective-permute-start | bytes 61448 | tf_op jit(solution)/shard_map/ppermute | solution.py:351
  120.8 1.8 %collective-permute-start.19 = (f32[8,640]{1,0:T(8,128)S(1)}, f32[8,640]{1,0:T(8,128)S(1)}, u32[]{:S(2)}, u32[]{:S(2)}) collective-permute-start(f32[8,640]{1,0:T(8,128)S(1)} %add_core.5.mine_ref), channel_id=1, source_target_pairs={{0,132},{1,133},{2,134},{3,135},{4,128},{5,129},{6,130},{7,131},{8... | collective-permute-start | bytes 61448 | tf_op jit(solution)/shard_map/ppermute | solution.py:352
  122.6 1.1 collective-permute-start.20
  125.1 1.7 collective-permute-done.20.b_ref
  126.9 1.3 row_sums.5
  128.2 18.2 %all_to_all.27.got_ref = f32[32,18,1,128]{3,2,1,0:T(1,128)S(1)} all-to-all(f32[32,18,1,128]{3,2,1,0:T(1,128)S(1)} %row_sums.5), channel_id=1, replica_groups={{0,1,2,3,16,17,18,19,32,33,34,35,48,49,50,51,64,65,66,67,80,81,82,83,96..., dimensions={0} | all-to-all | bytes 589824 | tf_op jit(solution)/shard_map/all_to_all | solution.py:55
  147.3 7.7 %all-to-all-start.4 = ((f32[32,4,512]{2,1,0:T(4,128)}), f32[32,4,512]{2,1,0:T(4,128)S(1)}, u32[]{:S(2)}, u32[]{:S(2)}) async-start(f32[32,4,512]{2,1,0:T(4,128)} %get-tuple-element.20), calls=%async_computation.4 | async-start | bytes 524288 | tf_op jit(solution)/shard_map/all_to_all | solution.py:364
  155.0 10.4 %final_scale.1 = bf16[256,16384]{1,0:T(8,128)(2,1)} custom-call(s32[5]{0:T(128)S(1)} %stack.23.where_ref, bf16[16,384,512]{2,1,0:T(8,128)(2,1)} %bitcast.7, bf16[16,384,512]{2,1,0:T(8,128)(2,1)} %bitcast.8, bf16[256,384]{1,0:T(8,128)(2,1)S(1)} %units.1.unit_ref.units_ref, f32[32,1,512]{2,1,0:T(1,128)S(1)} %get-tuple-element.23.cols_ref, ...), custom_call_target="tpu_custom_call" | custom-call | flops 103079215104 | bytes 536870912 | tf_op jit(solution)/shard_map/final_scale/pallas_call | solution.py:285
  165.4 3.0 %all-to-all-done.4.scaled_ref = f32[32,4,512]{2,1,0:T(4,128)S(1)} async-done(((f32[32,4,512]{2,1,0:T(4,128)}), f32[32,4,512]{2,1,0:T(4,128)S(1)}, u32[]{:S(2)}, u32[]{:S(2)}) %all-to-all-start.4) | async-done | bytes 262176 | tf_op jit(solution)/shard_map/all_to_all | solution.py:364
  168.4 1.4 cls_final.1
  (66 shorter events, 22.7 us)
Async XLA Ops:
  7.2 8.9 %collective-permute-start = (bf16[4,384]{1,0:T(4,128)(2,1)}, bf16[4,384]{1,0:T(4,128)(2,1)S(1)}, u32[]{:S(2)}, u32[]{:S(2)}) collective-permute-start(bf16[4,384]{1,0:T(4,128)(2,1)} %cls_ref.2), channel_id=1, source_target_pairs={{0,8},{1,9},{2,10},{3,11},{4,12},{5,13},{6,14},{7,15},{8,0},{9,1},... | collective-permute-start | bytes 9224 | tf_op jit(solution)/shard_map/ppermute | solution.py:309
  10.5 5.5 %collective-permute-start.1 = (bf16[4,384]{1,0:T(4,128)(2,1)}, bf16[4,384]{1,0:T(4,128)(2,1)S(1)}, u32[]{:S(2)}, u32[]{:S(2)}) collective-permute-start(bf16[4,384]{1,0:T(4,128)(2,1)} %cls_ref.2), channel_id=1, source_target_pairs={{0,128},{1,129},{2,130},{3,131},{4,132},{5,133},{6,134},{7,135},{8... | collective-permute-start | bytes 9224 | tf_op jit(solution)/shard_map/ppermute | solution.py:309
  11.7 4.7 %collective-permute-start.2 = (bf16[4,384]{1,0:T(4,128)(2,1)}, bf16[4,384]{1,0:T(4,128)(2,1)S(1)}, u32[]{:S(2)}, u32[]{:S(2)}) collective-permute-start(bf16[4,384]{1,0:T(4,128)(2,1)} %cls_ref.2), channel_id=1, source_target_pairs={{0,136},{1,137},{2,138},{3,139},{4,140},{5,141},{6,142},{7,143},{8... | collective-permute-start | bytes 9224 | tf_op jit(solution)/shard_map/ppermute | solution.py:309
  18.7 33.9 %all-to-all-start = ((bf16[8,144,384]{2,1,0:T(8,128)(2,1)}), bf16[8,144,384]{2,1,0:T(8,128)(2,1)S(1)}, u32[]{:S(2)}, u32[]{:S(2)}) async-start(bf16[8,144,384]{2,1,0:T(8,128)(2,1)} %send.1), calls=%async_computation | async-start | bytes 1769472 | tf_op jit(solution)/shard_map/all_to_all | solution.py:55
  26.9 128.1 %all-gather.5.cloned.1.call-start = ((), (), s32[]{:S(2)}) async-start(), calls=%async_computation.5 | async-start | bytes 6684672 | tf_op jit(solution)/shard_map/all_gather | solution.py:322
  26.9 10.3 %collective-permute-start.3 = (bf16[384,512]{1,0:T(8,128)(2,1)}, bf16[384,512]{1,0:T(8,128)(2,1)S(1)}, u32[]{:S(2)}, u32[]{:S(2)}) collective-permute-start(bf16[384,512]{1,0:T(8,128)(2,1)} %refs_0_.1), channel_id=1, source_target_pairs={{0,4},{1,5},{2,6},{3,7},{4,0},{5,1},{6,2},{7,3},{8,12},{9,13},{10,... | collective-permute-start | bytes 1179656 | tf_op jit(solution)/shard_map/ppermute | solution.py:313
  27.4 18.8 %collective-permute-start.4 = (bf16[384,512]{1,0:T(8,128)(2,1)}, bf16[384,512]{1,0:T(8,128)(2,1)S(1)}, u32[]{:S(2)}, u32[]{:S(2)}) collective-permute-start(bf16[384,512]{1,0:T(8,128)(2,1)} %refs_0_.1), channel_id=1, source_target_pairs={{0,128},{1,129},{2,130},{3,131},{4,132},{5,133},{6,134},{7,135},{8... | collective-permute-start | bytes 1179656 | tf_op jit(solution)/shard_map/ppermute | solution.py:313
  28.9 19.3 %collective-permute-start.5 = (bf16[384,512]{1,0:T(8,128)(2,1)}, bf16[384,512]{1,0:T(8,128)(2,1)S(1)}, u32[]{:S(2)}, u32[]{:S(2)}) collective-permute-start(bf16[384,512]{1,0:T(8,128)(2,1)} %refs_0_.1), channel_id=1, source_target_pairs={{0,132},{1,133},{2,134},{3,135},{4,128},{5,129},{6,130},{7,131},{8... | collective-permute-start | bytes 1179656 | tf_op jit(solution)/shard_map/ppermute | solution.py:313
  30.9 19.5 %collective-permute-start.6 = (bf16[384,512]{1,0:T(8,128)(2,1)}, bf16[384,512]{1,0:T(8,128)(2,1)S(1)}, u32[]{:S(2)}, u32[]{:S(2)}) collective-permute-start(bf16[384,512]{1,0:T(8,128)(2,1)} %refs_0_.1), channel_id=1, source_target_pairs={{0,8},{1,9},{2,10},{3,11},{4,12},{5,13},{6,14},{7,15},{8,0},{9,1},... | collective-permute-start | bytes 1179656 | tf_op jit(solution)/shard_map/ppermute | solution.py:315
  37.2 16.1 %copy-start.7 = (bf16[384,512]{1,0:T(8,128)(2,1)}, bf16[384,512]{1,0:T(8,128)(2,1)S(1)}, u32[]{:S(2)}) copy-start(bf16[384,512]{1,0:T(8,128)(2,1)S(1)} %collective-permute-done.3.refs_1_) | copy-start | bytes 1179652
  37.2 13.1 %collective-permute-start.7 = (bf16[384,512]{1,0:T(8,128)(2,1)S(1)}, bf16[384,512]{1,0:T(8,128)(2,1)S(1)}, u32[]{:S(2)}, u32[]{:S(2)}) collective-permute-start(bf16[384,512]{1,0:T(8,128)(2,1)S(1)} %collective-permute-done.3.refs_1_), channel_id=1, source_target_pairs={{0,8},{1,9},{2,10},{3,11},{4,12},{5,13},{6,14},{7,15},{8,0},{9,1},... | collective-permute-start | bytes 1179656 | tf_op jit(solution)/shard_map/ppermute | solution.py:315
  46.2 6.4 %copy-start.6 = (bf16[384,512]{1,0:T(8,128)(2,1)}, bf16[384,512]{1,0:T(8,128)(2,1)S(1)}, u32[]{:S(2)}) copy-start(bf16[384,512]{1,0:T(8,128)(2,1)S(1)} %collective-permute-done.4.refs_2_) | copy-start | bytes 1179652
  46.2 4.2 %collective-permute-start.8 = (bf16[384,512]{1,0:T(8,128)(2,1)S(1)}, bf16[384,512]{1,0:T(8,128)(2,1)S(1)}, u32[]{:S(2)}, u32[]{:S(2)}) collective-permute-start(bf16[384,512]{1,0:T(8,128)(2,1)S(1)} %collective-permute-done.4.refs_2_), channel_id=1, source_target_pairs={{0,8},{1,9},{2,10},{3,11},{4,12},{5,13},{6,14},{7,15},{8,0},{9,1},... | collective-permute-start | bytes 1179656 | tf_op jit(solution)/shard_map/ppermute | solution.py:315
  48.2 5.1 %copy-start.8 = (bf16[384,512]{1,0:T(8,128)(2,1)}, bf16[384,512]{1,0:T(8,128)(2,1)S(1)}, u32[]{:S(2)}) copy-start(bf16[384,512]{1,0:T(8,128)(2,1)S(1)} %collective-permute-done.5.refs_3_) | copy-start | bytes 1179652
  48.2 3.6 %collective-permute-start.9 = (bf16[384,512]{1,0:T(8,128)(2,1)S(1)}, bf16[384,512]{1,0:T(8,128)(2,1)}, u32[]{:S(2)}, u32[]{:S(2)}) collective-permute-start(bf16[384,512]{1,0:T(8,128)(2,1)S(1)} %collective-permute-done.5.refs_3_), channel_id=1, source_target_pairs={{0,8},{1,9},{2,10},{3,11},{4,12},{5,13},{6,14},{7,15},{8,0},{9,1},... | collective-permute-start | bytes 1179656 | tf_op jit(solution)/shard_map/ppermute | solution.py:315
  50.3 3.0 %copy-start.10 = (bf16[384,512]{1,0:T(8,128)(2,1)}, bf16[384,512]{1,0:T(8,128)(2,1)S(1)}, u32[]{:S(2)}) copy-start(bf16[384,512]{1,0:T(8,128)(2,1)S(1)} %collective-permute-done.7.refs_5_) | copy-start | bytes 1179652
  52.6 102.5 %all-gather.7.cloned.1.call-start = ((), (), s32[]{:S(2)}) async-start(), calls=%async_computation.6 | async-start | bytes 6684672 | tf_op jit(solution)/shard_map/all_gather | solution.py:322
  61.6 1.6 collective-permute-start.10
  64.0 4.2 %collective-permute-start.11 = (f32[8,640]{1,0:T(8,128)S(1)}, f32[8,640]{1,0:T(8,128)S(1)}, u32[]{:S(2)}, u32[]{:S(2)}) collective-permute-start(f32[8,640]{1,0:T(8,128)S(1)} %add_core.3.mine_ref), channel_id=1, source_target_pairs={{0,132},{1,133},{2,134},{3,135},{4,128},{5,129},{6,130},{7,131},{8... | collective-permute-start | bytes 61448 | tf_op jit(solution)/shard_map/ppermute | solution.py:352
  65.1 4.2 %collective-permute-start.12 = (f32[8,640]{1,0:T(8,128)S(1)}, f32[8,640]{1,0:T(8,128)S(1)}, u32[]{:S(2)}, u32[]{:S(2)}) collective-permute-start(f32[8,640]{1,0:T(8,128)S(1)} %add_core.3.mine_ref), channel_id=1, source_target_pairs={{0,128},{1,129},{2,130},{3,131},{4,132},{5,133},{6,134},{7,135},{8... | collective-permute-start | bytes 61448 | tf_op jit(solution)/shard_map/ppermute | solution.py:352
  66.2 3.1 %collective-permute-start.13 = (f32[8,640]{1,0:T(8,128)S(1)}, f32[8,640]{1,0:T(8,128)S(1)}, u32[]{:S(2)}, u32[]{:S(2)}) collective-permute-start(f32[8,640]{1,0:T(8,128)S(1)} %add_core.3.mine_ref), channel_id=1, source_target_pairs={{0,4},{1,5},{2,6},{3,7},{4,0},{5,1},{6,2},{7,3},{8,12},{9,13},{10,... | collective-permute-start | bytes 61448 | tf_op jit(solution)/shard_map/ppermute | solution.py:352
  69.3 21.5 %copy-start = (f32[128,512]{1,0:T(8,128)S(1)}, f32[128,512]{1,0:T(8,128)}, u32[]{:S(2)}) copy-start(f32[128,512]{1,0:T(8,128)} %get-tuple-element.16.cls_kern_ref) | copy-start | bytes 786436
  92.2 4.2 %collective-permute-start.14 = (f32[8,640]{1,0:T(8,128)S(1)}, f32[8,640]{1,0:T(8,128)S(1)}, u32[]{:S(2)}, u32[]{:S(2)}) collective-permute-start(f32[8,640]{1,0:T(8,128)S(1)} %column_sums.2.mine_ref), channel_id=1, source_target_pairs={{0,8},{1,9},{2,10},{3,11},{4,12},{5,13},{6,14},{7,15},{8,0},{9,1},... | collective-permute-start | bytes 61448 | tf_op jit(solution)/shard_map/ppermute | solution.py:351
  96.4 3.8 %collective-permute-start.15 = (f32[8,640]{1,0:T(8,128)S(1)}, f32[8,640]{1,0:T(8,128)S(1)}, u32[]{:S(2)}, u32[]{:S(2)}) collective-permute-start(f32[8,640]{1,0:T(8,128)S(1)} %add_core.4.mine_ref), channel_id=1, source_target_pairs={{0,132},{1,133},{2,134},{3,135},{4,128},{5,129},{6,130},{7,131},{8... | collective-permute-start | bytes 61448 | tf_op jit(solution)/shard_map/ppermute | solution.py:352
  97.2 4.1 %collective-permute-start.16 = (f32[8,640]{1,0:T(8,128)S(1)}, f32[8,640]{1,0:T(8,128)S(1)}, u32[]{:S(2)}, u32[]{:S(2)}) collective-permute-start(f32[8,640]{1,0:T(8,128)S(1)} %add_core.4.mine_ref), channel_id=1, source_target_pairs={{0,128},{1,129},{2,130},{3,131},{4,132},{5,133},{6,134},{7,135},{8... | collective-permute-start | bytes 61448 | tf_op jit(solution)/shard_map/ppermute | solution.py:352
  98.3 3.0 %collective-permute-start.17 = (f32[8,640]{1,0:T(8,128)S(1)}, f32[8,640]{1,0:T(8,128)S(1)}, u32[]{:S(2)}, u32[]{:S(2)}) collective-permute-start(f32[8,640]{1,0:T(8,128)S(1)} %add_core.4.mine_ref), channel_id=1, source_target_pairs={{0,4},{1,5},{2,6},{3,7},{4,0},{5,1},{6,2},{7,3},{8,12},{9,13},{10,... | collective-permute-start | bytes 61448 | tf_op jit(solution)/shard_map/ppermute | solution.py:352
  116.6 4.2 %collective-permute-start.18 = (f32[8,640]{1,0:T(8,128)S(1)}, f32[8,640]{1,0:T(8,128)S(1)}, u32[]{:S(2)}, u32[]{:S(2)}) collective-permute-start(f32[8,640]{1,0:T(8,128)S(1)} %get-tuple-element.18.mine_ref), channel_id=1, source_target_pairs={{0,8},{1,9},{2,10},{3,11},{4,12},{5,13},{6,14},{7,15},{8,0},{9,1},... | collective-permute-start | bytes 61448 | tf_op jit(solution)/shard_map/ppermute | solution.py:351
  120.8 4.2 %collective-permute-start.19 = (f32[8,640]{1,0:T(8,128)S(1)}, f32[8,640]{1,0:T(8,128)S(1)}, u32[]{:S(2)}, u32[]{:S(2)}) collective-permute-start(f32[8,640]{1,0:T(8,128)S(1)} %add_core.5.mine_ref), channel_id=1, source_target_pairs={{0,132},{1,133},{2,134},{3,135},{4,128},{5,129},{6,130},{7,131},{8... | collective-permute-start | bytes 61448 | tf_op jit(solution)/shard_map/ppermute | solution.py:352
  122.6 4.2 %collective-permute-start.20 = (f32[8,640]{1,0:T(8,128)S(1)}, f32[8,640]{1,0:T(8,128)S(1)}, u32[]{:S(2)}, u32[]{:S(2)}) collective-permute-start(f32[8,640]{1,0:T(8,128)S(1)} %add_core.5.mine_ref), channel_id=1, source_target_pairs={{0,128},{1,129},{2,130},{3,131},{4,132},{5,133},{6,134},{7,135},{8... | collective-permute-start | bytes 61448 | tf_op jit(solution)/shard_map/ppermute | solution.py:352
  123.7 3.2 %collective-permute-start.21 = (f32[8,640]{1,0:T(8,128)S(1)}, f32[8,640]{1,0:T(8,128)S(1)}, u32[]{:S(2)}, u32[]{:S(2)}) collective-permute-start(f32[8,640]{1,0:T(8,128)S(1)} %add_core.5.mine_ref), channel_id=1, source_target_pairs={{0,4},{1,5},{2,6},{3,7},{4,0},{5,1},{6,2},{7,3},{8,12},{9,13},{10,... | collective-permute-start | bytes 61448 | tf_op jit(solution)/shard_map/ppermute | solution.py:352
  147.1 7.9 %collective-permute-start.22 = (f32[8,128]{1,0:T(8,128)S(1)}, f32[8,128]{1,0:T(8,128)S(1)}, u32[]{:S(2)}, u32[]{:S(2)}) collective-permute-start(f32[8,128]{1,0:T(8,128)S(1)} %get-tuple-element.19.mine_ref.sums_ref), channel_id=1, source_target_pairs={{0,4},{1,5},{2,6},{3,7},{4,0},{5,1},{6,2},{7,3},{8,12},{9,13},{10,... | collective-permute-start | bytes 12296 | tf_op jit(solution)/shard_map/ppermute | solution.py:365
  147.3 21.1 %all-to-all-start.4 = ((f32[32,4,512]{2,1,0:T(4,128)}), f32[32,4,512]{2,1,0:T(4,128)S(1)}, u32[]{:S(2)}, u32[]{:S(2)}) async-start(f32[32,4,512]{2,1,0:T(4,128)} %get-tuple-element.20), calls=%async_computation.4 | async-start | bytes 524288 | tf_op jit(solution)/shard_map/all_to_all | solution.py:364
  (7 other events, 8.0 us)
Sparse Core Ops, SparseCore 0:
  52.7 48.8 all-gather.4
  103.4 50.9 all-gather.6

commit v7 on v5

--- a/solution.py
+++ b/solution.py
@@ -359,7 +359,7 @@
         got = exchange(send, GROUPS_ZX)
 
     cols, sums = call(settle_body, (shape((32, 1, 512)), shape((8, 128))), [SM, VM], "settle")(where, got)
-    cls_scaled = lax.optimization_barrier((done[1], sums))[0]
+    cls_scaled = lax.optimization_barrier((done[1], got))[0]
     cls_scaled = lax.all_to_all(cls_scaled, "dp", 0, 0, tiled=True)
     other = lax.ppermute(sums, BOTH, swap(dyl=1))
     patch_targets = final(where, *gathered, units, cols, sums, other)

time: 177 us -> 176 us (level)
  transfers between devices with their start and end apart: 27 -> 27, of which waited for: 18 -> 17; matrix products, arithmetic and copies ran while one was open for 0% -> 0% of each run, Pallas kernels for 15% -> 15%
where the time goes in v7:
time: 176 us
  blocking collectives  51.1 us (29%)
  starting transfers between devices  51 us (29%)
  Pallas kernels  29 us (16%)
  waiting for transfers between devices  26.3 us (15%)
  between operations  14.2 us (8%)
  local copies, waits for them, and re-layouts  4.23 us (2%)
    all_to_all x3, blocking collectives, exchange(): lax.all_to_all(value, BOTH, 0, 0, axis_index_groups=group, tiled=True)  51.1 us
    ppermute x3, waiting for transfers between devices, per_device(): near[dyh, dyl] = lax.ppermute(patch_protos, BOTH, swap(dyh=dyh, dyl=dyl))  11.7 us
    pallas_call x1, Pallas kernels, final(): pl.pallas_call(final_body, out_shape=shape((256, 16384), BF16), in_specs=...  10.3 us
    ppermute x9, starting transfers between devices, per_device(): lax.ppermute(message, BOTH, swap(dyh=dyh, dyl=dyl))  9.76 us
    all_to_all x1, starting transfers between devices, exchange(): lax.all_to_all(value, BOTH, 0, 0, axis_index_groups=group, tiled=True)  8.19 us
    pallas_call x1, Pallas kernels, per_device(): call(kernel_body, (pltpu.VMEM((1024, 4096), F32), shape((128, 512)), shap...  8.18 us
    ppermute x4, starting transfers between devices, per_device(): pieces += [lax.ppermute(piece, BOTH, CORE) for piece in pieces]  7.79 us
    all_to_all x1, starting transfers between devices, per_device(): cls_scaled = lax.all_to_all(cls_scaled, 'dp', 0, 0, tiled=True)  7.31 us
  transfers between devices with their start and end apart: 27, of which 17 were waited for; matrix products, arithmetic and copies ran while one was open for 0% of the time, Pallas kernels for 15%

profile of v7, /device:TPU:1, one launch (start us, length us, event | category | flops | bytes accessed | tf_op | source)
XLA Modules:
  0.0 175.8 jit_solution(17166846887174327497)
XLA Ops:
  7.2 3.3 %collective-permute-start = (bf16[4,384]{1,0:T(4,128)(2,1)}, bf16[4,384]{1,0:T(4,128)(2,1)S(1)}, u32[]{:S(2)}, u32[]{:S(2)}) collective-permute-start(bf16[4,384]{1,0:T(4,128)(2,1)} %cls_ref.2), channel_id=1, source_target_pairs={{0,8},{1,9},{2,10},{3,11},{4,12},{5,13},{6,14},{7,15},{8,0},{9,1},... | collective-permute-start | bytes 9224 | tf_op jit(solution)/shard_map/ppermute | solution.py:308
  10.5 1.2 collective-permute-start.1
  11.7 2.0 %collective-permute-start.2 = (bf16[4,384]{1,0:T(4,128)(2,1)}, bf16[4,384]{1,0:T(4,128)(2,1)S(1)}, u32[]{:S(2)}, u32[]{:S(2)}) collective-permute-start(bf16[4,384]{1,0:T(4,128)(2,1)} %cls_ref.2), channel_id=1, source_target_pairs={{0,136},{1,137},{2,138},{3,139},{4,140},{5,141},{6,142},{7,143},{8... | collective-permute-start | bytes 9224 | tf_op jit(solution)/shard_map/ppermute | solution.py:308
  17.1 1.6 send.1
  18.7 8.2 %all-to-all-start = ((bf16[8,144,384]{2,1,0:T(8,128)(2,1)}), bf16[8,144,384]{2,1,0:T(8,128)(2,1)S(1)}, u32[]{:S(2)}, u32[]{:S(2)}) async-start(bf16[8,144,384]{2,1,0:T(8,128)(2,1)} %send.1), calls=%async_computation | async-start | bytes 1769472 | tf_op jit(solution)/shard_map/all_to_all | solution.py:55
  27.4 1.6 collective-permute-start.4
  28.9 1.9 %collective-permute-start.5 = (bf16[384,512]{1,0:T(8,128)(2,1)}, bf16[384,512]{1,0:T(8,128)(2,1)S(1)}, u32[]{:S(2)}, u32[]{:S(2)}) collective-permute-start(bf16[384,512]{1,0:T(8,128)(2,1)} %refs_0_.1), channel_id=1, source_target_pairs={{0,132},{1,133},{2,134},{3,135},{4,128},{5,129},{6,130},{7,131},{8... | collective-permute-start | bytes 1179656 | tf_op jit(solution)/shard_map/ppermute | solution.py:312
  30.9 1.5 collective-permute-start.6
  32.3 4.9 %collective-permute-done.3.refs_1_ = bf16[384,512]{1,0:T(8,128)(2,1)S(1)} collective-permute-done((bf16[384,512]{1,0:T(8,128)(2,1)}, bf16[384,512]{1,0:T(8,128)(2,1)S(1)}, u32[]{:S(2)}, u32[]{:S(2)}) %collective-permute-start.3) | collective-permute-done | bytes 393248 | tf_op jit(solution)/shard_map/ppermute | solution.py:312
  37.2 2.6 %collective-permute-start.7 = (bf16[384,512]{1,0:T(8,128)(2,1)S(1)}, bf16[384,512]{1,0:T(8,128)(2,1)S(1)}, u32[]{:S(2)}, u32[]{:S(2)}) collective-permute-start(bf16[384,512]{1,0:T(8,128)(2,1)S(1)} %collective-permute-done.3.refs_1_), channel_id=1, source_target_pairs={{0,8},{1,9},{2,10},{3,11},{4,12},{5,13},{6,14},{7,15},{8,0},{9,1},... | collective-permute-start | bytes 1179656 | tf_op jit(solution)/shard_map/ppermute | solution.py:314
  39.8 6.3 %collective-permute-done.4.refs_2_ = bf16[384,512]{1,0:T(8,128)(2,1)S(1)} collective-permute-done((bf16[384,512]{1,0:T(8,128)(2,1)}, bf16[384,512]{1,0:T(8,128)(2,1)S(1)}, u32[]{:S(2)}, u32[]{:S(2)}) %collective-permute-start.4) | collective-permute-done | bytes 393248 | tf_op jit(solution)/shard_map/ppermute | solution.py:312
  46.2 1.6 collective-permute-start.8
  48.2 2.1 %collective-permute-start.9 = (bf16[384,512]{1,0:T(8,128)(2,1)S(1)}, bf16[384,512]{1,0:T(8,128)(2,1)}, u32[]{:S(2)}, u32[]{:S(2)}) collective-permute-start(bf16[384,512]{1,0:T(8,128)(2,1)S(1)} %collective-permute-done.5.refs_3_), channel_id=1, source_target_pairs={{0,8},{1,9},{2,10},{3,11},{4,12},{5,13},{6,14},{7,15},{8,0},{9,1},... | collective-permute-start | bytes 1179656 | tf_op jit(solution)/shard_map/ppermute | solution.py:314
  53.5 8.2 %patch_kernel.1 = (f32[1024,4096]{1,0:T(8,128)S(1)}, f32[128,512]{1,0:T(8,128)}, f32[8,640]{1,0:T(8,128)}) custom-call(bf16[8,144,384]{2,1,0:T(8,128)(2,1)} %copy-done.5, bf16[384,512]{1,0:T(8,128)(2,1)} %cls_ref.3, bf16[384,512]{1,0:T(8,128)(2,1)} %refs_0_.1, bf16[384,512]{1,0:T(8,128)(2,1)} %copy-done.7, bf16[384,512]{1,0:T(8,128)(2,1)} %copy-done.6, ...), custom_call_target="tpu_custom_call" | custom-call | tf_op jit(solution)/shard_map/patch_kernel/pallas_call | solution.py:323
  69.3 1.2 row_sums.3
  70.5 20.3 %all_to_all.25.got_ref = f32[32,9,1,128]{3,2,1,0:T(1,128)S(1)} all-to-all(f32[32,9,1,128]{3,2,1,0:T(1,128)S(1)} %row_sums.3), channel_id=1, replica_groups={{0,1,2,3,16,17,18,19,32,33,34,35,48,49,50,51,64,65,66,67,80,81,82,83,96..., dimensions={0} | all-to-all | bytes 294912 | tf_op jit(solution)/shard_map/all_to_all | solution.py:55
  90.8 1.4 column_sums.2.mine_ref
  92.2 3.3 %collective-permute-start.14 = (f32[8,640]{1,0:T(8,128)S(1)}, f32[8,640]{1,0:T(8,128)S(1)}, u32[]{:S(2)}, u32[]{:S(2)}) collective-permute-start(f32[8,640]{1,0:T(8,128)S(1)} %column_sums.2.mine_ref), channel_id=1, source_target_pairs={{0,8},{1,9},{2,10},{3,11},{4,12},{5,13},{6,14},{7,15},{8,0},{9,1},... | collective-permute-start | bytes 61448 | tf_op jit(solution)/shard_map/ppermute | solution.py:350
  98.3 1.3 collective-permute-start.17
  101.3 1.2 row_sums.4
  102.6 12.6 %all_to_all.26.got_ref = f32[32,9,1,128]{3,2,1,0:T(1,128)S(1)} all-to-all(f32[32,9,1,128]{3,2,1,0:T(1,128)S(1)} %row_sums.4), channel_id=1, replica_groups={{0,1,2,3,16,17,18,19,32,33,34,35,48,49,50,51,64,65,66,67,80,81,82,83,96..., dimensions={0} | all-to-all | bytes 294912 | tf_op jit(solution)/shard_map/all_to_all | solution.py:55
  115.1 1.4 column_sums.3
  116.6 3.4 %collective-permute-start.18 = (f32[8,640]{1,0:T(8,128)S(1)}, f32[8,640]{1,0:T(8,128)S(1)}, u32[]{:S(2)}, u32[]{:S(2)}) collective-permute-start(f32[8,640]{1,0:T(8,128)S(1)} %get-tuple-element.18.mine_ref), channel_id=1, source_target_pairs={{0,8},{1,9},{2,10},{3,11},{4,12},{5,13},{6,14},{7,15},{8,0},{9,1},... | collective-permute-start | bytes 61448 | tf_op jit(solution)/shard_map/ppermute | solution.py:350
  120.8 1.8 %collective-permute-start.19 = (f32[8,640]{1,0:T(8,128)S(1)}, f32[8,640]{1,0:T(8,128)S(1)}, u32[]{:S(2)}, u32[]{:S(2)}) collective-permute-start(f32[8,640]{1,0:T(8,128)S(1)} %add_core.5.mine_ref), channel_id=1, source_target_pairs={{0,132},{1,133},{2,134},{3,135},{4,128},{5,129},{6,130},{7,131},{8... | collective-permute-start | bytes 61448 | tf_op jit(solution)/shard_map/ppermute | solution.py:351
  122.6 1.1 collective-permute-start.20
  125.0 1.7 collective-permute-done.20.b_ref
  126.9 1.3 row_sums.5
  128.2 18.2 %all_to_all.27.got_ref = f32[32,18,1,128]{3,2,1,0:T(1,128)S(1)} all-to-all(f32[32,18,1,128]{3,2,1,0:T(1,128)S(1)} %row_sums.5), channel_id=1, replica_groups={{0,1,2,3,16,17,18,19,32,33,34,35,48,49,50,51,64,65,66,67,80,81,82,83,96..., dimensions={0} | all-to-all | bytes 589824 | tf_op jit(solution)/shard_map/all_to_all | solution.py:55
  146.4 7.3 %all-to-all-start.4 = ((f32[32,4,512]{2,1,0:T(4,128)}), f32[32,4,512]{2,1,0:T(4,128)S(1)}, u32[]{:S(2)}, u32[]{:S(2)}) async-start(f32[32,4,512]{2,1,0:T(4,128)} %get-tuple-element.19), calls=%async_computation.4 | async-start | bytes 524288 | tf_op jit(solution)/shard_map/all_to_all | solution.py:363
  154.5 2.8 %collective-permute-done.22.other_ref = f32[8,128]{1,0:T(8,128)S(1)} collective-permute-done((f32[8,128]{1,0:T(8,128)S(1)}, f32[8,128]{1,0:T(8,128)S(1)}, u32[]{:S(2)}, u32[]{:S(2)}) %collective-permute-start.22) | collective-permute-done | bytes 4128 | tf_op jit(solution)/shard_map/ppermute | solution.py:364
  157.2 10.3 %final_scale.1 = bf16[256,16384]{1,0:T(8,128)(2,1)} custom-call(s32[5]{0:T(128)S(1)} %stack.23.where_ref, bf16[16,384,512]{2,1,0:T(8,128)(2,1)} %bitcast.7, bf16[16,384,512]{2,1,0:T(8,128)(2,1)} %bitcast.8, bf16[256,384]{1,0:T(8,128)(2,1)S(1)} %units.1.unit_ref.units_ref, f32[32,1,512]{2,1,0:T(1,128)S(1)} %get-tuple-element.22.cols_ref, ...), custom_call_target="tpu_custom_call" | custom-call | tf_op jit(solution)/shard_map/final_scale/pallas_call | solution.py:285
  167.6 1.4 cls_final.1
  (66 shorter events, 22.6 us)
Async XLA Ops:
  7.2 8.9 %collective-permute-start = (bf16[4,384]{1,0:T(4,128)(2,1)}, bf16[4,384]{1,0:T(4,128)(2,1)S(1)}, u32[]{:S(2)}, u32[]{:S(2)}) collective-permute-start(bf16[4,384]{1,0:T(4,128)(2,1)} %cls_ref.2), channel_id=1, source_target_pairs={{0,8},{1,9},{2,10},{3,11},{4,12},{5,13},{6,14},{7,15},{8,0},{9,1},... | collective-permute-start | bytes 9224 | tf_op jit(solution)/shard_map/ppermute | solution.py:308
  10.5 5.5 %collective-permute-start.1 = (bf16[4,384]{1,0:T(4,128)(2,1)}, bf16[4,384]{1,0:T(4,128)(2,1)S(1)}, u32[]{:S(2)}, u32[]{:S(2)}) collective-permute-start(bf16[4,384]{1,0:T(4,128)(2,1)} %cls_ref.2), channel_id=1, source_target_pairs={{0,128},{1,129},{2,130},{3,131},{4,132},{5,133},{6,134},{7,135},{8... | collective-permute-start | bytes 9224 | tf_op jit(solution)/shard_map/ppermute | solution.py:308
  11.7 4.7 %collective-permute-start.2 = (bf16[4,384]{1,0:T(4,128)(2,1)}, bf16[4,384]{1,0:T(4,128)(2,1)S(1)}, u32[]{:S(2)}, u32[]{:S(2)}) collective-permute-start(bf16[4,384]{1,0:T(4,128)(2,1)} %cls_ref.2), channel_id=1, source_target_pairs={{0,136},{1,137},{2,138},{3,139},{4,140},{5,141},{6,142},{7,143},{8... | collective-permute-start | bytes 9224 | tf_op jit(solution)/shard_map/ppermute | solution.py:308
  18.7 33.9 %all-to-all-start = ((bf16[8,144,384]{2,1,0:T(8,128)(2,1)}), bf16[8,144,384]{2,1,0:T(8,128)(2,1)S(1)}, u32[]{:S(2)}, u32[]{:S(2)}) async-start(bf16[8,144,384]{2,1,0:T(8,128)(2,1)} %send.1), calls=%async_computation | async-start | bytes 1769472 | tf_op jit(solution)/shard_map/all_to_all | solution.py:55
  26.9 130.4 %all-gather.5.cloned.1.call-start = ((), (), s32[]{:S(2)}) async-start(), calls=%async_computation.5 | async-start | bytes 6684672 | tf_op jit(solution)/shard_map/all_gather | solution.py:321
  26.9 10.3 %collective-permute-start.3 = (bf16[384,512]{1,0:T(8,128)(2,1)}, bf16[384,512]{1,0:T(8,128)(2,1)S(1)}, u32[]{:S(2)}, u32[]{:S(2)}) collective-permute-start(bf16[384,512]{1,0:T(8,128)(2,1)} %refs_0_.1), channel_id=1, source_target_pairs={{0,4},{1,5},{2,6},{3,7},{4,0},{5,1},{6,2},{7,3},{8,12},{9,13},{10,... | collective-permute-start | bytes 1179656 | tf_op jit(solution)/shard_map/ppermute | solution.py:312
  27.4 18.8 %collective-permute-start.4 = (bf16[384,512]{1,0:T(8,128)(2,1)}, bf16[384,512]{1,0:T(8,128)(2,1)S(1)}, u32[]{:S(2)}, u32[]{:S(2)}) collective-permute-start(bf16[384,512]{1,0:T(8,128)(2,1)} %refs_0_.1), channel_id=1, source_target_pairs={{0,128},{1,129},{2,130},{3,131},{4,132},{5,133},{6,134},{7,135},{8... | collective-permute-start | bytes 1179656 | tf_op jit(solution)/shard_map/ppermute | solution.py:312
  28.9 19.3 %collective-permute-start.5 = (bf16[384,512]{1,0:T(8,128)(2,1)}, bf16[384,512]{1,0:T(8,128)(2,1)S(1)}, u32[]{:S(2)}, u32[]{:S(2)}) collective-permute-start(bf16[384,512]{1,0:T(8,128)(2,1)} %refs_0_.1), channel_id=1, source_target_pairs={{0,132},{1,133},{2,134},{3,135},{4,128},{5,129},{6,130},{7,131},{8... | collective-permute-start | bytes 1179656 | tf_op jit(solution)/shard_map/ppermute | solution.py:312
  30.9 19.5 %collective-permute-start.6 = (bf16[384,512]{1,0:T(8,128)(2,1)}, bf16[384,512]{1,0:T(8,128)(2,1)S(1)}, u32[]{:S(2)}, u32[]{:S(2)}) collective-permute-start(bf16[384,512]{1,0:T(8,128)(2,1)} %refs_0_.1), channel_id=1, source_target_pairs={{0,8},{1,9},{2,10},{3,11},{4,12},{5,13},{6,14},{7,15},{8,0},{9,1},... | collective-permute-start | bytes 1179656 | tf_op jit(solution)/shard_map/ppermute | solution.py:314
  37.2 16.1 %copy-start.7 = (bf16[384,512]{1,0:T(8,128)(2,1)}, bf16[384,512]{1,0:T(8,128)(2,1)S(1)}, u32[]{:S(2)}) copy-start(bf16[384,512]{1,0:T(8,128)(2,1)S(1)} %collective-permute-done.3.refs_1_) | copy-start | bytes 1179652
  37.2 13.1 %collective-permute-start.7 = (bf16[384,512]{1,0:T(8,128)(2,1)S(1)}, bf16[384,512]{1,0:T(8,128)(2,1)S(1)}, u32[]{:S(2)}, u32[]{:S(2)}) collective-permute-start(bf16[384,512]{1,0:T(8,128)(2,1)S(1)} %collective-permute-done.3.refs_1_), channel_id=1, source_target_pairs={{0,8},{1,9},{2,10},{3,11},{4,12},{5,13},{6,14},{7,15},{8,0},{9,1},... | collective-permute-start | bytes 1179656 | tf_op jit(solution)/shard_map/ppermute | solution.py:314
  46.2 6.4 %copy-start.6 = (bf16[384,512]{1,0:T(8,128)(2,1)}, bf16[384,512]{1,0:T(8,128)(2,1)S(1)}, u32[]{:S(2)}) copy-start(bf16[384,512]{1,0:T(8,128)(2,1)S(1)} %collective-permute-done.4.refs_2_) | copy-start | bytes 1179652
  46.2 4.2 %collective-permute-start.8 = (bf16[384,512]{1,0:T(8,128)(2,1)S(1)}, bf16[384,512]{1,0:T(8,128)(2,1)S(1)}, u32[]{:S(2)}, u32[]{:S(2)}) collective-permute-start(bf16[384,512]{1,0:T(8,128)(2,1)S(1)} %collective-permute-done.4.refs_2_), channel_id=1, source_target_pairs={{0,8},{1,9},{2,10},{3,11},{4,12},{5,13},{6,14},{7,15},{8,0},{9,1},... | collective-permute-start | bytes 1179656 | tf_op jit(solution)/shard_map/ppermute | solution.py:314
  48.2 5.1 %copy-start.8 = (bf16[384,512]{1,0:T(8,128)(2,1)}, bf16[384,512]{1,0:T(8,128)(2,1)S(1)}, u32[]{:S(2)}) copy-start(bf16[384,512]{1,0:T(8,128)(2,1)S(1)} %collective-permute-done.5.refs_3_) | copy-start | bytes 1179652
  48.2 3.6 %collective-permute-start.9 = (bf16[384,512]{1,0:T(8,128)(2,1)S(1)}, bf16[384,512]{1,0:T(8,128)(2,1)}, u32[]{:S(2)}, u32[]{:S(2)}) collective-permute-start(bf16[384,512]{1,0:T(8,128)(2,1)S(1)} %collective-permute-done.5.refs_3_), channel_id=1, source_target_pairs={{0,8},{1,9},{2,10},{3,11},{4,12},{5,13},{6,14},{7,15},{8,0},{9,1},... | collective-permute-start | bytes 1179656 | tf_op jit(solution)/shard_map/ppermute | solution.py:314
  50.3 3.0 %copy-start.10 = (bf16[384,512]{1,0:T(8,128)(2,1)}, bf16[384,512]{1,0:T(8,128)(2,1)S(1)}, u32[]{:S(2)}) copy-start(bf16[384,512]{1,0:T(8,128)(2,1)S(1)} %collective-permute-done.7.refs_5_) | copy-start | bytes 1179652
  52.6 104.7 %all-gather.7.cloned.1.call-start = ((), (), s32[]{:S(2)}) async-start(), calls=%async_computation.6 | async-start | bytes 6684672 | tf_op jit(solution)/shard_map/all_gather | solution.py:321
  61.6 1.6 collective-permute-start.10
  64.0 4.2 %collective-permute-start.11 = (f32[8,640]{1,0:T(8,128)S(1)}, f32[8,640]{1,0:T(8,128)S(1)}, u32[]{:S(2)}, u32[]{:S(2)}) collective-permute-start(f32[8,640]{1,0:T(8,128)S(1)} %add_core.3.mine_ref), channel_id=1, source_target_pairs={{0,132},{1,133},{2,134},{3,135},{4,128},{5,129},{6,130},{7,131},{8... | collective-permute-start | bytes 61448 | tf_op jit(solution)/shard_map/ppermute | solution.py:351
  65.1 4.2 %collective-permute-start.12 = (f32[8,640]{1,0:T(8,128)S(1)}, f32[8,640]{1,0:T(8,128)S(1)}, u32[]{:S(2)}, u32[]{:S(2)}) collective-permute-start(f32[8,640]{1,0:T(8,128)S(1)} %add_core.3.mine_ref), channel_id=1, source_target_pairs={{0,128},{1,129},{2,130},{3,131},{4,132},{5,133},{6,134},{7,135},{8... | collective-permute-start | bytes 61448 | tf_op jit(solution)/shard_map/ppermute | solution.py:351
  66.2 3.1 %collective-permute-start.13 = (f32[8,640]{1,0:T(8,128)S(1)}, f32[8,640]{1,0:T(8,128)S(1)}, u32[]{:S(2)}, u32[]{:S(2)}) collective-permute-start(f32[8,640]{1,0:T(8,128)S(1)} %add_core.3.mine_ref), channel_id=1, source_target_pairs={{0,4},{1,5},{2,6},{3,7},{4,0},{5,1},{6,2},{7,3},{8,12},{9,13},{10,... | collective-permute-start | bytes 61448 | tf_op jit(solution)/shard_map/ppermute | solution.py:351
  69.3 21.5 %copy-start = (f32[128,512]{1,0:T(8,128)S(1)}, f32[128,512]{1,0:T(8,128)}, u32[]{:S(2)}) copy-start(f32[128,512]{1,0:T(8,128)} %get-tuple-element.16.cls_kern_ref) | copy-start | bytes 786436
  92.2 4.2 %collective-permute-start.14 = (f32[8,640]{1,0:T(8,128)S(1)}, f32[8,640]{1,0:T(8,128)S(1)}, u32[]{:S(2)}, u32[]{:S(2)}) collective-permute-start(f32[8,640]{1,0:T(8,128)S(1)} %column_sums.2.mine_ref), channel_id=1, source_target_pairs={{0,8},{1,9},{2,10},{3,11},{4,12},{5,13},{6,14},{7,15},{8,0},{9,1},... | collective-permute-start | bytes 61448 | tf_op jit(solution)/shard_map/ppermute | solution.py:350
  96.4 3.8 %collective-permute-start.15 = (f32[8,640]{1,0:T(8,128)S(1)}, f32[8,640]{1,0:T(8,128)S(1)}, u32[]{:S(2)}, u32[]{:S(2)}) collective-permute-start(f32[8,640]{1,0:T(8,128)S(1)} %add_core.4.mine_ref), channel_id=1, source_target_pairs={{0,132},{1,133},{2,134},{3,135},{4,128},{5,129},{6,130},{7,131},{8... | collective-permute-start | bytes 61448 | tf_op jit(solution)/shard_map/ppermute | solution.py:351
  97.2 4.1 %collective-permute-start.16 = (f32[8,640]{1,0:T(8,128)S(1)}, f32[8,640]{1,0:T(8,128)S(1)}, u32[]{:S(2)}, u32[]{:S(2)}) collective-permute-start(f32[8,640]{1,0:T(8,128)S(1)} %add_core.4.mine_ref), channel_id=1, source_target_pairs={{0,128},{1,129},{2,130},{3,131},{4,132},{5,133},{6,134},{7,135},{8... | collective-permute-start | bytes 61448 | tf_op jit(solution)/shard_map/ppermute | solution.py:351
  98.3 3.0 %collective-permute-start.17 = (f32[8,640]{1,0:T(8,128)S(1)}, f32[8,640]{1,0:T(8,128)S(1)}, u32[]{:S(2)}, u32[]{:S(2)}) collective-permute-start(f32[8,640]{1,0:T(8,128)S(1)} %add_core.4.mine_ref), channel_id=1, source_target_pairs={{0,4},{1,5},{2,6},{3,7},{4,0},{5,1},{6,2},{7,3},{8,12},{9,13},{10,... | collective-permute-start | bytes 61448 | tf_op jit(solution)/shard_map/ppermute | solution.py:351
  116.6 4.2 %collective-permute-start.18 = (f32[8,640]{1,0:T(8,128)S(1)}, f32[8,640]{1,0:T(8,128)S(1)}, u32[]{:S(2)}, u32[]{:S(2)}) collective-permute-start(f32[8,640]{1,0:T(8,128)S(1)} %get-tuple-element.18.mine_ref), channel_id=1, source_target_pairs={{0,8},{1,9},{2,10},{3,11},{4,12},{5,13},{6,14},{7,15},{8,0},{9,1},... | collective-permute-start | bytes 61448 | tf_op jit(solution)/shard_map/ppermute | solution.py:350
  120.8 4.2 %collective-permute-start.19 = (f32[8,640]{1,0:T(8,128)S(1)}, f32[8,640]{1,0:T(8,128)S(1)}, u32[]{:S(2)}, u32[]{:S(2)}) collective-permute-start(f32[8,640]{1,0:T(8,128)S(1)} %add_core.5.mine_ref), channel_id=1, source_target_pairs={{0,132},{1,133},{2,134},{3,135},{4,128},{5,129},{6,130},{7,131},{8... | collective-permute-start | bytes 61448 | tf_op jit(solution)/shard_map/ppermute | solution.py:351
  122.6 4.2 %collective-permute-start.20 = (f32[8,640]{1,0:T(8,128)S(1)}, f32[8,640]{1,0:T(8,128)S(1)}, u32[]{:S(2)}, u32[]{:S(2)}) collective-permute-start(f32[8,640]{1,0:T(8,128)S(1)} %add_core.5.mine_ref), channel_id=1, source_target_pairs={{0,128},{1,129},{2,130},{3,131},{4,132},{5,133},{6,134},{7,135},{8... | collective-permute-start | bytes 61448 | tf_op jit(solution)/shard_map/ppermute | solution.py:351
  123.7 3.2 %collective-permute-start.21 = (f32[8,640]{1,0:T(8,128)S(1)}, f32[8,640]{1,0:T(8,128)S(1)}, u32[]{:S(2)}, u32[]{:S(2)}) collective-permute-start(f32[8,640]{1,0:T(8,128)S(1)} %add_core.5.mine_ref), channel_id=1, source_target_pairs={{0,4},{1,5},{2,6},{3,7},{4,0},{5,1},{6,2},{7,3},{8,12},{9,13},{10,... | collective-permute-start | bytes 61448 | tf_op jit(solution)/shard_map/ppermute | solution.py:351
  146.4 21.2 %all-to-all-start.4 = ((f32[32,4,512]{2,1,0:T(4,128)}), f32[32,4,512]{2,1,0:T(4,128)S(1)}, u32[]{:S(2)}, u32[]{:S(2)}) async-start(f32[32,4,512]{2,1,0:T(4,128)} %get-tuple-element.19), calls=%async_computation.4 | async-start | bytes 524288 | tf_op jit(solution)/shard_map/all_to_all | solution.py:363
  154.4 2.9 %collective-permute-start.22 = (f32[8,128]{1,0:T(8,128)S(1)}, f32[8,128]{1,0:T(8,128)S(1)}, u32[]{:S(2)}, u32[]{:S(2)}) collective-permute-start(f32[8,128]{1,0:T(8,128)S(1)} %get-tuple-element.23.mine_ref.sums_ref), channel_id=1, source_target_pairs={{0,4},{1,5},{2,6},{3,7},{4,0},{5,1},{6,2},{7,3},{8,12},{9,13},{10,... | collective-permute-start | bytes 12296 | tf_op jit(solution)/shard_map/ppermute | solution.py:364
  (7 other events, 8.0 us)
Sparse Core Ops, SparseCore 0:
  52.7 48.8 all-gather.4
  103.4 50.9 all-gather.6
